TPU v7x, 32 devices: a whole 2x2x4 slice. The times are simulated.
32 devices in a mesh: fsdp: 16 (over z, y, core), ctx: 2 (over x).
Axes of the slice: x: 2, y: 2, z: 4, core: 2. Of those that a mesh axis runs over, the one named last changes fastest.
Arguments:
- hidden: bfloat16 [16, 512, 5120], P('fsdp', 'ctx'), may hold values from -6 to 6
- queries: bfloat16 [16, 512, 4096], P('fsdp', 'ctx'), may hold values from -300 to 300, as said below
- norm_gain: float32 [5120], replicated, may hold values from 0.1 to 1.9
- key_gain: float32 [128], replicated, may hold values from 0.1 to 1.9
- k_weight: bfloat16 [5120, 512], P('fsdp'), may hold values from -0.078125 to 0.078125
- v_weight: bfloat16 [5120, 512], P('fsdp'), may hold values from -0.078125 to 0.078125
- segment: int32 [16, 512], P('fsdp', 'ctx'), may hold values from 0 to 3, as said below
- position: int32 [16, 512], P('fsdp', 'ctx'), may hold values from 0 to 8191, as said below
Outputs:
- attended: bfloat16 [16, 512, 4096], P('fsdp', 'ctx')
Inputs may be any that keep to these rules, and one draw needn't show every extreme that they name: queries keep to the stated range. `segment`: in each stretch, read in the tokens' order, rollout numbers never fall; the tokens of a stretch lie in its slots in an order that keeps 256 slots on each index of ctx, one token of every 2 consecutive ones on each. `position`: within one rollout of a stretch positions rise by one from token to token.
All inputs are finite; a program needn't handle non-finite values.
Results may differ from a plain program's by a relative error of at most 0.0075.
The roundings to bfloat16 on the way count: a program that leaves them out, or rounds other values in their place, can miss the bound.
Values may be sent and summed in bfloat16 or wider, within the bound.
No kernel may reach another device: no remote copies, remote signals or barrier semaphores. Data moves between devices by JAX's collectives and lax.ppermute only.
A program may use at most 192 MiB of HBM per device.

v0:
```python
import functools
import math

import jax
import jax.numpy as jnp
import numpy as np
from jax import lax
from jax.experimental import pallas as pl
from jax.experimental.pallas import tpu as pltpu
from jax.sharding import Mesh
from jax.sharding import PartitionSpec as P

KVH = 4
HD = 128
G = 8
EPS = 1e-06
THETA = 1000000.0
MASKED = -1e30
VMEM_LIMIT = 24 * 2**20
NORM_ROWS = 64
WIDE = 4
TILES = 2
HINT = 8
MASK_COST = 1 * 10**9


def norm_kernel(chunks, hidden, gain, out, held, sems):
    steps = held.shape[0] // NORM_ROWS
    copies = []
    for i in range(steps):
        at = pl.ds(i * NORM_ROWS, NORM_ROWS)
        copies.append(pltpu.make_async_copy(hidden.at[at], held.at[at], sems.at[i]))
        copies[-1].start()
    for i, copy in enumerate(copies):
        copy.wait()
        at = pl.ds(i * NORM_ROWS, NORM_ROWS)
        inputs = held[at, :].astype(jnp.float32)
        scale = lax.rsqrt(jnp.mean(inputs * inputs, axis=-1, keepdims=True) + EPS)
        normed = (inputs * scale * gain[...]).astype(jnp.bfloat16)
        rows = normed.shape[1] // chunks
        for j in range(chunks):
            out[j, at, :] = normed[:, j * rows : (j + 1) * rows]


def project_kernel(groups, alone, first, last, count, place, own, other, *rest):
    chips_z = own.shape[0] // 2
    y, x, spot = place[0], place[1], place[2]
    rest = list(rest) if alone else list(rest[1:])
    weight, lhs, sems = rest[-3:]
    waits = []
    for g, (k, near) in enumerate(groups):
        i = lax.rem(spot - k + chips_z, chips_z)
        chunk = (i ^ (i >> 1)) * 2 + (y if near else 1 - y)
        pairs = [
            (own.at[chunk], lhs.at[g, pl.ds(0, count)]),
            (other.at[chunk], lhs.at[g, pl.ds(count, count)]),
        ]
        if k == 0:
            pairs.append((rest.pop(0), weight.at[g]))
        else:
            pairs.append((rest.pop(0), weight.at[g, x]))
            pairs.append((rest.pop(0), weight.at[g, 1 - x]))
        copies = [
            pltpu.make_async_copy(source, target, sems.at[g, i])
            for i, (source, target) in enumerate(pairs)
        ]
        for copy in copies:
            copy.start()
        waits.append(copies)
    earlier = None if first else rest.pop(0)
    terms = [None, None]
    for g, copies in enumerate(waits):
        for copy in copies:
            copy.wait()
        for half in range(2):
            part = jnp.dot(lhs[g], weight[g, half], preferred_element_type=jnp.float32)
            terms[half] = part if terms[half] is None else terms[half] + part
    for half in range(2):
        if not first:
            terms[half] += earlier[half]
        if not last:
            rest[0][half] = terms[half]
    if not last:
        return
    cosine, sine, gain = rest[:3]
    outs = rest[3:5]
    for head in range(2):
        columns = slice(head * HD, (head + 1) * HD)
        for part, out in enumerate(outs):
            at = slice(part * count, (part + 1) * count)
            raw = terms[0][at, columns]
            normk = raw * lax.rsqrt(jnp.mean(raw * raw, axis=-1, keepdims=True) + EPS) * gain[...]
            turned = normk * cosine[at, :] + pltpu.roll(normk, HD // 2, 1) * sine[at, :]
            out[:, 2 * head * HD : (2 * head + 1) * HD] = turned.astype(jnp.bfloat16)
            out[:, (2 * head + 1) * HD : (2 * head + 2) * HD] = terms[1][at, columns].astype(
                jnp.bfloat16
            )


def mask_kernel(*refs):
    pieces, (bias, needs) = refs[1:-2], refs[-2:]
    count = bias.shape[0]
    size = count // TILES
    seg_q, pos_q = (
        jnp.transpose(jnp.broadcast_to(pieces[0][i : i + 1, :], (count, count))) for i in range(2)
    )
    width = len(pieces) * size
    for tile in range(TILES):
        for i, piece in enumerate(pieces):
            at = slice(tile * size, (tile + 1) * size)
            allowed = (piece[:1, at] == seg_q[:, at]) & (piece[1:, at] <= pos_q[:, at])
            there = tile * width + i * size
            bias[:, there : there + size] = jnp.where(allowed, 0.0, MASKED)
    for tile in range(TILES - 1):
        rows = slice(tile * size, (tile + 1) * size)
        needs[tile] = (jnp.max(bias[rows, (tile + 1) * width :]) == 0.0).astype(jnp.int32)
    needs[TILES - 1] = 0


def attend_kernel(pieces, count, place, needs, queries, bias, *rest):
    sources, (out, keys, values) = rest[:pieces], rest[-3:]
    step = pl.program_id(0)
    tile_rows = count // TILES
    length = pieces * tile_rows

    for head in range(2):

        @pl.when(step == head)
        def _():
            left = 2 * head * HD
            for i, source in enumerate(sources):
                for tile in range(TILES):
                    here = slice(tile * tile_rows, (tile + 1) * tile_rows)
                    there = tile * length + i * tile_rows
                    keys[there : there + tile_rows, :] = source[here, left : left + HD]
                    values[there : there + tile_rows, :] = source[here, left + HD : left + 2 * HD]

    factor = math.log2(math.e) / math.sqrt(HD)

    def tile_body(tile, high):
        rows = slice(tile * tile_rows, (tile + 1) * tile_rows)
        k, v, b = keys[:high, :], values[:high, :], bias[rows, :high]

        def score(step):
            heads = range(step * WIDE, (step + 1) * WIDE)
            q = jnp.concatenate([queries[rows, g * HD : (g + 1) * HD] for g in heads], axis=0)
            return lax.dot_general(
                q, k, (((1,), (1,)), ((), ())), preferred_element_type=jnp.float32
            )

        ahead = score(0)
        for step in range(G // WIDE):
            scores = ahead.reshape(WIDE, tile_rows, high) + b[None]
            if step + 1 < G // WIDE:
                ahead = score(step + 1)
            top = jnp.max(scores, axis=-1, keepdims=True)
            weights = jnp.exp2((scores - top) * factor)
            total = jnp.sum(weights, axis=-1, keepdims=True)
            summed = jnp.dot(
                weights.astype(jnp.bfloat16).reshape(WIDE * tile_rows, high),
                v,
                preferred_element_type=jnp.float32,
            ).reshape(WIDE, tile_rows, HD)
            result = (summed * (1.0 / total)).astype(jnp.bfloat16)
            for i in range(WIDE):
                g = step * WIDE + i
                out[rows, g * HD : (g + 1) * HD] = result[i]

    for tile in range(TILES):
        for need, high in ((0, tile + 1), (1, TILES)):

            @pl.when(needs[tile] == need)
            def _():
                tile_body(tile, high * length)


def swap(array, axis):
    return lax.ppermute(array, axis, [(0, 1), (1, 0)])


def on_device(
    sizes, hidden, queries, norm_gain, key_gain, k_weight, v_weight, segment, position
):
    chips_z, groups = sizes[0], sizes[3]
    count, width = hidden.shape[1:]
    own_rows = k_weight.shape[0]
    rows = 2 * own_rows
    chunks = 2 * chips_z
    m = 2 * groups
    z, y = lax.axis_index("z"), lax.axis_index("y")
    core, x = lax.axis_index("core"), lax.axis_index("x")
    bf16 = jnp.bfloat16
    whole = pl.BlockSpec(memory_space=pltpu.VMEM)
    params = pltpu.CompilerParams(vmem_limit_bytes=VMEM_LIMIT)

    def along_ctx(array, d, cross=False):
        pairs = []
        for c in range(2):
            for i in range(m):
                pairs.append((c * m + i, (c ^ int(cross)) * m + (i + d) % m))
        return lax.ppermute(array, ("core", "ctx", "x"), pairs)

    def columns(which):
        at = which * 2 * HD
        return jnp.stack(
            [lax.dynamic_slice_in_dim(w, at, 2 * HD, 1) for w in (k_weight, v_weight)]
        )

    taken = swap(columns(1 - core), "core")
    kept = columns(core)
    chip = lax.dynamic_update_slice(
        jnp.zeros((2, rows, 2 * HD), bf16), kept, (0, core * own_rows, 0)
    )
    chip = lax.dynamic_update_slice(chip, taken, (0, (1 - core) * own_rows, 0))
    hidden, segment, position, chip = lax.optimization_barrier((hidden, segment, position, chip))

    def norm(array):
        return pl.pallas_call(
            functools.partial(norm_kernel, chunks),
            out_shape=jax.ShapeDtypeStruct((chunks, count, rows), bf16),
            in_specs=[pl.BlockSpec(memory_space=pltpu.HBM), whole],
            out_specs=whole,
            scratch_shapes=[
                pltpu.VMEM((count, width), bf16),
                pltpu.SemaphoreType.DMA((count // NORM_ROWS,)),
            ],
            compiler_params=params,
            cost_estimate=pl.CostEstimate(
                flops=4 * count * width, bytes_accessed=4 * count * width, transcendentals=0
            ),
            name="norm",
        )(array[0], norm_gain[None])

    normed, normed_other = norm(hidden), norm(swap(hidden, "core"))
    ints = jnp.concatenate([segment, position])
    ints_all = [ints] + [along_ctx(ints, d) for d in range(1, m)]
    ints_other = swap(ints, "core")

    acc_shape = jax.ShapeDtypeStruct((2, 2 * count, 2 * HD), jnp.float32)
    kv_shape = jax.ShapeDtypeStruct((count, 4 * HD), bf16)

    def project(groups, acc=None, last=False, also=None, hint=1):
        arrays = [] if also is None else [also]
        for k, near in groups:
            if k == 0:
                arrays.append(chip if near else chip_beside)
            else:
                arrays += [mine[k], across[k]] if near else [beside[k], corner[k]]
        accs = [] if acc is None else [acc]
        outs = pl.pallas_call(
            functools.partial(project_kernel, groups, also is None, acc is None, last, count),
            out_shape=[kv_shape] * 2 if last else [acc_shape],
            in_specs=[pl.BlockSpec(memory_space=pltpu.SMEM)]
            + [pl.BlockSpec(memory_space=pltpu.HBM)] * (2 + len(arrays))
            + [whole] * (len(accs) + (3 if last else 0)),
            out_specs=[whole] * (2 if last else 1),
            scratch_shapes=[
                pltpu.VMEM((len(groups), 2, rows, 2 * HD), bf16),
                pltpu.VMEM((len(groups), 2 * count, rows), bf16),
                pltpu.SemaphoreType.DMA((len(groups), 4)),
            ],
            compiler_params=params,
            cost_estimate=pl.CostEstimate(
                flops=hint * 2 * 2 * count * rows * 4 * HD * len(groups),
                bytes_accessed=hint * 2 * rows * (4 * HD + 2 * count) * len(groups),
                transcendentals=0,
            ),
            name="project",
        )(
            place, normed, normed_other, *arrays, *accs,
            *((cosine, sine, key_gain[None]) if last else ()),
        )
        return outs if last else outs[0]

    order = [i ^ (i >> 1) for i in range(chips_z)]
    ring = [(order[i], order[(i + 1) % chips_z]) for i in range(chips_z)]
    spot = sum(jnp.where(z == order[i], i, 0) for i in range(chips_z))
    place = jnp.stack([y, x, spot]).astype(jnp.int32)
    tie = lax.optimization_barrier
    end = chips_z - 1
    mine = {0: lax.dynamic_index_in_dim(chip, x, 0, keepdims=False)}
    across, beside, corner = {}, {}, {}
    chip_beside = swap(chip, "y")
    acc = None
    for k in range(1, chips_z):
        mine[k] = lax.ppermute(mine[k - 1], "z", ring)
        if k == 1:
            tied = tie((mine[k], normed, normed_other, ints_all, ints_other))
            mine[k], normed, normed_other, ints_all, ints_other = tied
            bias, needs = pl.pallas_call(
                mask_kernel,
                out_shape=[
                    jax.ShapeDtypeStruct((count, m * count), jnp.float32),
                    jax.ShapeDtypeStruct((TILES,), jnp.int32),
                ],
                in_specs=[pl.BlockSpec(memory_space=pltpu.HBM)] + [whole] * m,
                out_specs=[whole, pl.BlockSpec(memory_space=pltpu.SMEM)],
                compiler_params=params,
                cost_estimate=pl.CostEstimate(
                    flops=MASK_COST, bytes_accessed=MASK_COST // 300, transcendentals=0
                ),
                name="mask",
            )(chip_beside, *ints_all)
        elif k > 2:
            if acc is None:
                acc = project([(0, True), (0, False)])
            acc = project([(k - 2, True)], acc, also=beside[k - 2])
            if k == 3:
                mine[k], acc, bias = tie((mine[k], acc, bias))
            else:
                mine[k], acc = tie((mine[k], acc))
        across[k], beside[k] = swap(mine[k], "x"), swap(mine[k], "y")
    for k in range(1, chips_z):
        if k < end:
            corner[k] = swap(beside[k], "x") if k % 2 else swap(across[k], "y")
    acc = project([(end - 1, True), (1, False)], acc, also=beside[end - 1], hint=HINT)
    beside[end], acc = tie((beside[end], acc))
    corner[end] = swap(beside[end], "x")

    where = jnp.concatenate([position[0], ints_other[1]]).astype(jnp.float32)
    half = HD // 2
    freq = np.exp(np.arange(half, dtype=np.float32) * np.float32(-2.0 * math.log(THETA) / HD))
    angle = where[:, None] * freq[None, :]
    cosine, sine = jnp.cos(angle), jnp.sin(angle)
    cosine = jnp.concatenate([cosine, cosine], axis=1)
    sine = jnp.concatenate([-sine, sine], axis=1)

    acc = project([(end, True)] + [(k, False) for k in range(2, end)], acc)
    kv_own, kv_other = project([(end, False)], acc, last=True)

    result = None
    for cross, kv in enumerate((kv_own, kv_other)):
        sources = [kv if d == 0 and not cross else along_ctx(kv, d, cross) for d in range(m)]

        def block(step, place, needs, cross=cross):
            return (0, lax.rem(place[0] + cross, 2) * 2 + step)

        earlier = [] if result is None else [result]
        result = pl.pallas_call(
            functools.partial(attend_kernel, m, count),
            out_shape=jax.ShapeDtypeStruct((count, KVH * G * HD), bf16),
            grid_spec=pltpu.PrefetchScalarGridSpec(
                num_scalar_prefetch=2,
                grid=(2,),
                in_specs=[pl.BlockSpec((count, G * HD), block)]
                + [whole] * (1 + m)
                + [pl.BlockSpec(memory_space=pl.ANY)] * len(earlier),
                out_specs=pl.BlockSpec((count, G * HD), block),
                scratch_shapes=[
                    pltpu.VMEM((m * count, HD), bf16),
                    pltpu.VMEM((m * count, HD), bf16),
                ],
            ),
            input_output_aliases={4 + m: 0} if earlier else {},
            compiler_params=params,
            cost_estimate=pl.CostEstimate(
                flops=2 * count * m * count * KVH * G * HD,
                bytes_accessed=2 * count * KVH * G * HD,
                transcendentals=count * m * count * KVH * G // 2,
            ),
            name="attend",
        )(core.astype(jnp.int32)[None], needs, queries[0], bias, *sources, *earlier)
    return result[None]


def solution(mesh):
    n, m = mesh.shape["fsdp"], mesh.shape["ctx"]
    sizes = (n // 4, 2, 2, m // 2, 2)
    fine = Mesh(mesh.devices.reshape(sizes), ("z", "y", "core", "ctx", "x"))
    fsdp, ctx = ("z", "y", "core"), ("ctx", "x")
    placed = (
        P(fsdp, ctx, None),
        P(fsdp, ctx, None),
        P(),
        P(),
        P(fsdp, None),
        P(fsdp, None),
        P(fsdp, ctx),
        P(fsdp, ctx),
    )
    return jax.shard_map(
        functools.partial(on_device, sizes),
        mesh=fine,
        in_specs=placed,
        out_specs=P(fsdp, ctx, None),
        check_vma=False,
    )
```

profile of v0, /device:TPU:0, one launch (start us, length us, event | category | flops | bytes accessed | tf_op | source)
XLA Modules:
  0.0 80.7 jit_solution(7507668966857708638)
XLA Ops:
  0.0 1.2 %dynamic-slice_bitcast_fusion.1 = (bf16[1,320,256]{2,1,0:T(8,128)(2,1)S(1)}, bf16[1,320,256]{2,1,0:T(8,128)(2,1)S(1)}, bf16[1,320,256]{2,1,0:T(8,128)(2,1)S(1)}, bf16[1,320,256]{2,1,0:T(8,128)(2,1)S(1)}) fusion(bf16[320,512]{1,0:T(8,128)(2,1)} %param.14, s32[]{:T(128)S(6)} %select_n.31, s32[]{:T(128)S(6)} %select_n.29, bf16[320,512]{1,0:T(8,128)(2,1)} %param.13), kind=kLoop, calls=%fused_computation.7 | loop fusion | bytes 1310728 | tf_op jit(solution)/shard_map/stack | solution.py:205
  1.3 0.5 collective-permute-start
  1.9 1.2 %collective-permute-done = bf16[2,320,256]{2,1,0:T(8,128)(2,1)S(1)} collective-permute-done((bf16[2,320,256]{2,1,0:T(8,128)(2,1)S(1)}, bf16[2,320,256]{2,1,0:T(8,128)(2,1)S(1)}, u32[]{:S(2)}, u32[]{:S(2)}) %collective-permute-start) | collective-permute-done | bytes 327712 | tf_op jit(solution)/shard_map/ppermute | solution.py:178
  3.1 0.4 collective-permute-start.3
  3.6 2.8 %collective-permute-start.2 = (bf16[640,256]{1,0:T(8,128)(2,1)S(1)}, bf16[640,256]{1,0:T(8,128)(2,1)}, u32[]{:S(2)}, u32[]{:S(2)}) collective-permute-start(bf16[640,256]{1,0:T(8,128)(2,1)S(1)} %dynamic-slice_bitcast_fusion), channel_id=1, source_target_pairs={{0,8},{8,24},{24,16},{16,0},{1,9},{9,25},{25,17},{17,1},{2,10},{10... | collective-permute-start | bytes 983048 | tf_op jit(solution)/shard_map/ppermute | solution.py:286
  6.3 1.5 %collective-permute-start.1 = (bf16[2,640,256]{2,1,0:T(8,128)(2,1)S(1)}, bf16[2,640,256]{2,1,0:T(8,128)(2,1)}, u32[]{:S(2)}, u32[]{:S(2)}) collective-permute-start(bf16[2,640,256]{2,1,0:T(8,128)(2,1)S(1)} %constant_dynamic-update-slice_fusion.rest_0_), channel_id=1, source_target_pairs={{0,4},{4,0},{1,5},{5,1},{2,6},{6,2},{3,7},{7,3},{8,12},{12,8},{9,1... | collective-permute-start | bytes 1966088 | tf_op jit(solution)/shard_map/ppermute | solution.py:178
  7.9 1.6 %collective-permute-start.4 = (s32[2,256]{1,0:T(2,128)S(1)}, s32[2,256]{1,0:T(2,128)S(1)}, u32[]{:S(2)}, u32[]{:S(2)}) collective-permute-start(s32[2,256]{1,0:T(2,128)S(1)} %pad_add_fusion.refs_1_), channel_id=1, source_target_pairs={{0,1},{1,0},{2,3},{3,2},{4,5},{5,4},{6,7},{7,6},{8,9},{9,8},{10,11... | collective-permute-start | bytes 6152 | tf_op jit(solution)/shard_map/ppermute | solution.py:201
  9.4 2.6 %norm.2.own = bf16[8,256,640]{2,1,0:T(8,128)(2,1)S(1)} custom-call(bf16[256,5120]{1,0:T(8,128)(2,1)} %bitcast.6.hidden, f32[1,5120]{1,0:T(1,128)S(1)} %bitcast.24), custom_call_target="tpu_custom_call" | custom-call | flops 5242880 | bytes 5242880 | tf_op jit(solution)/shard_map/norm/pallas_call | solution.py:218
  12.1 0.0 collective-permute-done.3
  12.1 2.6 %norm.3.other = bf16[8,256,640]{2,1,0:T(8,128)(2,1)S(1)} custom-call(bf16[256,5120]{1,0:T(8,128)(2,1)} %bitcast.8.hidden, f32[1,5120]{1,0:T(1,128)S(1)} %bitcast.25), custom_call_target="tpu_custom_call" | custom-call | flops 5242880 | bytes 5242880 | tf_op jit(solution)/shard_map/norm/pallas_call | solution.py:218
  14.7 1.5 %copy-done = bf16[8,256,640]{2,1,0:T(8,128)(2,1)} copy-done((bf16[8,256,640]{2,1,0:T(8,128)(2,1)}, bf16[8,256,640]{2,1,0:T(8,128)(2,1)S(1)}, u32[]{:S(2)}) %copy-start) | copy-done | bytes 2621464
  16.2 2.6 %collective-permute-start.6 = (bf16[640,256]{1,0:T(8,128)(2,1)}, bf16[640,256]{1,0:T(8,128)(2,1)}, u32[]{:S(2)}, u32[]{:S(2)}) collective-permute-start(bf16[640,256]{1,0:T(8,128)(2,1)} %collective-permute-done.2.rest_1_), channel_id=1, source_target_pairs={{0,8},{8,24},{24,16},{16,0},{1,9},{9,25},{25,17},{17,1},{2,10},{10... | collective-permute-start | bytes 983048 | tf_op jit(solution)/shard_map/ppermute | solution.py:286
  18.9 0.5 collective-permute-start.8
  19.4 0.5 collective-permute-start.9
  19.9 7.7 %collective-permute-done.6.rest_1_ = bf16[640,256]{1,0:T(8,128)(2,1)} collective-permute-done((bf16[640,256]{1,0:T(8,128)(2,1)}, bf16[640,256]{1,0:T(8,128)(2,1)}, u32[]{:S(2)}, u32[]{:S(2)}) %collective-permute-start.6) | collective-permute-done | bytes 327712 | tf_op jit(solution)/shard_map/ppermute | solution.py:286
  27.6 1.7 %collective-permute-start.7 = (bf16[640,256]{1,0:T(8,128)(2,1)}, bf16[640,256]{1,0:T(8,128)(2,1)S(1)}, u32[]{:S(2)}, u32[]{:S(2)}) collective-permute-start(bf16[640,256]{1,0:T(8,128)(2,1)} %collective-permute-done.6.rest_1_), channel_id=1, source_target_pairs={{0,8},{8,24},{24,16},{16,0},{1,9},{9,25},{25,17},{17,1},{2,10},{10... | collective-permute-start | bytes 983048 | tf_op jit(solution)/shard_map/ppermute | solution.py:286
  29.3 0.5 collective-permute-start.11
  29.8 0.0 collective-permute-done.1.refs_0_.rest_1_
  29.8 0.5 collective-permute-start.12
  30.4 1.5 %collective-permute-start.13 = (bf16[640,256]{1,0:T(8,128)(2,1)}, bf16[640,256]{1,0:T(8,128)(2,1)S(1)}, u32[]{:S(2)}, u32[]{:S(2)}) collective-permute-start(bf16[640,256]{1,0:T(8,128)(2,1)} %collective-permute-done.8.rest_0_.rest_3_), channel_id=1, source_target_pairs={{0,1},{1,0},{2,3},{3,2},{4,5},{5,4},{6,7},{7,6},{8,9},{9,8},{10,11... | collective-permute-start | bytes 983048 | tf_op jit(solution)/shard_map/ppermute | solution.py:178
  31.9 0.1 pad_add_fusion.1.place
  31.9 1.7 %copy-done.1 = bf16[8,256,640]{2,1,0:T(8,128)(2,1)S(1)} copy-done((bf16[8,256,640]{2,1,0:T(8,128)(2,1)S(1)}, bf16[8,256,640]{2,1,0:T(8,128)(2,1)}, u32[]{:S(2)}) %copy-start.1) | copy-done | bytes 2621464
  33.7 3.3 %project.5.rest_3_ = f32[2,512,256]{2,1,0:T(8,128)S(1)} custom-call(s32[3]{0:T(128)S(1)} %pad_add_fusion.1.place, bf16[8,256,640]{2,1,0:T(8,128)(2,1)S(1)} %norm.2.own, bf16[8,256,640]{2,1,0:T(8,128)(2,1)S(1)} %copy-done.1, bf16[2,640,256]{2,1,0:T(8,128)(2,1)S(1)} %constant_dynamic-update-slice_fusion.rest_0_, ...), custom_call_target="tpu_custom_call" | custom-call | flops 671088640 | bytes 2621440 | tf_op jit(solution)/shard_map/project/pallas_call | solution.py:250
  37.0 0.8 %mask.1 = (f32[256,512]{1,0:T(8,128)S(1)}, s32[2]{0:T(128)S(1)}) custom-call(bf16[2,640,256]{2,1,0:T(8,128)(2,1)} %collective-permute-done.1.refs_0_.rest_1_, s32[2,256]{1,0:T(2,128)S(1)} %pad_add_fusion.refs_1_, s32[2,256]{1,0:T(2,128)S(1)} %collective-permute-done.4.refs_2_), custom_call_target="tpu_custom_call" | custom-call | flops 1000000000 | bytes 3333333 | tf_op jit(solution)/shard_map/mask/pallas_call | solution.py:290
  37.9 0.9 %copy-done.2 = bf16[8,256,640]{2,1,0:T(8,128)(2,1)S(1)} copy-done((bf16[8,256,640]{2,1,0:T(8,128)(2,1)S(1)}, bf16[8,256,640]{2,1,0:T(8,128)(2,1)}, u32[]{:S(2)}) %copy-start.2) | copy-done | bytes 2621464
  38.7 2.3 %project.6.rest_5_ = f32[2,512,256]{2,1,0:T(8,128)S(1)} custom-call(s32[3]{0:T(128)S(1)} %pad_add_fusion.1.place, bf16[8,256,640]{2,1,0:T(8,128)(2,1)S(1)} %norm.2.own, bf16[8,256,640]{2,1,0:T(8,128)(2,1)S(1)} %copy-done.2, bf16[640,256]{1,0:T(8,128)(2,1)} %collective-permute-done.8.rest_0_.rest_3_, bf16[640,256]{1,0:T(8,128)(2,1)} %collective-permute-done.2.rest_1_, ...), custom_call_target="tpu_custom_call" | custom-call | flops 335544320 | bytes 1310720 | tf_op jit(solution)/shard_map/project/pallas_call | solution.py:250
  41.1 0.0 copy-start.8
  41.1 1.8 %collective-permute-start.10 = (bf16[640,256]{1,0:T(8,128)(2,1)S(1)}, bf16[640,256]{1,0:T(8,128)(2,1)S(1)}, u32[]{:S(2)}, u32[]{:S(2)}) collective-permute-start(bf16[640,256]{1,0:T(8,128)(2,1)S(1)} %collective-permute-done.7.rest_0_), channel_id=1, source_target_pairs={{0,4},{4,0},{1,5},{5,1},{2,6},{6,2},{3,7},{7,3},{8,12},{12,8},{9,1... | collective-permute-start | bytes 983048 | tf_op jit(solution)/shard_map/ppermute | solution.py:178
  42.9 0.3 collective-permute-start.15
  43.2 0.5 collective-permute-start.16
  43.7 4.0 %collective-permute-done.13.rest_4_ = bf16[640,256]{1,0:T(8,128)(2,1)S(1)} collective-permute-done((bf16[640,256]{1,0:T(8,128)(2,1)}, bf16[640,256]{1,0:T(8,128)(2,1)S(1)}, u32[]{:S(2)}, u32[]{:S(2)}) %collective-permute-start.13) | collective-permute-done | bytes 327712 | tf_op jit(solution)/shard_map/ppermute | solution.py:178
  47.7 3.1 %project.7.rest_4_ = f32[2,512,256]{2,1,0:T(8,128)S(1)} custom-call(s32[3]{0:T(128)S(1)} %pad_add_fusion.1.place, bf16[8,256,640]{2,1,0:T(8,128)(2,1)S(1)} %norm.2.own, bf16[8,256,640]{2,1,0:T(8,128)(2,1)S(1)} %copy-done.2, bf16[640,256]{1,0:T(8,128)(2,1)S(1)} %collective-permute-done.11.rest_0_.rest_2_, bf16[640,256]{1,0:T(8,128)(2,1)} %collective-permute-done.6.rest_1_, ...), custom_call_target="tpu_custom_call" | custom-call | flops 5368709120 | bytes 20971520 | tf_op jit(solution)/shard_map/project/pallas_call | solution.py:250
  50.8 1.0 %collective-permute-done.10.rest_0_ = bf16[640,256]{1,0:T(8,128)(2,1)S(1)} collective-permute-done((bf16[640,256]{1,0:T(8,128)(2,1)S(1)}, bf16[640,256]{1,0:T(8,128)(2,1)S(1)}, u32[]{:S(2)}, u32[]{:S(2)}) %collective-permute-start.10) | collective-permute-done | bytes 327712 | tf_op jit(solution)/shard_map/ppermute | solution.py:178
  51.8 0.5 collective-permute-start.14
  52.4 1.0 %fusion = (f32[512,64]{1,0:T(8,128)S(1)}, f32[512,64]{1,0:T(8,128)S(1)}, f32[512,64]{1,0:T(8,128)S(1)}) fusion(f32[64]{0:T(128)S(1)} %copy-done.8, f32[512]{0:T(512)S(1)} %add_convert_fusion), kind=kLoop, calls=%fused_computation.11 | loop fusion | flops 65536 | bytes 395520 | tf_op jit(solution)/shard_map/neg | solution.py:326
  53.4 0.1 pad_maximum_fusion.1.rest_3_
  53.5 0.1 pad_maximum_fusion.2.rest_4_
  53.6 0.0 copy-start.5
  53.6 1.1 %collective-permute-done.15.rest_1_ = bf16[640,256]{1,0:T(8,128)(2,1)S(1)} collective-permute-done((bf16[640,256]{1,0:T(8,128)(2,1)S(1)}, bf16[640,256]{1,0:T(8,128)(2,1)S(1)}, u32[]{:S(2)}, u32[]{:S(2)}) %collective-permute-start.15) | collective-permute-done | bytes 327712 | tf_op jit(solution)/shard_map/ppermute | solution.py:178
  54.7 1.8 %collective-permute-done.16.rest_3_ = bf16[640,256]{1,0:T(8,128)(2,1)S(1)} collective-permute-done((bf16[640,256]{1,0:T(8,128)(2,1)S(1)}, bf16[640,256]{1,0:T(8,128)(2,1)S(1)}, u32[]{:S(2)}, u32[]{:S(2)}) %collective-permute-start.16) | collective-permute-done | bytes 327712 | tf_op jit(solution)/shard_map/ppermute | solution.py:178
  56.6 2.5 %project.8.rest_2_ = f32[2,512,256]{2,1,0:T(8,128)S(1)} custom-call(s32[3]{0:T(128)S(1)} %pad_add_fusion.1.place, bf16[8,256,640]{2,1,0:T(8,128)(2,1)S(1)} %norm.2.own, bf16[8,256,640]{2,1,0:T(8,128)(2,1)S(1)} %copy-done.2, bf16[640,256]{1,0:T(8,128)(2,1)S(1)} %collective-permute-done.7.rest_0_, bf16[640,256]{1,0:T(8,128)(2,1)S(1)} %collective-permute-done.15.rest_1_, ...), custom_call_target="tpu_custom_call" | custom-call | flops 671088640 | bytes 2621440 | tf_op jit(solution)/shard_map/project/pallas_call | solution.py:250
  59.1 0.8 collective-permute-done.14.rest_1_
  59.9 2.0 %project.9 = (bf16[256,512]{1,0:T(8,128)(2,1)S(1)}, bf16[256,512]{1,0:T(8,128)(2,1)S(1)}) custom-call(s32[3]{0:T(128)S(1)} %pad_add_fusion.1.place, bf16[8,256,640]{2,1,0:T(8,128)(2,1)S(1)} %norm.2.own, bf16[8,256,640]{2,1,0:T(8,128)(2,1)S(1)} %copy-done.2, bf16[640,256]{1,0:T(8,128)(2,1)S(1)} %collective-permute-done.10.rest_0_, ...), custom_call_target="tpu_custom_call" | custom-call | flops 335544320 | bytes 1310720 | tf_op jit(solution)/shard_map/project/pallas_call | solution.py:250
  62.0 0.6 collective-permute-start.19
  62.6 1.6 %collective-permute-start.18 = (bf16[256,512]{1,0:T(8,128)(2,1)S(1)}, bf16[256,512]{1,0:T(8,128)(2,1)S(1)}, u32[]{:S(2)}, u32[]{:S(2)}) collective-permute-start(bf16[256,512]{1,0:T(8,128)(2,1)S(1)} %get-tuple-element.41), channel_id=1, source_target_pairs={{0,3},{1,2},{2,1},{3,0},{4,7},{5,6},{6,5},{7,4},{8,11},{9,10},{10,... | collective-permute-start | bytes 786440 | tf_op jit(solution)/shard_map/ppermute | solution.py:201
  64.2 7.0 %collective-permute-done.19.rest_1_ = bf16[256,512]{1,0:T(8,128)(2,1)S(1)} collective-permute-done((bf16[256,512]{1,0:T(8,128)(2,1)S(1)}, bf16[256,512]{1,0:T(8,128)(2,1)S(1)}, u32[]{:S(2)}, u32[]{:S(2)}) %collective-permute-start.19) | collective-permute-done | bytes 262176 | tf_op jit(solution)/shard_map/ppermute | solution.py:201
  71.2 4.7 %attend.2.rest_2_ = bf16[256,4096]{1,0:T(8,128)(2,1)} custom-call(s32[1]{0:T(128)} %bitcast.place, s32[2]{0:T(128)S(1)} %get-tuple-element.30.needs, bf16[256,4096]{1,0:T(8,128)(2,1)S(1)} %bitcast.22, f32[256,512]{1,0:T(8,128)S(1)} %get-tuple-element.35.bias, bf16[256,512]{1,0:T(8,128)(2,1)S(1)} %get-tuple-element.42.rest_0_, ...), custom_call_target="tpu_custom_call" | custom-call | flops 1073741824 | bytes 2097152 | tf_op jit(solution)/shard_map/attend/pallas_call | solution.py:339
  75.8 4.9 %attend.3 = bf16[256,4096]{1,0:T(8,128)(2,1)} custom-call(s32[1]{0:T(128)} %bitcast.place, s32[2]{0:T(128)S(1)} %get-tuple-element.30.needs, bf16[256,4096]{1,0:T(8,128)(2,1)S(1)} %bitcast.23, f32[256,512]{1,0:T(8,128)S(1)} %get-tuple-element.35.bias, bf16[256,512]{1,0:T(8,128)(2,1)S(1)} %collective-permute-done.17.rest_0_, ...), custom_call_target="tpu_custom_call", output_to_operand_aliasing={{}: (6, {})} | custom-call | flops 1073741824 | bytes 2097152 | tf_op jit(solution)/shard_map/attend/pallas_call | solution.py:339
  (33 shorter events, 0.2 us)
Async XLA Ops:
  0.0 7.8 %copy-start.7 = (s32[1,256]{1,0:T(1,128)S(1)}, s32[1,256]{1,0:T(1,128)}, u32[]{:S(2)}) copy-start(s32[1,256]{1,0:T(1,128)} %param.15) | copy-start | bytes 3076
  0.0 7.8 %copy-start.6 = (s32[1,256]{1,0:T(1,128)S(1)}, s32[1,256]{1,0:T(1,128)}, u32[]{:S(2)}) copy-start(s32[1,256]{1,0:T(1,128)} %param.16) | copy-start | bytes 3076
  0.0 9.4 %copy-start.4 = (f32[5120]{0:T(1024)S(1)}, f32[5120]{0:T(1024)}, u32[]{:S(2)}) copy-start(f32[5120]{0:T(1024)} %param.11) | copy-start | bytes 61444
  1.3 1.8 %collective-permute-start = (bf16[2,320,256]{2,1,0:T(8,128)(2,1)S(1)}, bf16[2,320,256]{2,1,0:T(8,128)(2,1)S(1)}, u32[]{:S(2)}, u32[]{:S(2)}) collective-permute-start(bf16[2,320,256]{2,1,0:T(8,128)(2,1)S(1)} %pad_maximum_fusion), channel_id=1, source_target_pairs={{0,2},{2,0},{1,3},{3,1},{4,6},{6,4},{5,7},{7,5},{8,10},{10,8},{9,1... | collective-permute-start | bytes 983048 | tf_op jit(solution)/shard_map/ppermute | solution.py:178
  3.1 9.0 %collective-permute-start.3 = (bf16[1,256,5120]{2,1,0:T(8,128)(2,1)}, bf16[1,256,5120]{2,1,0:T(8,128)(2,1)}, u32[]{:S(2)}, u32[]{:S(2)}) collective-permute-start(bf16[1,256,5120]{2,1,0:T(8,128)(2,1)} %param.9), channel_id=1, source_target_pairs={{0,2},{2,0},{1,3},{3,1},{4,6},{6,4},{5,7},{7,5},{8,10},{10,8},{9,1... | collective-permute-start | bytes 7864328 | tf_op jit(solution)/shard_map/ppermute | solution.py:178
  3.6 12.7 %collective-permute-start.2 = (bf16[640,256]{1,0:T(8,128)(2,1)S(1)}, bf16[640,256]{1,0:T(8,128)(2,1)}, u32[]{:S(2)}, u32[]{:S(2)}) collective-permute-start(bf16[640,256]{1,0:T(8,128)(2,1)S(1)} %dynamic-slice_bitcast_fusion), channel_id=1, source_target_pairs={{0,8},{8,24},{24,16},{16,0},{1,9},{9,25},{25,17},{17,1},{2,10},{10... | collective-permute-start | bytes 983048 | tf_op jit(solution)/shard_map/ppermute | solution.py:286
  6.3 23.5 %collective-permute-start.1 = (bf16[2,640,256]{2,1,0:T(8,128)(2,1)S(1)}, bf16[2,640,256]{2,1,0:T(8,128)(2,1)}, u32[]{:S(2)}, u32[]{:S(2)}) collective-permute-start(bf16[2,640,256]{2,1,0:T(8,128)(2,1)S(1)} %constant_dynamic-update-slice_fusion.rest_0_), channel_id=1, source_target_pairs={{0,4},{4,0},{1,5},{5,1},{2,6},{6,2},{3,7},{7,3},{8,12},{12,8},{9,1... | collective-permute-start | bytes 1966088 | tf_op jit(solution)/shard_map/ppermute | solution.py:178
  7.9 8.4 %collective-permute-start.4 = (s32[2,256]{1,0:T(2,128)S(1)}, s32[2,256]{1,0:T(2,128)S(1)}, u32[]{:S(2)}, u32[]{:S(2)}) collective-permute-start(s32[2,256]{1,0:T(2,128)S(1)} %pad_add_fusion.refs_1_), channel_id=1, source_target_pairs={{0,1},{1,0},{2,3},{3,2},{4,5},{5,4},{6,7},{7,6},{8,9},{9,8},{10,11... | collective-permute-start | bytes 6152 | tf_op jit(solution)/shard_map/ppermute | solution.py:201
  9.4 6.8 %collective-permute-start.5 = (s32[2,256]{1,0:T(2,128)S(1)}, s32[2,256]{1,0:T(2,128)S(1)}, u32[]{:S(2)}, u32[]{:S(2)}) collective-permute-start(s32[2,256]{1,0:T(2,128)S(1)} %pad_add_fusion.refs_1_), channel_id=1, source_target_pairs={{0,2},{2,0},{1,3},{3,1},{4,6},{6,4},{5,7},{7,5},{8,10},{10,8},{9,1... | collective-permute-start | bytes 6152 | tf_op jit(solution)/shard_map/ppermute | solution.py:178
  14.7 1.5 %copy-start = (bf16[8,256,640]{2,1,0:T(8,128)(2,1)}, bf16[8,256,640]{2,1,0:T(8,128)(2,1)S(1)}, u32[]{:S(2)}) copy-start(bf16[8,256,640]{2,1,0:T(8,128)(2,1)S(1)} %norm.3.other) | copy-start | bytes 7864324
  16.2 11.4 %collective-permute-start.6 = (bf16[640,256]{1,0:T(8,128)(2,1)}, bf16[640,256]{1,0:T(8,128)(2,1)}, u32[]{:S(2)}, u32[]{:S(2)}) collective-permute-start(bf16[640,256]{1,0:T(8,128)(2,1)} %collective-permute-done.2.rest_1_), channel_id=1, source_target_pairs={{0,8},{8,24},{24,16},{16,0},{1,9},{9,25},{25,17},{17,1},{2,10},{10... | collective-permute-start | bytes 983048 | tf_op jit(solution)/shard_map/ppermute | solution.py:286
  18.9 11.5 %collective-permute-start.8 = (bf16[640,256]{1,0:T(8,128)(2,1)}, bf16[640,256]{1,0:T(8,128)(2,1)}, u32[]{:S(2)}, u32[]{:S(2)}) collective-permute-start(bf16[640,256]{1,0:T(8,128)(2,1)} %collective-permute-done.2.rest_1_), channel_id=1, source_target_pairs={{0,4},{4,0},{1,5},{5,1},{2,6},{6,2},{3,7},{7,3},{8,12},{12,8},{9,1... | collective-permute-start | bytes 983048 | tf_op jit(solution)/shard_map/ppermute | solution.py:178
  19.4 18.5 %collective-permute-start.9 = (bf16[640,256]{1,0:T(8,128)(2,1)}, bf16[640,256]{1,0:T(8,128)(2,1)S(1)}, u32[]{:S(2)}, u32[]{:S(2)}) collective-permute-start(bf16[640,256]{1,0:T(8,128)(2,1)} %collective-permute-done.2.rest_1_), channel_id=1, source_target_pairs={{0,1},{1,0},{2,3},{3,2},{4,5},{5,4},{6,7},{7,6},{8,9},{9,8},{10,11... | collective-permute-start | bytes 983048 | tf_op jit(solution)/shard_map/ppermute | solution.py:178
  27.6 13.5 %collective-permute-start.7 = (bf16[640,256]{1,0:T(8,128)(2,1)}, bf16[640,256]{1,0:T(8,128)(2,1)S(1)}, u32[]{:S(2)}, u32[]{:S(2)}) collective-permute-start(bf16[640,256]{1,0:T(8,128)(2,1)} %collective-permute-done.6.rest_1_), channel_id=1, source_target_pairs={{0,8},{8,24},{24,16},{16,0},{1,9},{9,25},{25,17},{17,1},{2,10},{10... | collective-permute-start | bytes 983048 | tf_op jit(solution)/shard_map/ppermute | solution.py:286
  29.3 14.4 %collective-permute-start.11 = (bf16[640,256]{1,0:T(8,128)(2,1)}, bf16[640,256]{1,0:T(8,128)(2,1)S(1)}, u32[]{:S(2)}, u32[]{:S(2)}) collective-permute-start(bf16[640,256]{1,0:T(8,128)(2,1)} %collective-permute-done.6.rest_1_), channel_id=1, source_target_pairs={{0,4},{4,0},{1,5},{5,1},{2,6},{6,2},{3,7},{7,3},{8,12},{12,8},{9,1... | collective-permute-start | bytes 983048 | tf_op jit(solution)/shard_map/ppermute | solution.py:178
  29.8 13.4 %collective-permute-start.12 = (bf16[640,256]{1,0:T(8,128)(2,1)}, bf16[640,256]{1,0:T(8,128)(2,1)S(1)}, u32[]{:S(2)}, u32[]{:S(2)}) collective-permute-start(bf16[640,256]{1,0:T(8,128)(2,1)} %collective-permute-done.6.rest_1_), channel_id=1, source_target_pairs={{0,1},{1,0},{2,3},{3,2},{4,5},{5,4},{6,7},{7,6},{8,9},{9,8},{10,11... | collective-permute-start | bytes 983048 | tf_op jit(solution)/shard_map/ppermute | solution.py:178
  30.4 17.3 %collective-permute-start.13 = (bf16[640,256]{1,0:T(8,128)(2,1)}, bf16[640,256]{1,0:T(8,128)(2,1)S(1)}, u32[]{:S(2)}, u32[]{:S(2)}) collective-permute-start(bf16[640,256]{1,0:T(8,128)(2,1)} %collective-permute-done.8.rest_0_.rest_3_), channel_id=1, source_target_pairs={{0,1},{1,0},{2,3},{3,2},{4,5},{5,4},{6,7},{7,6},{8,9},{9,8},{10,11... | collective-permute-start | bytes 983048 | tf_op jit(solution)/shard_map/ppermute | solution.py:178
  31.9 1.7 %copy-start.1 = (bf16[8,256,640]{2,1,0:T(8,128)(2,1)S(1)}, bf16[8,256,640]{2,1,0:T(8,128)(2,1)}, u32[]{:S(2)}) copy-start(bf16[8,256,640]{2,1,0:T(8,128)(2,1)} %copy-done) | copy-start | bytes 7864324
  37.0 1.7 %copy-start.2 = (bf16[8,256,640]{2,1,0:T(8,128)(2,1)S(1)}, bf16[8,256,640]{2,1,0:T(8,128)(2,1)}, u32[]{:S(2)}) copy-start(bf16[8,256,640]{2,1,0:T(8,128)(2,1)} %copy-done) | copy-start | bytes 7864324
  41.1 11.3 %copy-start.8 = (f32[64]{0:T(128)S(1)}, f32[64]{0:T(128)}, u32[]{:S(2)}) copy-start(f32[64]{0:T(128)} %constant.45) | copy-start | bytes 772
  41.1 10.7 %collective-permute-start.10 = (bf16[640,256]{1,0:T(8,128)(2,1)S(1)}, bf16[640,256]{1,0:T(8,128)(2,1)S(1)}, u32[]{:S(2)}, u32[]{:S(2)}) collective-permute-start(bf16[640,256]{1,0:T(8,128)(2,1)S(1)} %collective-permute-done.7.rest_0_), channel_id=1, source_target_pairs={{0,4},{4,0},{1,5},{5,1},{2,6},{6,2},{3,7},{7,3},{8,12},{12,8},{9,1... | collective-permute-start | bytes 983048 | tf_op jit(solution)/shard_map/ppermute | solution.py:178
  42.9 11.8 %collective-permute-start.15 = (bf16[640,256]{1,0:T(8,128)(2,1)S(1)}, bf16[640,256]{1,0:T(8,128)(2,1)S(1)}, u32[]{:S(2)}, u32[]{:S(2)}) collective-permute-start(bf16[640,256]{1,0:T(8,128)(2,1)S(1)} %collective-permute-done.7.rest_0_), channel_id=1, source_target_pairs={{0,1},{1,0},{2,3},{3,2},{4,5},{5,4},{6,7},{7,6},{8,9},{9,8},{10,11... | collective-permute-start | bytes 983048 | tf_op jit(solution)/shard_map/ppermute | solution.py:178
  43.2 13.3 %collective-permute-start.16 = (bf16[640,256]{1,0:T(8,128)(2,1)S(1)}, bf16[640,256]{1,0:T(8,128)(2,1)S(1)}, u32[]{:S(2)}, u32[]{:S(2)}) collective-permute-start(bf16[640,256]{1,0:T(8,128)(2,1)S(1)} %collective-permute-done.12.rest_2_), channel_id=1, source_target_pairs={{0,4},{4,0},{1,5},{5,1},{2,6},{6,2},{3,7},{7,3},{8,12},{12,8},{9,1... | collective-permute-start | bytes 983048 | tf_op jit(solution)/shard_map/ppermute | solution.py:178
  51.8 8.1 %collective-permute-start.14 = (bf16[640,256]{1,0:T(8,128)(2,1)S(1)}, bf16[640,256]{1,0:T(8,128)(2,1)S(1)}, u32[]{:S(2)}, u32[]{:S(2)}) collective-permute-start(bf16[640,256]{1,0:T(8,128)(2,1)S(1)} %collective-permute-done.10.rest_0_), channel_id=1, source_target_pairs={{0,1},{1,0},{2,3},{3,2},{4,5},{5,4},{6,7},{7,6},{8,9},{9,8},{10,11... | collective-permute-start | bytes 983048 | tf_op jit(solution)/shard_map/ppermute | solution.py:178
  53.6 6.3 %copy-start.5 = (f32[128]{0:T(128)S(1)}, f32[128]{0:T(128)}, u32[]{:S(2)}) copy-start(f32[128]{0:T(128)} %param.12) | copy-start | bytes 1540
  59.9 11.3 %copy-start.3 = (bf16[1,256,4096]{2,1,0:T(8,128)(2,1)S(1)}, bf16[1,256,4096]{2,1,0:T(8,128)(2,1)}, u32[]{:S(2)}) copy-start(bf16[1,256,4096]{2,1,0:T(8,128)(2,1)} %param.10) | copy-start | bytes 6291460
  62.0 9.2 %collective-permute-start.19 = (bf16[256,512]{1,0:T(8,128)(2,1)S(1)}, bf16[256,512]{1,0:T(8,128)(2,1)S(1)}, u32[]{:S(2)}, u32[]{:S(2)}) collective-permute-start(bf16[256,512]{1,0:T(8,128)(2,1)S(1)} %get-tuple-element.42.rest_0_), channel_id=1, source_target_pairs={{0,1},{1,0},{2,3},{3,2},{4,5},{5,4},{6,7},{7,6},{8,9},{9,8},{10,11... | collective-permute-start | bytes 786440 | tf_op jit(solution)/shard_map/ppermute | solution.py:201
  62.6 13.3 %collective-permute-start.17 = (bf16[256,512]{1,0:T(8,128)(2,1)S(1)}, bf16[256,512]{1,0:T(8,128)(2,1)S(1)}, u32[]{:S(2)}, u32[]{:S(2)}) collective-permute-start(bf16[256,512]{1,0:T(8,128)(2,1)S(1)} %get-tuple-element.41), channel_id=1, source_target_pairs={{0,2},{1,3},{2,0},{3,1},{4,6},{5,7},{6,4},{7,5},{8,10},{9,11},{10,... | collective-permute-start | bytes 786440 | tf_op jit(solution)/shard_map/ppermute | solution.py:201
  62.6 13.3 %collective-permute-start.18 = (bf16[256,512]{1,0:T(8,128)(2,1)S(1)}, bf16[256,512]{1,0:T(8,128)(2,1)S(1)}, u32[]{:S(2)}, u32[]{:S(2)}) collective-permute-start(bf16[256,512]{1,0:T(8,128)(2,1)S(1)} %get-tuple-element.41), channel_id=1, source_target_pairs={{0,3},{1,2},{2,1},{3,0},{4,7},{5,6},{6,5},{7,4},{8,11},{9,10},{10,... | collective-permute-start | bytes 786440 | tf_op jit(solution)/shard_map/ppermute | solution.py:201
where the time goes:
time: 81.1 us; the launch traced here: 80.7 us
  Pallas kernels  29 us (36%)
  waiting for transfers between devices  24.6 us (30%)
  starting transfers between devices  20.1 us (25%)
  local copies, waits for them, and re-layouts  5.47 us (7%)
  other arithmetic  1.42 us (2%)
    pallas_call x5, Pallas kernels, project(): pl.pallas_call(functools.partial(project_kernel, groups, also is None, ac...  13.3 us
    ppermute x13, waiting for transfers between devices, swap(): return lax.ppermute(array, axis, [(0, 1), (1, 0)])  9.85 us
    pallas_call x2, Pallas kernels, on_device(): pl.pallas_call(functools.partial(attend_kernel, m, count), out_shape=jax....  9.55 us
    ppermute x13, starting transfers between devices, swap(): return lax.ppermute(array, axis, [(0, 1), (1, 0)])  9.22 us
    ppermute x3, waiting for transfers between devices, on_device(): mine[k] = lax.ppermute(mine[k - 1], 'z', ring)  7.71 us
    ppermute x3, starting transfers between devices, on_device(): mine[k] = lax.ppermute(mine[k - 1], 'z', ring)  7.11 us
    ppermute x4, waiting for transfers between devices, along_ctx(): return lax.ppermute(array, ('core', 'ctx', 'x'), pairs)  7.01 us
    pallas_call x2, Pallas kernels, norm(): pl.pallas_call(functools.partial(norm_kernel, chunks), out_shape=jax.Shap...  5.27 us
  transfers between devices with their start and end apart: 20, of which 8 were waited for; matrix products, arithmetic and copies ran while one was open for 2% of the time, Pallas kernels for 27%

commit v1 on v0

--- a/solution.py
+++ b/solution.py
@@ -24,22 +24,26 @@
 MASK_COST = 1 * 10**9
 
 
-def norm_kernel(chunks, hidden, gain, out, held, sems):
+def norm_kernel(chunks, hidden, gain, out, held, made, sems):
     steps = held.shape[0] // NORM_ROWS
-    copies = []
+    reads, writes = [], []
     for i in range(steps):
         at = pl.ds(i * NORM_ROWS, NORM_ROWS)
-        copies.append(pltpu.make_async_copy(hidden.at[at], held.at[at], sems.at[i]))
-        copies[-1].start()
-    for i, copy in enumerate(copies):
-        copy.wait()
+        reads.append(pltpu.make_async_copy(hidden.at[at], held.at[at], sems.at[0, i]))
+        writes.append(pltpu.make_async_copy(made.at[:, at], out.at[:, at], sems.at[1, i]))
+        reads[-1].start()
+    for i in range(steps):
+        reads[i].wait()
         at = pl.ds(i * NORM_ROWS, NORM_ROWS)
         inputs = held[at, :].astype(jnp.float32)
         scale = lax.rsqrt(jnp.mean(inputs * inputs, axis=-1, keepdims=True) + EPS)
         normed = (inputs * scale * gain[...]).astype(jnp.bfloat16)
         rows = normed.shape[1] // chunks
         for j in range(chunks):
-            out[j, at, :] = normed[:, j * rows : (j + 1) * rows]
+            made[j, at, :] = normed[:, j * rows : (j + 1) * rows]
+        writes[i].start()
+    for write in writes:
+        write.wait()
 
 
 def project_kernel(groups, alone, first, last, count, place, own, other, *rest):
@@ -219,10 +223,11 @@
             functools.partial(norm_kernel, chunks),
             out_shape=jax.ShapeDtypeStruct((chunks, count, rows), bf16),
             in_specs=[pl.BlockSpec(memory_space=pltpu.HBM), whole],
-            out_specs=whole,
+            out_specs=pl.BlockSpec(memory_space=pltpu.HBM),
             scratch_shapes=[
                 pltpu.VMEM((count, width), bf16),
-                pltpu.SemaphoreType.DMA((count // NORM_ROWS,)),
+                pltpu.VMEM((chunks, count, rows), bf16),
+                pltpu.SemaphoreType.DMA((2, count // NORM_ROWS)),
             ],
             compiler_params=params,
             cost_estimate=pl.CostEstimate(

time: 81.1 us -> 81.6 us (level)
  transfers between devices with their start and end apart: 20 -> 20, of which waited for: 8 -> 8; matrix products, arithmetic and copies ran while one was open for 2% -> 2% of each run, Pallas kernels for 27% -> 28%
where the time goes in v1:
time: 81.6 us; the launch traced here: 81.3 us
  Pallas kernels  29.5 us (36%)
  waiting for transfers between devices  24.5 us (30%)
  starting transfers between devices  20.1 us (25%)
  local copies, waits for them, and re-layouts  5.47 us (7%)
  other arithmetic  1.42 us (2%)
    pallas_call x5, Pallas kernels, project(): pl.pallas_call(functools.partial(project_kernel, groups, also is None, ac...  13.3 us
    ppermute x13, waiting for transfers between devices, swap(): return lax.ppermute(array, axis, [(0, 1), (1, 0)])  9.81 us
    pallas_call x2, Pallas kernels, on_device(): pl.pallas_call(functools.partial(attend_kernel, m, count), out_shape=jax....  9.55 us
    ppermute x13, starting transfers between devices, swap(): return lax.ppermute(array, axis, [(0, 1), (1, 0)])  9.25 us
    ppermute x3, waiting for transfers between devices, on_device(): mine[k] = lax.ppermute(mine[k - 1], 'z', ring)  7.71 us
    ppermute x3, starting transfers between devices, on_device(): mine[k] = lax.ppermute(mine[k - 1], 'z', ring)  7.11 us
    ppermute x4, waiting for transfers between devices, along_ctx(): return lax.ppermute(array, ('core', 'ctx', 'x'), pairs)  7.01 us
    pallas_call x2, Pallas kernels, norm(): pl.pallas_call(functools.partial(norm_kernel, chunks), out_shape=jax.Shap...  5.83 us
  transfers between devices with their start and end apart: 20, of which 8 were waited for; matrix products, arithmetic and copies ran while one was open for 2% of the time, Pallas kernels for 28%

profile of v1, /device:TPU:0, one launch (start us, length us, event | category | flops | bytes accessed | tf_op | source)
XLA Modules:
  0.0 81.3 jit_solution(7852982393453429278)
XLA Ops:
  0.0 1.2 %dynamic-slice_bitcast_fusion.1 = (bf16[1,320,256]{2,1,0:T(8,128)(2,1)S(1)}, bf16[1,320,256]{2,1,0:T(8,128)(2,1)S(1)}, bf16[1,320,256]{2,1,0:T(8,128)(2,1)S(1)}, bf16[1,320,256]{2,1,0:T(8,128)(2,1)S(1)}) fusion(bf16[320,512]{1,0:T(8,128)(2,1)} %param.14, s32[]{:T(128)S(6)} %select_n.31, s32[]{:T(128)S(6)} %select_n.29, bf16[320,512]{1,0:T(8,128)(2,1)} %param.13), kind=kLoop, calls=%fused_computation.7 | loop fusion | bytes 1310728 | tf_op jit(solution)/shard_map/stack | solution.py:209
  1.3 0.5 collective-permute-start
  1.9 1.2 %collective-permute-done = bf16[2,320,256]{2,1,0:T(8,128)(2,1)S(1)} collective-permute-done((bf16[2,320,256]{2,1,0:T(8,128)(2,1)S(1)}, bf16[2,320,256]{2,1,0:T(8,128)(2,1)S(1)}, u32[]{:S(2)}, u32[]{:S(2)}) %collective-permute-start) | collective-permute-done | bytes 327712 | tf_op jit(solution)/shard_map/ppermute | solution.py:182
  3.1 0.4 collective-permute-start.3
  3.6 2.8 %collective-permute-start.2 = (bf16[640,256]{1,0:T(8,128)(2,1)S(1)}, bf16[640,256]{1,0:T(8,128)(2,1)}, u32[]{:S(2)}, u32[]{:S(2)}) collective-permute-start(bf16[640,256]{1,0:T(8,128)(2,1)S(1)} %dynamic-slice_bitcast_fusion), channel_id=1, source_target_pairs={{0,8},{8,24},{24,16},{16,0},{1,9},{9,25},{25,17},{17,1},{2,10},{10... | collective-permute-start | bytes 983048 | tf_op jit(solution)/shard_map/ppermute | solution.py:291
  6.3 1.5 %collective-permute-start.1 = (bf16[2,640,256]{2,1,0:T(8,128)(2,1)S(1)}, bf16[2,640,256]{2,1,0:T(8,128)(2,1)}, u32[]{:S(2)}, u32[]{:S(2)}) collective-permute-start(bf16[2,640,256]{2,1,0:T(8,128)(2,1)S(1)} %constant_dynamic-update-slice_fusion.rest_0_), channel_id=1, source_target_pairs={{0,4},{4,0},{1,5},{5,1},{2,6},{6,2},{3,7},{7,3},{8,12},{12,8},{9,1... | collective-permute-start | bytes 1966088 | tf_op jit(solution)/shard_map/ppermute | solution.py:182
  7.9 1.6 %collective-permute-start.4 = (s32[2,256]{1,0:T(2,128)S(1)}, s32[2,256]{1,0:T(2,128)S(1)}, u32[]{:S(2)}, u32[]{:S(2)}) collective-permute-start(s32[2,256]{1,0:T(2,128)S(1)} %pad_add_fusion.refs_1_), channel_id=1, source_target_pairs={{0,1},{1,0},{2,3},{3,2},{4,5},{5,4},{6,7},{7,6},{8,9},{9,8},{10,11... | collective-permute-start | bytes 6152 | tf_op jit(solution)/shard_map/ppermute | solution.py:205
  9.4 2.9 %norm.2.own = bf16[8,256,640]{2,1,0:T(8,128)(2,1)S(1)} custom-call(bf16[256,5120]{1,0:T(8,128)(2,1)} %bitcast.6.hidden, f32[1,5120]{1,0:T(1,128)S(1)} %bitcast.24), custom_call_target="tpu_custom_call" | custom-call | flops 5242880 | bytes 5242880 | tf_op jit(solution)/shard_map/norm/pallas_call | solution.py:222
  12.3 0.0 collective-permute-done.3
  12.4 2.9 %norm.3.other = bf16[8,256,640]{2,1,0:T(8,128)(2,1)S(1)} custom-call(bf16[256,5120]{1,0:T(8,128)(2,1)} %bitcast.8.hidden, f32[1,5120]{1,0:T(1,128)S(1)} %bitcast.25), custom_call_target="tpu_custom_call" | custom-call | flops 5242880 | bytes 5242880 | tf_op jit(solution)/shard_map/norm/pallas_call | solution.py:222
  15.3 1.5 %copy-done = bf16[8,256,640]{2,1,0:T(8,128)(2,1)} copy-done((bf16[8,256,640]{2,1,0:T(8,128)(2,1)}, bf16[8,256,640]{2,1,0:T(8,128)(2,1)S(1)}, u32[]{:S(2)}) %copy-start) | copy-done | bytes 2621464
  16.8 0.0 collective-permute-done.4.refs_2_
  16.8 2.6 %collective-permute-start.6 = (bf16[640,256]{1,0:T(8,128)(2,1)}, bf16[640,256]{1,0:T(8,128)(2,1)}, u32[]{:S(2)}, u32[]{:S(2)}) collective-permute-start(bf16[640,256]{1,0:T(8,128)(2,1)} %collective-permute-done.2.rest_1_), channel_id=1, source_target_pairs={{0,8},{8,24},{24,16},{16,0},{1,9},{9,25},{25,17},{17,1},{2,10},{10... | collective-permute-start | bytes 983048 | tf_op jit(solution)/shard_map/ppermute | solution.py:291
  19.4 0.5 collective-permute-start.8
  19.9 0.5 collective-permute-start.9
  20.5 7.7 %collective-permute-done.6.rest_1_ = bf16[640,256]{1,0:T(8,128)(2,1)} collective-permute-done((bf16[640,256]{1,0:T(8,128)(2,1)}, bf16[640,256]{1,0:T(8,128)(2,1)}, u32[]{:S(2)}, u32[]{:S(2)}) %collective-permute-start.6) | collective-permute-done | bytes 327712 | tf_op jit(solution)/shard_map/ppermute | solution.py:291
  28.2 1.7 %collective-permute-start.7 = (bf16[640,256]{1,0:T(8,128)(2,1)}, bf16[640,256]{1,0:T(8,128)(2,1)S(1)}, u32[]{:S(2)}, u32[]{:S(2)}) collective-permute-start(bf16[640,256]{1,0:T(8,128)(2,1)} %collective-permute-done.6.rest_1_), channel_id=1, source_target_pairs={{0,8},{8,24},{24,16},{16,0},{1,9},{9,25},{25,17},{17,1},{2,10},{10... | collective-permute-start | bytes 983048 | tf_op jit(solution)/shard_map/ppermute | solution.py:291
  29.9 0.5 collective-permute-start.11
  30.4 0.6 collective-permute-start.12
  30.9 1.5 %collective-permute-start.13 = (bf16[640,256]{1,0:T(8,128)(2,1)}, bf16[640,256]{1,0:T(8,128)(2,1)S(1)}, u32[]{:S(2)}, u32[]{:S(2)}) collective-permute-start(bf16[640,256]{1,0:T(8,128)(2,1)} %collective-permute-done.8.rest_0_.rest_3_), channel_id=1, source_target_pairs={{0,1},{1,0},{2,3},{3,2},{4,5},{5,4},{6,7},{7,6},{8,9},{9,8},{10,11... | collective-permute-start | bytes 983048 | tf_op jit(solution)/shard_map/ppermute | solution.py:182
  32.4 0.1 pad_add_fusion.1.place
  32.5 1.7 %copy-done.1 = bf16[8,256,640]{2,1,0:T(8,128)(2,1)S(1)} copy-done((bf16[8,256,640]{2,1,0:T(8,128)(2,1)S(1)}, bf16[8,256,640]{2,1,0:T(8,128)(2,1)}, u32[]{:S(2)}) %copy-start.1) | copy-done | bytes 2621464
  34.2 3.3 %project.5.rest_3_ = f32[2,512,256]{2,1,0:T(8,128)S(1)} custom-call(s32[3]{0:T(128)S(1)} %pad_add_fusion.1.place, bf16[8,256,640]{2,1,0:T(8,128)(2,1)S(1)} %norm.2.own, bf16[8,256,640]{2,1,0:T(8,128)(2,1)S(1)} %copy-done.1, bf16[2,640,256]{2,1,0:T(8,128)(2,1)S(1)} %constant_dynamic-update-slice_fusion.rest_0_, ...), custom_call_target="tpu_custom_call" | custom-call | flops 671088640 | bytes 2621440 | tf_op jit(solution)/shard_map/project/pallas_call | solution.py:255
  37.6 0.8 %mask.1 = (f32[256,512]{1,0:T(8,128)S(1)}, s32[2]{0:T(128)S(1)}) custom-call(bf16[2,640,256]{2,1,0:T(8,128)(2,1)} %collective-permute-done.1.refs_0_.rest_1_, s32[2,256]{1,0:T(2,128)S(1)} %pad_add_fusion.refs_1_, s32[2,256]{1,0:T(2,128)S(1)} %collective-permute-done.4.refs_2_), custom_call_target="tpu_custom_call" | custom-call | flops 1000000000 | bytes 3333333 | tf_op jit(solution)/shard_map/mask/pallas_call | solution.py:295
  38.4 0.9 %copy-done.2 = bf16[8,256,640]{2,1,0:T(8,128)(2,1)S(1)} copy-done((bf16[8,256,640]{2,1,0:T(8,128)(2,1)S(1)}, bf16[8,256,640]{2,1,0:T(8,128)(2,1)}, u32[]{:S(2)}) %copy-start.2) | copy-done | bytes 2621464
  39.3 2.3 %project.6.rest_5_ = f32[2,512,256]{2,1,0:T(8,128)S(1)} custom-call(s32[3]{0:T(128)S(1)} %pad_add_fusion.1.place, bf16[8,256,640]{2,1,0:T(8,128)(2,1)S(1)} %norm.2.own, bf16[8,256,640]{2,1,0:T(8,128)(2,1)S(1)} %copy-done.2, bf16[640,256]{1,0:T(8,128)(2,1)} %collective-permute-done.8.rest_0_.rest_3_, bf16[640,256]{1,0:T(8,128)(2,1)} %collective-permute-done.2.rest_1_, ...), custom_call_target="tpu_custom_call" | custom-call | flops 335544320 | bytes 1310720 | tf_op jit(solution)/shard_map/project/pallas_call | solution.py:255
  41.7 0.0 copy-start.8
  41.7 1.6 %collective-permute-start.10 = (bf16[640,256]{1,0:T(8,128)(2,1)S(1)}, bf16[640,256]{1,0:T(8,128)(2,1)S(1)}, u32[]{:S(2)}, u32[]{:S(2)}) collective-permute-start(bf16[640,256]{1,0:T(8,128)(2,1)S(1)} %collective-permute-done.7.rest_0_), channel_id=1, source_target_pairs={{0,4},{4,0},{1,5},{5,1},{2,6},{6,2},{3,7},{7,3},{8,12},{12,8},{9,1... | collective-permute-start | bytes 983048 | tf_op jit(solution)/shard_map/ppermute | solution.py:182
  43.2 0.6 collective-permute-start.15
  43.8 0.5 collective-permute-start.16
  44.3 4.0 %collective-permute-done.13.rest_4_ = bf16[640,256]{1,0:T(8,128)(2,1)S(1)} collective-permute-done((bf16[640,256]{1,0:T(8,128)(2,1)}, bf16[640,256]{1,0:T(8,128)(2,1)S(1)}, u32[]{:S(2)}, u32[]{:S(2)}) %collective-permute-start.13) | collective-permute-done | bytes 327712 | tf_op jit(solution)/shard_map/ppermute | solution.py:182
  48.3 3.1 %project.7.rest_4_ = f32[2,512,256]{2,1,0:T(8,128)S(1)} custom-call(s32[3]{0:T(128)S(1)} %pad_add_fusion.1.place, bf16[8,256,640]{2,1,0:T(8,128)(2,1)S(1)} %norm.2.own, bf16[8,256,640]{2,1,0:T(8,128)(2,1)S(1)} %copy-done.2, bf16[640,256]{1,0:T(8,128)(2,1)S(1)} %collective-permute-done.11.rest_0_.rest_2_, bf16[640,256]{1,0:T(8,128)(2,1)} %collective-permute-done.6.rest_1_, ...), custom_call_target="tpu_custom_call" | custom-call | flops 5368709120 | bytes 20971520 | tf_op jit(solution)/shard_map/project/pallas_call | solution.py:255
  51.4 1.0 %collective-permute-done.10.rest_0_ = bf16[640,256]{1,0:T(8,128)(2,1)S(1)} collective-permute-done((bf16[640,256]{1,0:T(8,128)(2,1)S(1)}, bf16[640,256]{1,0:T(8,128)(2,1)S(1)}, u32[]{:S(2)}, u32[]{:S(2)}) %collective-permute-start.10) | collective-permute-done | bytes 327712 | tf_op jit(solution)/shard_map/ppermute | solution.py:182
  52.4 0.6 collective-permute-start.14
  52.9 1.0 %fusion = (f32[512,64]{1,0:T(8,128)S(1)}, f32[512,64]{1,0:T(8,128)S(1)}, f32[512,64]{1,0:T(8,128)S(1)}) fusion(f32[64]{0:T(128)S(1)} %copy-done.8, f32[512]{0:T(512)S(1)} %add_convert_fusion), kind=kLoop, calls=%fused_computation.11 | loop fusion | flops 65536 | bytes 395520 | tf_op jit(solution)/shard_map/neg | solution.py:331
  53.9 0.1 pad_maximum_fusion.1.rest_3_
  54.1 0.1 pad_maximum_fusion.2.rest_4_
  54.2 0.0 copy-start.5
  54.2 1.1 %collective-permute-done.15.rest_1_ = bf16[640,256]{1,0:T(8,128)(2,1)S(1)} collective-permute-done((bf16[640,256]{1,0:T(8,128)(2,1)S(1)}, bf16[640,256]{1,0:T(8,128)(2,1)S(1)}, u32[]{:S(2)}, u32[]{:S(2)}) %collective-permute-start.15) | collective-permute-done | bytes 327712 | tf_op jit(solution)/shard_map/ppermute | solution.py:182
  55.3 1.7 %collective-permute-done.16.rest_3_ = bf16[640,256]{1,0:T(8,128)(2,1)S(1)} collective-permute-done((bf16[640,256]{1,0:T(8,128)(2,1)S(1)}, bf16[640,256]{1,0:T(8,128)(2,1)S(1)}, u32[]{:S(2)}, u32[]{:S(2)}) %collective-permute-start.16) | collective-permute-done | bytes 327712 | tf_op jit(solution)/shard_map/ppermute | solution.py:182
  57.0 2.5 %project.8.rest_2_ = f32[2,512,256]{2,1,0:T(8,128)S(1)} custom-call(s32[3]{0:T(128)S(1)} %pad_add_fusion.1.place, bf16[8,256,640]{2,1,0:T(8,128)(2,1)S(1)} %norm.2.own, bf16[8,256,640]{2,1,0:T(8,128)(2,1)S(1)} %copy-done.2, bf16[640,256]{1,0:T(8,128)(2,1)S(1)} %collective-permute-done.7.rest_0_, bf16[640,256]{1,0:T(8,128)(2,1)S(1)} %collective-permute-done.15.rest_1_, ...), custom_call_target="tpu_custom_call" | custom-call | flops 671088640 | bytes 2621440 | tf_op jit(solution)/shard_map/project/pallas_call | solution.py:255
  59.5 0.9 %collective-permute-done.14.rest_1_ = bf16[640,256]{1,0:T(8,128)(2,1)S(1)} collective-permute-done((bf16[640,256]{1,0:T(8,128)(2,1)S(1)}, bf16[640,256]{1,0:T(8,128)(2,1)S(1)}, u32[]{:S(2)}, u32[]{:S(2)}) %collective-permute-start.14) | collective-permute-done | bytes 327712 | tf_op jit(solution)/shard_map/ppermute | solution.py:182
  60.5 2.1 %project.9 = (bf16[256,512]{1,0:T(8,128)(2,1)S(1)}, bf16[256,512]{1,0:T(8,128)(2,1)S(1)}) custom-call(s32[3]{0:T(128)S(1)} %pad_add_fusion.1.place, bf16[8,256,640]{2,1,0:T(8,128)(2,1)S(1)} %norm.2.own, bf16[8,256,640]{2,1,0:T(8,128)(2,1)S(1)} %copy-done.2, bf16[640,256]{1,0:T(8,128)(2,1)S(1)} %collective-permute-done.10.rest_0_, ...), custom_call_target="tpu_custom_call" | custom-call | flops 335544320 | bytes 1310720 | tf_op jit(solution)/shard_map/project/pallas_call | solution.py:255
  62.5 0.6 collective-permute-start.19
  63.1 1.6 %collective-permute-start.18 = (bf16[256,512]{1,0:T(8,128)(2,1)S(1)}, bf16[256,512]{1,0:T(8,128)(2,1)S(1)}, u32[]{:S(2)}, u32[]{:S(2)}) collective-permute-start(bf16[256,512]{1,0:T(8,128)(2,1)S(1)} %get-tuple-element.41), channel_id=1, source_target_pairs={{0,3},{1,2},{2,1},{3,0},{4,7},{5,6},{6,5},{7,4},{8,11},{9,10},{10,... | collective-permute-start | bytes 786440 | tf_op jit(solution)/shard_map/ppermute | solution.py:205
  64.7 7.0 %collective-permute-done.19.rest_1_ = bf16[256,512]{1,0:T(8,128)(2,1)S(1)} collective-permute-done((bf16[256,512]{1,0:T(8,128)(2,1)S(1)}, bf16[256,512]{1,0:T(8,128)(2,1)S(1)}, u32[]{:S(2)}, u32[]{:S(2)}) %collective-permute-start.19) | collective-permute-done | bytes 262176 | tf_op jit(solution)/shard_map/ppermute | solution.py:205
  71.7 4.7 %attend.2.rest_2_ = bf16[256,4096]{1,0:T(8,128)(2,1)} custom-call(s32[1]{0:T(128)} %bitcast.place, s32[2]{0:T(128)S(1)} %get-tuple-element.30.needs, bf16[256,4096]{1,0:T(8,128)(2,1)S(1)} %bitcast.22, f32[256,512]{1,0:T(8,128)S(1)} %get-tuple-element.35.bias, bf16[256,512]{1,0:T(8,128)(2,1)S(1)} %get-tuple-element.42.rest_0_, ...), custom_call_target="tpu_custom_call" | custom-call | flops 1073741824 | bytes 2097152 | tf_op jit(solution)/shard_map/attend/pallas_call | solution.py:344
  76.4 4.9 %attend.3 = bf16[256,4096]{1,0:T(8,128)(2,1)} custom-call(s32[1]{0:T(128)} %bitcast.place, s32[2]{0:T(128)S(1)} %get-tuple-element.30.needs, bf16[256,4096]{1,0:T(8,128)(2,1)S(1)} %bitcast.23, f32[256,512]{1,0:T(8,128)S(1)} %get-tuple-element.35.bias, bf16[256,512]{1,0:T(8,128)(2,1)S(1)} %collective-permute-done.17.rest_0_, ...), custom_call_target="tpu_custom_call", output_to_operand_aliasing={{}: (6, {})} | custom-call | flops 1073741824 | bytes 2097152 | tf_op jit(solution)/shard_map/attend/pallas_call | solution.py:344
  (33 shorter events, 0.2 us)
Async XLA Ops:
  0.0 7.8 %copy-start.7 = (s32[1,256]{1,0:T(1,128)S(1)}, s32[1,256]{1,0:T(1,128)}, u32[]{:S(2)}) copy-start(s32[1,256]{1,0:T(1,128)} %param.15) | copy-start | bytes 3076
  0.0 7.8 %copy-start.6 = (s32[1,256]{1,0:T(1,128)S(1)}, s32[1,256]{1,0:T(1,128)}, u32[]{:S(2)}) copy-start(s32[1,256]{1,0:T(1,128)} %param.16) | copy-start | bytes 3076
  0.0 9.4 %copy-start.4 = (f32[5120]{0:T(1024)S(1)}, f32[5120]{0:T(1024)}, u32[]{:S(2)}) copy-start(f32[5120]{0:T(1024)} %param.11) | copy-start | bytes 61444
  1.3 1.8 %collective-permute-start = (bf16[2,320,256]{2,1,0:T(8,128)(2,1)S(1)}, bf16[2,320,256]{2,1,0:T(8,128)(2,1)S(1)}, u32[]{:S(2)}, u32[]{:S(2)}) collective-permute-start(bf16[2,320,256]{2,1,0:T(8,128)(2,1)S(1)} %pad_maximum_fusion), channel_id=1, source_target_pairs={{0,2},{2,0},{1,3},{3,1},{4,6},{6,4},{5,7},{7,5},{8,10},{10,8},{9,1... | collective-permute-start | bytes 983048 | tf_op jit(solution)/shard_map/ppermute | solution.py:182
  3.1 9.3 %collective-permute-start.3 = (bf16[1,256,5120]{2,1,0:T(8,128)(2,1)}, bf16[1,256,5120]{2,1,0:T(8,128)(2,1)}, u32[]{:S(2)}, u32[]{:S(2)}) collective-permute-start(bf16[1,256,5120]{2,1,0:T(8,128)(2,1)} %param.9), channel_id=1, source_target_pairs={{0,2},{2,0},{1,3},{3,1},{4,6},{6,4},{5,7},{7,5},{8,10},{10,8},{9,1... | collective-permute-start | bytes 7864328 | tf_op jit(solution)/shard_map/ppermute | solution.py:182
  3.6 13.2 %collective-permute-start.2 = (bf16[640,256]{1,0:T(8,128)(2,1)S(1)}, bf16[640,256]{1,0:T(8,128)(2,1)}, u32[]{:S(2)}, u32[]{:S(2)}) collective-permute-start(bf16[640,256]{1,0:T(8,128)(2,1)S(1)} %dynamic-slice_bitcast_fusion), channel_id=1, source_target_pairs={{0,8},{8,24},{24,16},{16,0},{1,9},{9,25},{25,17},{17,1},{2,10},{10... | collective-permute-start | bytes 983048 | tf_op jit(solution)/shard_map/ppermute | solution.py:291
  6.3 24.1 %collective-permute-start.1 = (bf16[2,640,256]{2,1,0:T(8,128)(2,1)S(1)}, bf16[2,640,256]{2,1,0:T(8,128)(2,1)}, u32[]{:S(2)}, u32[]{:S(2)}) collective-permute-start(bf16[2,640,256]{2,1,0:T(8,128)(2,1)S(1)} %constant_dynamic-update-slice_fusion.rest_0_), channel_id=1, source_target_pairs={{0,4},{4,0},{1,5},{5,1},{2,6},{6,2},{3,7},{7,3},{8,12},{12,8},{9,1... | collective-permute-start | bytes 1966088 | tf_op jit(solution)/shard_map/ppermute | solution.py:182
  7.9 8.9 %collective-permute-start.4 = (s32[2,256]{1,0:T(2,128)S(1)}, s32[2,256]{1,0:T(2,128)S(1)}, u32[]{:S(2)}, u32[]{:S(2)}) collective-permute-start(s32[2,256]{1,0:T(2,128)S(1)} %pad_add_fusion.refs_1_), channel_id=1, source_target_pairs={{0,1},{1,0},{2,3},{3,2},{4,5},{5,4},{6,7},{7,6},{8,9},{9,8},{10,11... | collective-permute-start | bytes 6152 | tf_op jit(solution)/shard_map/ppermute | solution.py:205
  9.4 7.4 %collective-permute-start.5 = (s32[2,256]{1,0:T(2,128)S(1)}, s32[2,256]{1,0:T(2,128)S(1)}, u32[]{:S(2)}, u32[]{:S(2)}) collective-permute-start(s32[2,256]{1,0:T(2,128)S(1)} %pad_add_fusion.refs_1_), channel_id=1, source_target_pairs={{0,2},{2,0},{1,3},{3,1},{4,6},{6,4},{5,7},{7,5},{8,10},{10,8},{9,1... | collective-permute-start | bytes 6152 | tf_op jit(solution)/shard_map/ppermute | solution.py:182
  15.3 1.5 %copy-start = (bf16[8,256,640]{2,1,0:T(8,128)(2,1)}, bf16[8,256,640]{2,1,0:T(8,128)(2,1)S(1)}, u32[]{:S(2)}) copy-start(bf16[8,256,640]{2,1,0:T(8,128)(2,1)S(1)} %norm.3.other) | copy-start | bytes 7864324
  16.8 11.4 %collective-permute-start.6 = (bf16[640,256]{1,0:T(8,128)(2,1)}, bf16[640,256]{1,0:T(8,128)(2,1)}, u32[]{:S(2)}, u32[]{:S(2)}) collective-permute-start(bf16[640,256]{1,0:T(8,128)(2,1)} %collective-permute-done.2.rest_1_), channel_id=1, source_target_pairs={{0,8},{8,24},{24,16},{16,0},{1,9},{9,25},{25,17},{17,1},{2,10},{10... | collective-permute-start | bytes 983048 | tf_op jit(solution)/shard_map/ppermute | solution.py:291
  19.4 11.5 %collective-permute-start.8 = (bf16[640,256]{1,0:T(8,128)(2,1)}, bf16[640,256]{1,0:T(8,128)(2,1)}, u32[]{:S(2)}, u32[]{:S(2)}) collective-permute-start(bf16[640,256]{1,0:T(8,128)(2,1)} %collective-permute-done.2.rest_1_), channel_id=1, source_target_pairs={{0,4},{4,0},{1,5},{5,1},{2,6},{6,2},{3,7},{7,3},{8,12},{12,8},{9,1... | collective-permute-start | bytes 983048 | tf_op jit(solution)/shard_map/ppermute | solution.py:182
  19.9 18.5 %collective-permute-start.9 = (bf16[640,256]{1,0:T(8,128)(2,1)}, bf16[640,256]{1,0:T(8,128)(2,1)S(1)}, u32[]{:S(2)}, u32[]{:S(2)}) collective-permute-start(bf16[640,256]{1,0:T(8,128)(2,1)} %collective-permute-done.2.rest_1_), channel_id=1, source_target_pairs={{0,1},{1,0},{2,3},{3,2},{4,5},{5,4},{6,7},{7,6},{8,9},{9,8},{10,11... | collective-permute-start | bytes 983048 | tf_op jit(solution)/shard_map/ppermute | solution.py:182
  28.2 13.5 %collective-permute-start.7 = (bf16[640,256]{1,0:T(8,128)(2,1)}, bf16[640,256]{1,0:T(8,128)(2,1)S(1)}, u32[]{:S(2)}, u32[]{:S(2)}) collective-permute-start(bf16[640,256]{1,0:T(8,128)(2,1)} %collective-permute-done.6.rest_1_), channel_id=1, source_target_pairs={{0,8},{8,24},{24,16},{16,0},{1,9},{9,25},{25,17},{17,1},{2,10},{10... | collective-permute-start | bytes 983048 | tf_op jit(solution)/shard_map/ppermute | solution.py:291
  29.9 14.4 %collective-permute-start.11 = (bf16[640,256]{1,0:T(8,128)(2,1)}, bf16[640,256]{1,0:T(8,128)(2,1)S(1)}, u32[]{:S(2)}, u32[]{:S(2)}) collective-permute-start(bf16[640,256]{1,0:T(8,128)(2,1)} %collective-permute-done.6.rest_1_), channel_id=1, source_target_pairs={{0,4},{4,0},{1,5},{5,1},{2,6},{6,2},{3,7},{7,3},{8,12},{12,8},{9,1... | collective-permute-start | bytes 983048 | tf_op jit(solution)/shard_map/ppermute | solution.py:182
  30.4 13.4 %collective-permute-start.12 = (bf16[640,256]{1,0:T(8,128)(2,1)}, bf16[640,256]{1,0:T(8,128)(2,1)S(1)}, u32[]{:S(2)}, u32[]{:S(2)}) collective-permute-start(bf16[640,256]{1,0:T(8,128)(2,1)} %collective-permute-done.6.rest_1_), channel_id=1, source_target_pairs={{0,1},{1,0},{2,3},{3,2},{4,5},{5,4},{6,7},{7,6},{8,9},{9,8},{10,11... | collective-permute-start | bytes 983048 | tf_op jit(solution)/shard_map/ppermute | solution.py:182
  30.9 17.3 %collective-permute-start.13 = (bf16[640,256]{1,0:T(8,128)(2,1)}, bf16[640,256]{1,0:T(8,128)(2,1)S(1)}, u32[]{:S(2)}, u32[]{:S(2)}) collective-permute-start(bf16[640,256]{1,0:T(8,128)(2,1)} %collective-permute-done.8.rest_0_.rest_3_), channel_id=1, source_target_pairs={{0,1},{1,0},{2,3},{3,2},{4,5},{5,4},{6,7},{7,6},{8,9},{9,8},{10,11... | collective-permute-start | bytes 983048 | tf_op jit(solution)/shard_map/ppermute | solution.py:182
  32.5 1.7 %copy-start.1 = (bf16[8,256,640]{2,1,0:T(8,128)(2,1)S(1)}, bf16[8,256,640]{2,1,0:T(8,128)(2,1)}, u32[]{:S(2)}) copy-start(bf16[8,256,640]{2,1,0:T(8,128)(2,1)} %copy-done) | copy-start | bytes 7864324
  37.6 1.7 %copy-start.2 = (bf16[8,256,640]{2,1,0:T(8,128)(2,1)S(1)}, bf16[8,256,640]{2,1,0:T(8,128)(2,1)}, u32[]{:S(2)}) copy-start(bf16[8,256,640]{2,1,0:T(8,128)(2,1)} %copy-done) | copy-start | bytes 7864324
  41.7 11.3 %copy-start.8 = (f32[64]{0:T(128)S(1)}, f32[64]{0:T(128)}, u32[]{:S(2)}) copy-start(f32[64]{0:T(128)} %constant.45) | copy-start | bytes 772
  41.7 10.7 %collective-permute-start.10 = (bf16[640,256]{1,0:T(8,128)(2,1)S(1)}, bf16[640,256]{1,0:T(8,128)(2,1)S(1)}, u32[]{:S(2)}, u32[]{:S(2)}) collective-permute-start(bf16[640,256]{1,0:T(8,128)(2,1)S(1)} %collective-permute-done.7.rest_0_), channel_id=1, source_target_pairs={{0,4},{4,0},{1,5},{5,1},{2,6},{6,2},{3,7},{7,3},{8,12},{12,8},{9,1... | collective-permute-start | bytes 983048 | tf_op jit(solution)/shard_map/ppermute | solution.py:182
  43.2 12.0 %collective-permute-start.15 = (bf16[640,256]{1,0:T(8,128)(2,1)S(1)}, bf16[640,256]{1,0:T(8,128)(2,1)S(1)}, u32[]{:S(2)}, u32[]{:S(2)}) collective-permute-start(bf16[640,256]{1,0:T(8,128)(2,1)S(1)} %collective-permute-done.7.rest_0_), channel_id=1, source_target_pairs={{0,1},{1,0},{2,3},{3,2},{4,5},{5,4},{6,7},{7,6},{8,9},{9,8},{10,11... | collective-permute-start | bytes 983048 | tf_op jit(solution)/shard_map/ppermute | solution.py:182
  43.8 13.2 %collective-permute-start.16 = (bf16[640,256]{1,0:T(8,128)(2,1)S(1)}, bf16[640,256]{1,0:T(8,128)(2,1)S(1)}, u32[]{:S(2)}, u32[]{:S(2)}) collective-permute-start(bf16[640,256]{1,0:T(8,128)(2,1)S(1)} %collective-permute-done.12.rest_2_), channel_id=1, source_target_pairs={{0,4},{4,0},{1,5},{5,1},{2,6},{6,2},{3,7},{7,3},{8,12},{12,8},{9,1... | collective-permute-start | bytes 983048 | tf_op jit(solution)/shard_map/ppermute | solution.py:182
  52.4 8.1 %collective-permute-start.14 = (bf16[640,256]{1,0:T(8,128)(2,1)S(1)}, bf16[640,256]{1,0:T(8,128)(2,1)S(1)}, u32[]{:S(2)}, u32[]{:S(2)}) collective-permute-start(bf16[640,256]{1,0:T(8,128)(2,1)S(1)} %collective-permute-done.10.rest_0_), channel_id=1, source_target_pairs={{0,1},{1,0},{2,3},{3,2},{4,5},{5,4},{6,7},{7,6},{8,9},{9,8},{10,11... | collective-permute-start | bytes 983048 | tf_op jit(solution)/shard_map/ppermute | solution.py:182
  54.2 6.2 %copy-start.5 = (f32[128]{0:T(128)S(1)}, f32[128]{0:T(128)}, u32[]{:S(2)}) copy-start(f32[128]{0:T(128)} %param.12) | copy-start | bytes 1540
  60.5 11.3 %copy-start.3 = (bf16[1,256,4096]{2,1,0:T(8,128)(2,1)S(1)}, bf16[1,256,4096]{2,1,0:T(8,128)(2,1)}, u32[]{:S(2)}) copy-start(bf16[1,256,4096]{2,1,0:T(8,128)(2,1)} %param.10) | copy-start | bytes 6291460
  62.5 9.2 %collective-permute-start.19 = (bf16[256,512]{1,0:T(8,128)(2,1)S(1)}, bf16[256,512]{1,0:T(8,128)(2,1)S(1)}, u32[]{:S(2)}, u32[]{:S(2)}) collective-permute-start(bf16[256,512]{1,0:T(8,128)(2,1)S(1)} %get-tuple-element.42.rest_0_), channel_id=1, source_target_pairs={{0,1},{1,0},{2,3},{3,2},{4,5},{5,4},{6,7},{7,6},{8,9},{9,8},{10,11... | collective-permute-start | bytes 786440 | tf_op jit(solution)/shard_map/ppermute | solution.py:205
  63.1 13.3 %collective-permute-start.17 = (bf16[256,512]{1,0:T(8,128)(2,1)S(1)}, bf16[256,512]{1,0:T(8,128)(2,1)S(1)}, u32[]{:S(2)}, u32[]{:S(2)}) collective-permute-start(bf16[256,512]{1,0:T(8,128)(2,1)S(1)} %get-tuple-element.41), channel_id=1, source_target_pairs={{0,2},{1,3},{2,0},{3,1},{4,6},{5,7},{6,4},{7,5},{8,10},{9,11},{10,... | collective-permute-start | bytes 786440 | tf_op jit(solution)/shard_map/ppermute | solution.py:205
  63.1 13.3 %collective-permute-start.18 = (bf16[256,512]{1,0:T(8,128)(2,1)S(1)}, bf16[256,512]{1,0:T(8,128)(2,1)S(1)}, u32[]{:S(2)}, u32[]{:S(2)}) collective-permute-start(bf16[256,512]{1,0:T(8,128)(2,1)S(1)} %get-tuple-element.41), channel_id=1, source_target_pairs={{0,3},{1,2},{2,1},{3,0},{4,7},{5,6},{6,5},{7,4},{8,11},{9,10},{10,... | collective-permute-start | bytes 786440 | tf_op jit(solution)/shard_map/ppermute | solution.py:205

commit v2 on v0

--- a/solution.py
+++ b/solution.py
@@ -24,7 +24,7 @@
 MASK_COST = 1 * 10**9
 
 
-def norm_kernel(chunks, hidden, gain, out, held, sems):
+def norm_kernel(chunks, hidden, gain, out, token, held, sems):
     steps = held.shape[0] // NORM_ROWS
     copies = []
     for i in range(steps):
@@ -40,6 +40,7 @@
         rows = normed.shape[1] // chunks
         for j in range(chunks):
             out[j, at, :] = normed[:, j * rows : (j + 1) * rows]
+    token[...] = jnp.zeros_like(token)
 
 
 def project_kernel(groups, alone, first, last, count, place, own, other, *rest):
@@ -98,7 +99,7 @@
 
 
 def mask_kernel(*refs):
-    pieces, (bias, needs) = refs[1:-2], refs[-2:]
+    pieces, (bias, needs) = refs[3:-2], refs[-2:]
     count = bias.shape[0]
     size = count // TILES
     seg_q, pos_q = (
@@ -217,9 +218,12 @@
     def norm(array):
         return pl.pallas_call(
             functools.partial(norm_kernel, chunks),
-            out_shape=jax.ShapeDtypeStruct((chunks, count, rows), bf16),
+            out_shape=[
+                jax.ShapeDtypeStruct((chunks, count, rows), bf16),
+                jax.ShapeDtypeStruct((8, 128), jnp.float32),
+            ],
             in_specs=[pl.BlockSpec(memory_space=pltpu.HBM), whole],
-            out_specs=whole,
+            out_specs=[whole] * 2,
             scratch_shapes=[
                 pltpu.VMEM((count, width), bf16),
                 pltpu.SemaphoreType.DMA((count // NORM_ROWS,)),
@@ -231,7 +235,8 @@
             name="norm",
         )(array[0], norm_gain[None])
 
-    normed, normed_other = norm(hidden), norm(swap(hidden, "core"))
+    normed, token = norm(hidden)
+    normed_other, token_other = norm(swap(hidden, "core"))
     ints = jnp.concatenate([segment, position])
     ints_all = [ints] + [along_ctx(ints, d) for d in range(1, m)]
     ints_other = swap(ints, "core")
@@ -285,22 +290,22 @@
     for k in range(1, chips_z):
         mine[k] = lax.ppermute(mine[k - 1], "z", ring)
         if k == 1:
-            tied = tie((mine[k], normed, normed_other, ints_all, ints_other))
-            mine[k], normed, normed_other, ints_all, ints_other = tied
+            tied = tie((mine[k], token, token_other, ints_all, ints_other))
+            mine[k], token, token_other, ints_all, ints_other = tied
             bias, needs = pl.pallas_call(
                 mask_kernel,
                 out_shape=[
                     jax.ShapeDtypeStruct((count, m * count), jnp.float32),
                     jax.ShapeDtypeStruct((TILES,), jnp.int32),
                 ],
-                in_specs=[pl.BlockSpec(memory_space=pltpu.HBM)] + [whole] * m,
+                in_specs=[pl.BlockSpec(memory_space=pltpu.HBM)] * 3 + [whole] * m,
                 out_specs=[whole, pl.BlockSpec(memory_space=pltpu.SMEM)],
                 compiler_params=params,
                 cost_estimate=pl.CostEstimate(
                     flops=MASK_COST, bytes_accessed=MASK_COST // 300, transcendentals=0
                 ),
                 name="mask",
-            )(chip_beside, *ints_all)
+            )(chip_beside, token, token_other, *ints_all)
         elif k > 2:
             if acc is None:
                 acc = project([(0, True), (0, False)])

time: 81.1 us -> 81.1 us (level)
  no operation moved by 1% of the time
where the time goes in v2:
time: 81.1 us; the launch traced here: 80.8 us
  Pallas kernels  29.1 us (36%)
  waiting for transfers between devices  24.6 us (30%)
  starting transfers between devices  20.1 us (25%)
  local copies, waits for them, and re-layouts  5.46 us (7%)
  other arithmetic  1.42 us (2%)
    pallas_call x5, Pallas kernels, project(): pl.pallas_call(functools.partial(project_kernel, groups, also is None, ac...  13.3 us
    ppermute x13, waiting for transfers between devices, swap(): return lax.ppermute(array, axis, [(0, 1), (1, 0)])  9.85 us
    pallas_call x2, Pallas kernels, on_device(): pl.pallas_call(functools.partial(attend_kernel, m, count), out_shape=jax....  9.62 us
    ppermute x13, starting transfers between devices, swap(): return lax.ppermute(array, axis, [(0, 1), (1, 0)])  9.22 us
    ppermute x3, waiting for transfers between devices, on_device(): mine[k] = lax.ppermute(mine[k - 1], 'z', ring)  7.71 us
    ppermute x3, starting transfers between devices, on_device(): mine[k] = lax.ppermute(mine[k - 1], 'z', ring)  7.11 us
    ppermute x4, waiting for transfers between devices, along_ctx(): return lax.ppermute(array, ('core', 'ctx', 'x'), pairs)  7.01 us
    pallas_call x2, Pallas kernels, norm(): pl.pallas_call(functools.partial(norm_kernel, chunks), out_shape=[jax.Sha...  5.27 us
  transfers between devices with their start and end apart: 20, of which 8 were waited for; matrix products, arithmetic and copies ran while one was open for 2% of the time, Pallas kernels for 27%

profile of v2, /device:TPU:0, one launch (start us, length us, event | category | flops | bytes accessed | tf_op | source)
XLA Modules:
  0.0 80.8 jit_solution(1040752203812612753)
XLA Ops:
  0.0 1.2 %dynamic-slice_bitcast_fusion.1 = (bf16[1,320,256]{2,1,0:T(8,128)(2,1)S(1)}, bf16[1,320,256]{2,1,0:T(8,128)(2,1)S(1)}, bf16[1,320,256]{2,1,0:T(8,128)(2,1)S(1)}, bf16[1,320,256]{2,1,0:T(8,128)(2,1)S(1)}) fusion(bf16[320,512]{1,0:T(8,128)(2,1)} %param.14, s32[]{:T(128)S(6)} %select_n.31, s32[]{:T(128)S(6)} %select_n.29, bf16[320,512]{1,0:T(8,128)(2,1)} %param.13), kind=kLoop, calls=%fused_computation.7 | loop fusion | bytes 1310728 | tf_op jit(solution)/shard_map/stack | solution.py:206
  1.3 0.5 collective-permute-start
  1.9 1.2 %collective-permute-done = bf16[2,320,256]{2,1,0:T(8,128)(2,1)S(1)} collective-permute-done((bf16[2,320,256]{2,1,0:T(8,128)(2,1)S(1)}, bf16[2,320,256]{2,1,0:T(8,128)(2,1)S(1)}, u32[]{:S(2)}, u32[]{:S(2)}) %collective-permute-start) | collective-permute-done | bytes 327712 | tf_op jit(solution)/shard_map/ppermute | solution.py:179
  3.1 0.4 collective-permute-start.3
  3.6 2.8 %collective-permute-start.2 = (bf16[640,256]{1,0:T(8,128)(2,1)S(1)}, bf16[640,256]{1,0:T(8,128)(2,1)}, u32[]{:S(2)}, u32[]{:S(2)}) collective-permute-start(bf16[640,256]{1,0:T(8,128)(2,1)S(1)} %dynamic-slice_bitcast_fusion), channel_id=1, source_target_pairs={{0,8},{8,24},{24,16},{16,0},{1,9},{9,25},{25,17},{17,1},{2,10},{10... | collective-permute-start | bytes 983048 | tf_op jit(solution)/shard_map/ppermute | solution.py:291
  6.3 1.5 %collective-permute-start.1 = (bf16[2,640,256]{2,1,0:T(8,128)(2,1)S(1)}, bf16[2,640,256]{2,1,0:T(8,128)(2,1)}, u32[]{:S(2)}, u32[]{:S(2)}) collective-permute-start(bf16[2,640,256]{2,1,0:T(8,128)(2,1)S(1)} %constant_dynamic-update-slice_fusion.rest_0_), channel_id=1, source_target_pairs={{0,4},{4,0},{1,5},{5,1},{2,6},{6,2},{3,7},{7,3},{8,12},{12,8},{9,1... | collective-permute-start | bytes 1966088 | tf_op jit(solution)/shard_map/ppermute | solution.py:179
  7.9 1.6 %collective-permute-start.4 = (s32[2,256]{1,0:T(2,128)S(1)}, s32[2,256]{1,0:T(2,128)S(1)}, u32[]{:S(2)}, u32[]{:S(2)}) collective-permute-start(s32[2,256]{1,0:T(2,128)S(1)} %pad_add_fusion.refs_3_), channel_id=1, source_target_pairs={{0,1},{1,0},{2,3},{3,2},{4,5},{5,4},{6,7},{7,6},{8,9},{9,8},{10,11... | collective-permute-start | bytes 6152 | tf_op jit(solution)/shard_map/ppermute | solution.py:202
  9.4 0.0 collective-permute-start.5
  9.4 2.6 %norm.2 = (bf16[8,256,640]{2,1,0:T(8,128)(2,1)S(1)}, f32[8,128]{1,0:T(8,128)S(1)}) custom-call(bf16[256,5120]{1,0:T(8,128)(2,1)} %bitcast.6.hidden, f32[1,5120]{1,0:T(1,128)S(1)} %bitcast.24), custom_call_target="tpu_custom_call" | custom-call | flops 5242880 | bytes 5242880 | tf_op jit(solution)/shard_map/norm/pallas_call | solution.py:219
  12.1 0.0 collective-permute-done.3
  12.1 2.6 %norm.3 = (bf16[8,256,640]{2,1,0:T(8,128)(2,1)S(1)}, f32[8,128]{1,0:T(8,128)S(1)}) custom-call(bf16[256,5120]{1,0:T(8,128)(2,1)} %bitcast.8.hidden, f32[1,5120]{1,0:T(1,128)S(1)} %bitcast.25), custom_call_target="tpu_custom_call" | custom-call | flops 5242880 | bytes 5242880 | tf_op jit(solution)/shard_map/norm/pallas_call | solution.py:219
  14.7 1.5 %copy-done = bf16[8,256,640]{2,1,0:T(8,128)(2,1)} copy-done((bf16[8,256,640]{2,1,0:T(8,128)(2,1)}, bf16[8,256,640]{2,1,0:T(8,128)(2,1)S(1)}, u32[]{:S(2)}) %copy-start) | copy-done | bytes 2621464
  16.2 2.6 %collective-permute-start.6 = (bf16[640,256]{1,0:T(8,128)(2,1)}, bf16[640,256]{1,0:T(8,128)(2,1)}, u32[]{:S(2)}, u32[]{:S(2)}) collective-permute-start(bf16[640,256]{1,0:T(8,128)(2,1)} %collective-permute-done.2.rest_1_), channel_id=1, source_target_pairs={{0,8},{8,24},{24,16},{16,0},{1,9},{9,25},{25,17},{17,1},{2,10},{10... | collective-permute-start | bytes 983048 | tf_op jit(solution)/shard_map/ppermute | solution.py:291
  18.9 0.5 collective-permute-start.8
  19.4 0.5 collective-permute-start.9
  19.9 7.7 %collective-permute-done.6.rest_1_ = bf16[640,256]{1,0:T(8,128)(2,1)} collective-permute-done((bf16[640,256]{1,0:T(8,128)(2,1)}, bf16[640,256]{1,0:T(8,128)(2,1)}, u32[]{:S(2)}, u32[]{:S(2)}) %collective-permute-start.6) | collective-permute-done | bytes 327712 | tf_op jit(solution)/shard_map/ppermute | solution.py:291
  27.6 1.7 %collective-permute-start.7 = (bf16[640,256]{1,0:T(8,128)(2,1)}, bf16[640,256]{1,0:T(8,128)(2,1)S(1)}, u32[]{:S(2)}, u32[]{:S(2)}) collective-permute-start(bf16[640,256]{1,0:T(8,128)(2,1)} %collective-permute-done.6.rest_1_), channel_id=1, source_target_pairs={{0,8},{8,24},{24,16},{16,0},{1,9},{9,25},{25,17},{17,1},{2,10},{10... | collective-permute-start | bytes 983048 | tf_op jit(solution)/shard_map/ppermute | solution.py:291
  29.3 0.5 collective-permute-start.11
  29.8 0.5 collective-permute-start.12
  30.4 1.5 %collective-permute-start.13 = (bf16[640,256]{1,0:T(8,128)(2,1)}, bf16[640,256]{1,0:T(8,128)(2,1)S(1)}, u32[]{:S(2)}, u32[]{:S(2)}) collective-permute-start(bf16[640,256]{1,0:T(8,128)(2,1)} %collective-permute-done.8.rest_0_.rest_3_), channel_id=1, source_target_pairs={{0,1},{1,0},{2,3},{3,2},{4,5},{5,4},{6,7},{7,6},{8,9},{9,8},{10,11... | collective-permute-start | bytes 983048 | tf_op jit(solution)/shard_map/ppermute | solution.py:179
  31.9 0.1 pad_add_fusion.1.place
  31.9 1.7 %copy-done.1 = bf16[8,256,640]{2,1,0:T(8,128)(2,1)S(1)} copy-done((bf16[8,256,640]{2,1,0:T(8,128)(2,1)S(1)}, bf16[8,256,640]{2,1,0:T(8,128)(2,1)}, u32[]{:S(2)}) %copy-start.1) | copy-done | bytes 2621464
  33.7 3.3 %project.5.rest_3_ = f32[2,512,256]{2,1,0:T(8,128)S(1)} custom-call(s32[3]{0:T(128)S(1)} %pad_add_fusion.1.place, bf16[8,256,640]{2,1,0:T(8,128)(2,1)S(1)} %get-tuple-element.40.own, bf16[8,256,640]{2,1,0:T(8,128)(2,1)S(1)} %copy-done.1, bf16[2,640,256]{2,1,0:T(8,128)(2,1)S(1)} %constant_dynamic-update-slice_fusion.rest_0_, ...), custom_call_target="tpu_custom_call" | custom-call | flops 671088640 | bytes 2621440 | tf_op jit(solution)/shard_map/project/pallas_call | solution.py:255
  37.0 0.8 %mask.1 = (f32[256,512]{1,0:T(8,128)S(1)}, s32[2]{0:T(128)S(1)}) custom-call(bf16[2,640,256]{2,1,0:T(8,128)(2,1)} %collective-permute-done.1.refs_0_.rest_1_, f32[8,128]{1,0:T(8,128)S(1)} %get-tuple-element.34.refs_1_, f32[8,128]{1,0:T(8,128)S(1)} %get-tuple-element.35.refs_2_, s32[2,256]{1,0:T(2,128)S(1)} %pad_add_fusion.refs_3_, ...), custom_call_target="tpu_custom_call" | custom-call | flops 1000000000 | bytes 3333333 | tf_op jit(solution)/shard_map/mask/pallas_call | solution.py:295
  37.8 0.9 %copy-done.2 = bf16[8,256,640]{2,1,0:T(8,128)(2,1)S(1)} copy-done((bf16[8,256,640]{2,1,0:T(8,128)(2,1)S(1)}, bf16[8,256,640]{2,1,0:T(8,128)(2,1)}, u32[]{:S(2)}) %copy-start.2) | copy-done | bytes 2621464
  38.7 2.3 %project.6.rest_5_ = f32[2,512,256]{2,1,0:T(8,128)S(1)} custom-call(s32[3]{0:T(128)S(1)} %pad_add_fusion.1.place, bf16[8,256,640]{2,1,0:T(8,128)(2,1)S(1)} %get-tuple-element.40.own, bf16[8,256,640]{2,1,0:T(8,128)(2,1)S(1)} %copy-done.2, bf16[640,256]{1,0:T(8,128)(2,1)} %collective-permute-done.8.rest_0_.rest_3_, ...), custom_call_target="tpu_custom_call" | custom-call | flops 335544320 | bytes 1310720 | tf_op jit(solution)/shard_map/project/pallas_call | solution.py:255
  41.1 0.0 copy-start.8
  41.1 1.8 %collective-permute-start.10 = (bf16[640,256]{1,0:T(8,128)(2,1)S(1)}, bf16[640,256]{1,0:T(8,128)(2,1)S(1)}, u32[]{:S(2)}, u32[]{:S(2)}) collective-permute-start(bf16[640,256]{1,0:T(8,128)(2,1)S(1)} %collective-permute-done.7.rest_0_), channel_id=1, source_target_pairs={{0,4},{4,0},{1,5},{5,1},{2,6},{6,2},{3,7},{7,3},{8,12},{12,8},{9,1... | collective-permute-start | bytes 983048 | tf_op jit(solution)/shard_map/ppermute | solution.py:179
  42.9 0.3 collective-permute-start.15
  43.2 0.5 collective-permute-start.16
  43.7 4.0 %collective-permute-done.13.rest_4_ = bf16[640,256]{1,0:T(8,128)(2,1)S(1)} collective-permute-done((bf16[640,256]{1,0:T(8,128)(2,1)}, bf16[640,256]{1,0:T(8,128)(2,1)S(1)}, u32[]{:S(2)}, u32[]{:S(2)}) %collective-permute-start.13) | collective-permute-done | bytes 327712 | tf_op jit(solution)/shard_map/ppermute | solution.py:179
  47.7 3.1 %project.7.rest_4_ = f32[2,512,256]{2,1,0:T(8,128)S(1)} custom-call(s32[3]{0:T(128)S(1)} %pad_add_fusion.1.place, bf16[8,256,640]{2,1,0:T(8,128)(2,1)S(1)} %get-tuple-element.40.own, bf16[8,256,640]{2,1,0:T(8,128)(2,1)S(1)} %copy-done.2, bf16[640,256]{1,0:T(8,128)(2,1)S(1)} %collective-permute-done.11.rest_0_.rest_2_, ...), custom_call_target="tpu_custom_call" | custom-call | flops 5368709120 | bytes 20971520 | tf_op jit(solution)/shard_map/project/pallas_call | solution.py:255
  50.8 1.0 %collective-permute-done.10.rest_0_ = bf16[640,256]{1,0:T(8,128)(2,1)S(1)} collective-permute-done((bf16[640,256]{1,0:T(8,128)(2,1)S(1)}, bf16[640,256]{1,0:T(8,128)(2,1)S(1)}, u32[]{:S(2)}, u32[]{:S(2)}) %collective-permute-start.10) | collective-permute-done | bytes 327712 | tf_op jit(solution)/shard_map/ppermute | solution.py:179
  51.8 0.5 collective-permute-start.14
  52.3 1.0 %fusion = (f32[512,64]{1,0:T(8,128)S(1)}, f32[512,64]{1,0:T(8,128)S(1)}, f32[512,64]{1,0:T(8,128)S(1)}) fusion(f32[64]{0:T(128)S(1)} %copy-done.8, f32[512]{0:T(512)S(1)} %add_convert_fusion), kind=kLoop, calls=%fused_computation.11 | loop fusion | flops 65536 | bytes 395520 | tf_op jit(solution)/shard_map/neg | solution.py:331
  53.3 0.1 pad_maximum_fusion.1.rest_3_
  53.5 0.1 pad_maximum_fusion.2.rest_4_
  53.6 0.0 copy-start.5
  53.6 1.1 %collective-permute-done.15.rest_1_ = bf16[640,256]{1,0:T(8,128)(2,1)S(1)} collective-permute-done((bf16[640,256]{1,0:T(8,128)(2,1)S(1)}, bf16[640,256]{1,0:T(8,128)(2,1)S(1)}, u32[]{:S(2)}, u32[]{:S(2)}) %collective-permute-start.15) | collective-permute-done | bytes 327712 | tf_op jit(solution)/shard_map/ppermute | solution.py:179
  54.7 1.8 %collective-permute-done.16.rest_3_ = bf16[640,256]{1,0:T(8,128)(2,1)S(1)} collective-permute-done((bf16[640,256]{1,0:T(8,128)(2,1)S(1)}, bf16[640,256]{1,0:T(8,128)(2,1)S(1)}, u32[]{:S(2)}, u32[]{:S(2)}) %collective-permute-start.16) | collective-permute-done | bytes 327712 | tf_op jit(solution)/shard_map/ppermute | solution.py:179
  56.6 2.5 %project.8.rest_2_ = f32[2,512,256]{2,1,0:T(8,128)S(1)} custom-call(s32[3]{0:T(128)S(1)} %pad_add_fusion.1.place, bf16[8,256,640]{2,1,0:T(8,128)(2,1)S(1)} %get-tuple-element.40.own, bf16[8,256,640]{2,1,0:T(8,128)(2,1)S(1)} %copy-done.2, bf16[640,256]{1,0:T(8,128)(2,1)S(1)} %collective-permute-done.7.rest_0_, ...), custom_call_target="tpu_custom_call" | custom-call | flops 671088640 | bytes 2621440 | tf_op jit(solution)/shard_map/project/pallas_call | solution.py:255
  59.1 0.8 collective-permute-done.14.rest_1_
  59.9 2.1 %project.9 = (bf16[256,512]{1,0:T(8,128)(2,1)S(1)}, bf16[256,512]{1,0:T(8,128)(2,1)S(1)}) custom-call(s32[3]{0:T(128)S(1)} %pad_add_fusion.1.place, bf16[8,256,640]{2,1,0:T(8,128)(2,1)S(1)} %get-tuple-element.40.own, bf16[8,256,640]{2,1,0:T(8,128)(2,1)S(1)} %copy-done.2, bf16[640,256]{1,0:T(8,128)(2,1)S(1)} %collective-permute-done.10.rest_0_, ...), custom_call_target="tpu_custom_call" | custom-call | flops 335544320 | bytes 1310720 | tf_op jit(solution)/shard_map/project/pallas_call | solution.py:255
  61.9 0.6 collective-permute-start.19
  62.5 1.6 %collective-permute-start.18 = (bf16[256,512]{1,0:T(8,128)(2,1)S(1)}, bf16[256,512]{1,0:T(8,128)(2,1)S(1)}, u32[]{:S(2)}, u32[]{:S(2)}) collective-permute-start(bf16[256,512]{1,0:T(8,128)(2,1)S(1)} %get-tuple-element.49), channel_id=1, source_target_pairs={{0,3},{1,2},{2,1},{3,0},{4,7},{5,6},{6,5},{7,4},{8,11},{9,10},{10,... | collective-permute-start | bytes 786440 | tf_op jit(solution)/shard_map/ppermute | solution.py:202
  64.2 7.0 %collective-permute-done.19.rest_1_ = bf16[256,512]{1,0:T(8,128)(2,1)S(1)} collective-permute-done((bf16[256,512]{1,0:T(8,128)(2,1)S(1)}, bf16[256,512]{1,0:T(8,128)(2,1)S(1)}, u32[]{:S(2)}, u32[]{:S(2)}) %collective-permute-start.19) | collective-permute-done | bytes 262176 | tf_op jit(solution)/shard_map/ppermute | solution.py:202
  71.2 4.7 %attend.2.rest_2_ = bf16[256,4096]{1,0:T(8,128)(2,1)} custom-call(s32[1]{0:T(128)} %bitcast.place, s32[2]{0:T(128)S(1)} %get-tuple-element.38.needs, bf16[256,4096]{1,0:T(8,128)(2,1)S(1)} %bitcast.22, f32[256,512]{1,0:T(8,128)S(1)} %get-tuple-element.43.bias, bf16[256,512]{1,0:T(8,128)(2,1)S(1)} %get-tuple-element.50.rest_0_, ...), custom_call_target="tpu_custom_call" | custom-call | flops 1073741824 | bytes 2097152 | tf_op jit(solution)/shard_map/attend/pallas_call | solution.py:344
  75.9 4.9 %attend.3 = bf16[256,4096]{1,0:T(8,128)(2,1)} custom-call(s32[1]{0:T(128)} %bitcast.place, s32[2]{0:T(128)S(1)} %get-tuple-element.38.needs, bf16[256,4096]{1,0:T(8,128)(2,1)S(1)} %bitcast.23, f32[256,512]{1,0:T(8,128)S(1)} %get-tuple-element.43.bias, bf16[256,512]{1,0:T(8,128)(2,1)S(1)} %collective-permute-done.17.rest_0_, ...), custom_call_target="tpu_custom_call", output_to_operand_aliasing={{}: (6, {})} | custom-call | flops 1073741824 | bytes 2097152 | tf_op jit(solution)/shard_map/attend/pallas_call | solution.py:344
  (33 shorter events, 0.2 us)
Async XLA Ops:
  0.0 7.8 %copy-start.7 = (s32[1,256]{1,0:T(1,128)S(1)}, s32[1,256]{1,0:T(1,128)}, u32[]{:S(2)}) copy-start(s32[1,256]{1,0:T(1,128)} %param.15) | copy-start | bytes 3076
  0.0 7.8 %copy-start.6 = (s32[1,256]{1,0:T(1,128)S(1)}, s32[1,256]{1,0:T(1,128)}, u32[]{:S(2)}) copy-start(s32[1,256]{1,0:T(1,128)} %param.16) | copy-start | bytes 3076
  0.0 9.4 %copy-start.4 = (f32[5120]{0:T(1024)S(1)}, f32[5120]{0:T(1024)}, u32[]{:S(2)}) copy-start(f32[5120]{0:T(1024)} %param.11) | copy-start | bytes 61444
  1.3 1.8 %collective-permute-start = (bf16[2,320,256]{2,1,0:T(8,128)(2,1)S(1)}, bf16[2,320,256]{2,1,0:T(8,128)(2,1)S(1)}, u32[]{:S(2)}, u32[]{:S(2)}) collective-permute-start(bf16[2,320,256]{2,1,0:T(8,128)(2,1)S(1)} %pad_maximum_fusion), channel_id=1, source_target_pairs={{0,2},{2,0},{1,3},{3,1},{4,6},{6,4},{5,7},{7,5},{8,10},{10,8},{9,1... | collective-permute-start | bytes 983048 | tf_op jit(solution)/shard_map/ppermute | solution.py:179
  3.1 9.0 %collective-permute-start.3 = (bf16[1,256,5120]{2,1,0:T(8,128)(2,1)}, bf16[1,256,5120]{2,1,0:T(8,128)(2,1)}, u32[]{:S(2)}, u32[]{:S(2)}) collective-permute-start(bf16[1,256,5120]{2,1,0:T(8,128)(2,1)} %param.9), channel_id=1, source_target_pairs={{0,2},{2,0},{1,3},{3,1},{4,6},{6,4},{5,7},{7,5},{8,10},{10,8},{9,1... | collective-permute-start | bytes 7864328 | tf_op jit(solution)/shard_map/ppermute | solution.py:179
  3.6 12.7 %collective-permute-start.2 = (bf16[640,256]{1,0:T(8,128)(2,1)S(1)}, bf16[640,256]{1,0:T(8,128)(2,1)}, u32[]{:S(2)}, u32[]{:S(2)}) collective-permute-start(bf16[640,256]{1,0:T(8,128)(2,1)S(1)} %dynamic-slice_bitcast_fusion), channel_id=1, source_target_pairs={{0,8},{8,24},{24,16},{16,0},{1,9},{9,25},{25,17},{17,1},{2,10},{10... | collective-permute-start | bytes 983048 | tf_op jit(solution)/shard_map/ppermute | solution.py:291
  6.3 23.5 %collective-permute-start.1 = (bf16[2,640,256]{2,1,0:T(8,128)(2,1)S(1)}, bf16[2,640,256]{2,1,0:T(8,128)(2,1)}, u32[]{:S(2)}, u32[]{:S(2)}) collective-permute-start(bf16[2,640,256]{2,1,0:T(8,128)(2,1)S(1)} %constant_dynamic-update-slice_fusion.rest_0_), channel_id=1, source_target_pairs={{0,4},{4,0},{1,5},{5,1},{2,6},{6,2},{3,7},{7,3},{8,12},{12,8},{9,1... | collective-permute-start | bytes 1966088 | tf_op jit(solution)/shard_map/ppermute | solution.py:179
  7.9 8.4 %collective-permute-start.4 = (s32[2,256]{1,0:T(2,128)S(1)}, s32[2,256]{1,0:T(2,128)S(1)}, u32[]{:S(2)}, u32[]{:S(2)}) collective-permute-start(s32[2,256]{1,0:T(2,128)S(1)} %pad_add_fusion.refs_3_), channel_id=1, source_target_pairs={{0,1},{1,0},{2,3},{3,2},{4,5},{5,4},{6,7},{7,6},{8,9},{9,8},{10,11... | collective-permute-start | bytes 6152 | tf_op jit(solution)/shard_map/ppermute | solution.py:202
  9.4 6.8 %collective-permute-start.5 = (s32[2,256]{1,0:T(2,128)S(1)}, s32[2,256]{1,0:T(2,128)S(1)}, u32[]{:S(2)}, u32[]{:S(2)}) collective-permute-start(s32[2,256]{1,0:T(2,128)S(1)} %pad_add_fusion.refs_3_), channel_id=1, source_target_pairs={{0,2},{2,0},{1,3},{3,1},{4,6},{6,4},{5,7},{7,5},{8,10},{10,8},{9,1... | collective-permute-start | bytes 6152 | tf_op jit(solution)/shard_map/ppermute | solution.py:179
  14.7 1.5 %copy-start = (bf16[8,256,640]{2,1,0:T(8,128)(2,1)}, bf16[8,256,640]{2,1,0:T(8,128)(2,1)S(1)}, u32[]{:S(2)}) copy-start(bf16[8,256,640]{2,1,0:T(8,128)(2,1)S(1)} %get-tuple-element.41.other) | copy-start | bytes 7864324
  16.2 11.4 %collective-permute-start.6 = (bf16[640,256]{1,0:T(8,128)(2,1)}, bf16[640,256]{1,0:T(8,128)(2,1)}, u32[]{:S(2)}, u32[]{:S(2)}) collective-permute-start(bf16[640,256]{1,0:T(8,128)(2,1)} %collective-permute-done.2.rest_1_), channel_id=1, source_target_pairs={{0,8},{8,24},{24,16},{16,0},{1,9},{9,25},{25,17},{17,1},{2,10},{10... | collective-permute-start | bytes 983048 | tf_op jit(solution)/shard_map/ppermute | solution.py:291
  18.9 11.5 %collective-permute-start.8 = (bf16[640,256]{1,0:T(8,128)(2,1)}, bf16[640,256]{1,0:T(8,128)(2,1)}, u32[]{:S(2)}, u32[]{:S(2)}) collective-permute-start(bf16[640,256]{1,0:T(8,128)(2,1)} %collective-permute-done.2.rest_1_), channel_id=1, source_target_pairs={{0,4},{4,0},{1,5},{5,1},{2,6},{6,2},{3,7},{7,3},{8,12},{12,8},{9,1... | collective-permute-start | bytes 983048 | tf_op jit(solution)/shard_map/ppermute | solution.py:179
  19.4 18.5 %collective-permute-start.9 = (bf16[640,256]{1,0:T(8,128)(2,1)}, bf16[640,256]{1,0:T(8,128)(2,1)S(1)}, u32[]{:S(2)}, u32[]{:S(2)}) collective-permute-start(bf16[640,256]{1,0:T(8,128)(2,1)} %collective-permute-done.2.rest_1_), channel_id=1, source_target_pairs={{0,1},{1,0},{2,3},{3,2},{4,5},{5,4},{6,7},{7,6},{8,9},{9,8},{10,11... | collective-permute-start | bytes 983048 | tf_op jit(solution)/shard_map/ppermute | solution.py:179
  27.6 13.5 %collective-permute-start.7 = (bf16[640,256]{1,0:T(8,128)(2,1)}, bf16[640,256]{1,0:T(8,128)(2,1)S(1)}, u32[]{:S(2)}, u32[]{:S(2)}) collective-permute-start(bf16[640,256]{1,0:T(8,128)(2,1)} %collective-permute-done.6.rest_1_), channel_id=1, source_target_pairs={{0,8},{8,24},{24,16},{16,0},{1,9},{9,25},{25,17},{17,1},{2,10},{10... | collective-permute-start | bytes 983048 | tf_op jit(solution)/shard_map/ppermute | solution.py:291
  29.3 14.4 %collective-permute-start.11 = (bf16[640,256]{1,0:T(8,128)(2,1)}, bf16[640,256]{1,0:T(8,128)(2,1)S(1)}, u32[]{:S(2)}, u32[]{:S(2)}) collective-permute-start(bf16[640,256]{1,0:T(8,128)(2,1)} %collective-permute-done.6.rest_1_), channel_id=1, source_target_pairs={{0,4},{4,0},{1,5},{5,1},{2,6},{6,2},{3,7},{7,3},{8,12},{12,8},{9,1... | collective-permute-start | bytes 983048 | tf_op jit(solution)/shard_map/ppermute | solution.py:179
  29.8 13.4 %collective-permute-start.12 = (bf16[640,256]{1,0:T(8,128)(2,1)}, bf16[640,256]{1,0:T(8,128)(2,1)S(1)}, u32[]{:S(2)}, u32[]{:S(2)}) collective-permute-start(bf16[640,256]{1,0:T(8,128)(2,1)} %collective-permute-done.6.rest_1_), channel_id=1, source_target_pairs={{0,1},{1,0},{2,3},{3,2},{4,5},{5,4},{6,7},{7,6},{8,9},{9,8},{10,11... | collective-permute-start | bytes 983048 | tf_op jit(solution)/shard_map/ppermute | solution.py:179
  30.4 17.3 %collective-permute-start.13 = (bf16[640,256]{1,0:T(8,128)(2,1)}, bf16[640,256]{1,0:T(8,128)(2,1)S(1)}, u32[]{:S(2)}, u32[]{:S(2)}) collective-permute-start(bf16[640,256]{1,0:T(8,128)(2,1)} %collective-permute-done.8.rest_0_.rest_3_), channel_id=1, source_target_pairs={{0,1},{1,0},{2,3},{3,2},{4,5},{5,4},{6,7},{7,6},{8,9},{9,8},{10,11... | collective-permute-start | bytes 983048 | tf_op jit(solution)/shard_map/ppermute | solution.py:179
  31.9 1.7 %copy-start.1 = (bf16[8,256,640]{2,1,0:T(8,128)(2,1)S(1)}, bf16[8,256,640]{2,1,0:T(8,128)(2,1)}, u32[]{:S(2)}) copy-start(bf16[8,256,640]{2,1,0:T(8,128)(2,1)} %copy-done) | copy-start | bytes 7864324
  37.0 1.7 %copy-start.2 = (bf16[8,256,640]{2,1,0:T(8,128)(2,1)S(1)}, bf16[8,256,640]{2,1,0:T(8,128)(2,1)}, u32[]{:S(2)}) copy-start(bf16[8,256,640]{2,1,0:T(8,128)(2,1)} %copy-done) | copy-start | bytes 7864324
  41.1 11.3 %copy-start.8 = (f32[64]{0:T(128)S(1)}, f32[64]{0:T(128)}, u32[]{:S(2)}) copy-start(f32[64]{0:T(128)} %constant.45) | copy-start | bytes 772
  41.1 10.7 %collective-permute-start.10 = (bf16[640,256]{1,0:T(8,128)(2,1)S(1)}, bf16[640,256]{1,0:T(8,128)(2,1)S(1)}, u32[]{:S(2)}, u32[]{:S(2)}) collective-permute-start(bf16[640,256]{1,0:T(8,128)(2,1)S(1)} %collective-permute-done.7.rest_0_), channel_id=1, source_target_pairs={{0,4},{4,0},{1,5},{5,1},{2,6},{6,2},{3,7},{7,3},{8,12},{12,8},{9,1... | collective-permute-start | bytes 983048 | tf_op jit(solution)/shard_map/ppermute | solution.py:179
  42.9 11.8 %collective-permute-start.15 = (bf16[640,256]{1,0:T(8,128)(2,1)S(1)}, bf16[640,256]{1,0:T(8,128)(2,1)S(1)}, u32[]{:S(2)}, u32[]{:S(2)}) collective-permute-start(bf16[640,256]{1,0:T(8,128)(2,1)S(1)} %collective-permute-done.7.rest_0_), channel_id=1, source_target_pairs={{0,1},{1,0},{2,3},{3,2},{4,5},{5,4},{6,7},{7,6},{8,9},{9,8},{10,11... | collective-permute-start | bytes 983048 | tf_op jit(solution)/shard_map/ppermute | solution.py:179
  43.2 13.3 %collective-permute-start.16 = (bf16[640,256]{1,0:T(8,128)(2,1)S(1)}, bf16[640,256]{1,0:T(8,128)(2,1)S(1)}, u32[]{:S(2)}, u32[]{:S(2)}) collective-permute-start(bf16[640,256]{1,0:T(8,128)(2,1)S(1)} %collective-permute-done.12.rest_2_), channel_id=1, source_target_pairs={{0,4},{4,0},{1,5},{5,1},{2,6},{6,2},{3,7},{7,3},{8,12},{12,8},{9,1... | collective-permute-start | bytes 983048 | tf_op jit(solution)/shard_map/ppermute | solution.py:179
  51.8 8.1 %collective-permute-start.14 = (bf16[640,256]{1,0:T(8,128)(2,1)S(1)}, bf16[640,256]{1,0:T(8,128)(2,1)S(1)}, u32[]{:S(2)}, u32[]{:S(2)}) collective-permute-start(bf16[640,256]{1,0:T(8,128)(2,1)S(1)} %collective-permute-done.10.rest_0_), channel_id=1, source_target_pairs={{0,1},{1,0},{2,3},{3,2},{4,5},{5,4},{6,7},{7,6},{8,9},{9,8},{10,11... | collective-permute-start | bytes 983048 | tf_op jit(solution)/shard_map/ppermute | solution.py:179
  53.6 6.3 %copy-start.5 = (f32[128]{0:T(128)S(1)}, f32[128]{0:T(128)}, u32[]{:S(2)}) copy-start(f32[128]{0:T(128)} %param.12) | copy-start | bytes 1540
  59.9 11.3 %copy-start.3 = (bf16[1,256,4096]{2,1,0:T(8,128)(2,1)S(1)}, bf16[1,256,4096]{2,1,0:T(8,128)(2,1)}, u32[]{:S(2)}) copy-start(bf16[1,256,4096]{2,1,0:T(8,128)(2,1)} %param.10) | copy-start | bytes 6291460
  61.9 9.2 %collective-permute-start.19 = (bf16[256,512]{1,0:T(8,128)(2,1)S(1)}, bf16[256,512]{1,0:T(8,128)(2,1)S(1)}, u32[]{:S(2)}, u32[]{:S(2)}) collective-permute-start(bf16[256,512]{1,0:T(8,128)(2,1)S(1)} %get-tuple-element.50.rest_0_), channel_id=1, source_target_pairs={{0,1},{1,0},{2,3},{3,2},{4,5},{5,4},{6,7},{7,6},{8,9},{9,8},{10,11... | collective-permute-start | bytes 786440 | tf_op jit(solution)/shard_map/ppermute | solution.py:202
  62.5 13.3 %collective-permute-start.17 = (bf16[256,512]{1,0:T(8,128)(2,1)S(1)}, bf16[256,512]{1,0:T(8,128)(2,1)S(1)}, u32[]{:S(2)}, u32[]{:S(2)}) collective-permute-start(bf16[256,512]{1,0:T(8,128)(2,1)S(1)} %get-tuple-element.49), channel_id=1, source_target_pairs={{0,2},{1,3},{2,0},{3,1},{4,6},{5,7},{6,4},{7,5},{8,10},{9,11},{10,... | collective-permute-start | bytes 786440 | tf_op jit(solution)/shard_map/ppermute | solution.py:202
  62.5 13.3 %collective-permute-start.18 = (bf16[256,512]{1,0:T(8,128)(2,1)S(1)}, bf16[256,512]{1,0:T(8,128)(2,1)S(1)}, u32[]{:S(2)}, u32[]{:S(2)}) collective-permute-start(bf16[256,512]{1,0:T(8,128)(2,1)S(1)} %get-tuple-element.49), channel_id=1, source_target_pairs={{0,3},{1,2},{2,1},{3,0},{4,7},{5,6},{6,5},{7,4},{8,11},{9,10},{10,... | collective-permute-start | bytes 786440 | tf_op jit(solution)/shard_map/ppermute | solution.py:202

commit v3 on v2

--- a/solution.py
+++ b/solution.py
@@ -16,7 +16,7 @@
 EPS = 1e-06
 THETA = 1000000.0
 MASKED = -1e30
-VMEM_LIMIT = 24 * 2**20
+VMEM_LIMIT = 16 * 2**20
 NORM_ROWS = 64
 WIDE = 4
 TILES = 2
@@ -238,7 +238,6 @@
     normed, token = norm(hidden)
     normed_other, token_other = norm(swap(hidden, "core"))
     ints = jnp.concatenate([segment, position])
-    ints_all = [ints] + [along_ctx(ints, d) for d in range(1, m)]
     ints_other = swap(ints, "core")
 
     acc_shape = jax.ShapeDtypeStruct((2, 2 * count, 2 * HD), jnp.float32)
@@ -290,8 +289,9 @@
     for k in range(1, chips_z):
         mine[k] = lax.ppermute(mine[k - 1], "z", ring)
         if k == 1:
-            tied = tie((mine[k], token, token_other, ints_all, ints_other))
-            mine[k], token, token_other, ints_all, ints_other = tied
+            tied = tie((mine[k], token, token_other, ints, ints_other))
+            mine[k], token, token_other, ints, ints_other = tied
+            ints_all = [ints] + [along_ctx(ints, d) for d in range(1, m)]
             bias, needs = pl.pallas_call(
                 mask_kernel,
                 out_shape=[

time: 81.1 us -> 80.4 us (level)
  waiting for transfers between devices: 24.6 us -> 23.3 us
    ppermute x13, starting transfers between devices: 9.22 us -> 10.9 us  [swap(): return lax.ppermute(array, axis, [(0, 1), (1, 0)])]
    ppermute x3, starting transfers between devices: 7.11 us -> 5.89 us  [on_device(): mine[k] = lax.ppermute(mine[k - 1], 'z', ring)]
  transfers between devices with their start and end apart: 20 -> 20, of which waited for: 8 -> 8; matrix products, arithmetic and copies ran while one was open for 2% -> 2% of each run, Pallas kernels for 27% -> 28%
where the time goes in v3:
time: 80.4 us; the launch traced here: 80 us
  Pallas kernels  29.1 us (36%)
  waiting for transfers between devices  23.3 us (29%)
  starting transfers between devices  20.5 us (25%)
  local copies, waits for them, and re-layouts  5.46 us (7%)
  other arithmetic  1.42 us (2%)
    pallas_call x5, Pallas kernels, project(): pl.pallas_call(functools.partial(project_kernel, groups, also is None, ac...  13.3 us
    ppermute x13, starting transfers between devices, swap(): return lax.ppermute(array, axis, [(0, 1), (1, 0)])  10.9 us
    pallas_call x2, Pallas kernels, on_device(): pl.pallas_call(functools.partial(attend_kernel, m, count), out_shape=jax....  9.62 us
    ppermute x13, waiting for transfers between devices, swap(): return lax.ppermute(array, axis, [(0, 1), (1, 0)])  9.06 us
    ppermute x3, waiting for transfers between devices, on_device(): mine[k] = lax.ppermute(mine[k - 1], 'z', ring)  7.28 us
    ppermute x4, waiting for transfers between devices, along_ctx(): return lax.ppermute(array, ('core', 'ctx', 'x'), pairs)  6.99 us
    ppermute x3, starting transfers between devices, on_device(): mine[k] = lax.ppermute(mine[k - 1], 'z', ring)  5.89 us
    pallas_call x2, Pallas kernels, norm(): pl.pallas_call(functools.partial(norm_kernel, chunks), out_shape=[jax.Sha...  5.27 us
  transfers between devices with their start and end apart: 20, of which 8 were waited for; matrix products, arithmetic and copies ran while one was open for 2% of the time, Pallas kernels for 28%

profile of v3, /device:TPU:0, one launch (start us, length us, event | category | flops | bytes accessed | tf_op | source)
XLA Modules:
  0.0 80.0 jit_solution(6683976882988381980)
XLA Ops:
  0.0 1.2 %dynamic-slice_bitcast_fusion.1 = (bf16[1,320,256]{2,1,0:T(8,128)(2,1)S(1)}, bf16[1,320,256]{2,1,0:T(8,128)(2,1)S(1)}, bf16[1,320,256]{2,1,0:T(8,128)(2,1)S(1)}, bf16[1,320,256]{2,1,0:T(8,128)(2,1)S(1)}) fusion(bf16[320,512]{1,0:T(8,128)(2,1)} %param.14, s32[]{:T(128)S(6)} %select_n.31, s32[]{:T(128)S(6)} %select_n.29, bf16[320,512]{1,0:T(8,128)(2,1)} %param.13), kind=kLoop, calls=%fused_computation.7 | loop fusion | bytes 1310728 | tf_op jit(solution)/shard_map/stack | solution.py:206
  1.3 0.5 collective-permute-start
  1.9 1.2 %collective-permute-done = bf16[2,320,256]{2,1,0:T(8,128)(2,1)S(1)} collective-permute-done((bf16[2,320,256]{2,1,0:T(8,128)(2,1)S(1)}, bf16[2,320,256]{2,1,0:T(8,128)(2,1)S(1)}, u32[]{:S(2)}, u32[]{:S(2)}) %collective-permute-start) | collective-permute-done | bytes 327712 | tf_op jit(solution)/shard_map/ppermute | solution.py:179
  3.1 0.4 collective-permute-start.3
  3.6 2.8 %collective-permute-start.2 = (bf16[640,256]{1,0:T(8,128)(2,1)S(1)}, bf16[640,256]{1,0:T(8,128)(2,1)}, u32[]{:S(2)}, u32[]{:S(2)}) collective-permute-start(bf16[640,256]{1,0:T(8,128)(2,1)S(1)} %dynamic-slice_bitcast_fusion), channel_id=1, source_target_pairs={{0,8},{8,24},{24,16},{16,0},{1,9},{9,25},{25,17},{17,1},{2,10},{10... | collective-permute-start | bytes 983048 | tf_op jit(solution)/shard_map/ppermute | solution.py:290
  6.3 1.5 %collective-permute-start.1 = (bf16[2,640,256]{2,1,0:T(8,128)(2,1)S(1)}, bf16[2,640,256]{2,1,0:T(8,128)(2,1)}, u32[]{:S(2)}, u32[]{:S(2)}) collective-permute-start(bf16[2,640,256]{2,1,0:T(8,128)(2,1)S(1)} %constant_dynamic-update-slice_fusion.rest_0_), channel_id=1, source_target_pairs={{0,4},{4,0},{1,5},{5,1},{2,6},{6,2},{3,7},{7,3},{8,12},{12,8},{9,1... | collective-permute-start | bytes 1966088 | tf_op jit(solution)/shard_map/ppermute | solution.py:179
  7.9 0.1 collective-permute-start.4
  8.0 2.6 %norm.2 = (bf16[8,256,640]{2,1,0:T(8,128)(2,1)S(1)}, f32[8,128]{1,0:T(8,128)S(1)}) custom-call(bf16[256,5120]{1,0:T(8,128)(2,1)} %bitcast.6.hidden, f32[1,5120]{1,0:T(1,128)S(1)} %bitcast.24), custom_call_target="tpu_custom_call" | custom-call | flops 5242880 | bytes 5242880 | tf_op jit(solution)/shard_map/norm/pallas_call | solution.py:219
  10.6 2.6 %norm.3 = (bf16[8,256,640]{2,1,0:T(8,128)(2,1)S(1)}, f32[8,128]{1,0:T(8,128)S(1)}) custom-call(bf16[256,5120]{1,0:T(8,128)(2,1)} %bitcast.8.hidden, f32[1,5120]{1,0:T(1,128)S(1)} %bitcast.25), custom_call_target="tpu_custom_call" | custom-call | flops 5242880 | bytes 5242880 | tf_op jit(solution)/shard_map/norm/pallas_call | solution.py:219
  13.3 1.5 %copy-done = bf16[8,256,640]{2,1,0:T(8,128)(2,1)} copy-done((bf16[8,256,640]{2,1,0:T(8,128)(2,1)}, bf16[8,256,640]{2,1,0:T(8,128)(2,1)S(1)}, u32[]{:S(2)}) %copy-start) | copy-done | bytes 2621464
  14.8 0.9 %collective-permute-done.2.rest_1_ = bf16[640,256]{1,0:T(8,128)(2,1)} collective-permute-done((bf16[640,256]{1,0:T(8,128)(2,1)S(1)}, bf16[640,256]{1,0:T(8,128)(2,1)}, u32[]{:S(2)}, u32[]{:S(2)}) %collective-permute-start.2) | collective-permute-done | bytes 327712 | tf_op jit(solution)/shard_map/ppermute | solution.py:290
  15.7 1.7 %collective-permute-start.6 = (bf16[640,256]{1,0:T(8,128)(2,1)}, bf16[640,256]{1,0:T(8,128)(2,1)}, u32[]{:S(2)}, u32[]{:S(2)}) collective-permute-start(bf16[640,256]{1,0:T(8,128)(2,1)} %collective-permute-done.2.rest_1_), channel_id=1, source_target_pairs={{0,8},{8,24},{24,16},{16,0},{1,9},{9,25},{25,17},{17,1},{2,10},{10... | collective-permute-start | bytes 983048 | tf_op jit(solution)/shard_map/ppermute | solution.py:290
  17.3 0.6 collective-permute-start.8
  17.9 1.5 %collective-permute-start.5 = (s32[2,256]{1,0:T(2,128)S(1)}, s32[2,256]{1,0:T(2,128)S(1)}, u32[]{:S(2)}, u32[]{:S(2)}) collective-permute-start(s32[2,256]{1,0:T(2,128)S(1)} %pad_add_fusion.refs_3_), channel_id=1, source_target_pairs={{0,1},{1,0},{2,3},{3,2},{4,5},{5,4},{6,7},{7,6},{8,9},{9,8},{10,11... | collective-permute-start | bytes 6152 | tf_op jit(solution)/shard_map/ppermute | solution.py:202
  19.4 0.5 collective-permute-start.9
  20.0 6.4 %collective-permute-done.6.rest_1_ = bf16[640,256]{1,0:T(8,128)(2,1)} collective-permute-done((bf16[640,256]{1,0:T(8,128)(2,1)}, bf16[640,256]{1,0:T(8,128)(2,1)}, u32[]{:S(2)}, u32[]{:S(2)}) %collective-permute-start.6) | collective-permute-done | bytes 327712 | tf_op jit(solution)/shard_map/ppermute | solution.py:290
  26.3 1.5 %collective-permute-start.7 = (bf16[640,256]{1,0:T(8,128)(2,1)}, bf16[640,256]{1,0:T(8,128)(2,1)S(1)}, u32[]{:S(2)}, u32[]{:S(2)}) collective-permute-start(bf16[640,256]{1,0:T(8,128)(2,1)} %collective-permute-done.6.rest_1_), channel_id=1, source_target_pairs={{0,8},{8,24},{24,16},{16,0},{1,9},{9,25},{25,17},{17,1},{2,10},{10... | collective-permute-start | bytes 983048 | tf_op jit(solution)/shard_map/ppermute | solution.py:290
  27.8 0.7 collective-permute-start.11
  28.4 1.5 %collective-permute-start.12 = (bf16[640,256]{1,0:T(8,128)(2,1)}, bf16[640,256]{1,0:T(8,128)(2,1)S(1)}, u32[]{:S(2)}, u32[]{:S(2)}) collective-permute-start(bf16[640,256]{1,0:T(8,128)(2,1)} %collective-permute-done.6.rest_1_), channel_id=1, source_target_pairs={{0,1},{1,0},{2,3},{3,2},{4,5},{5,4},{6,7},{7,6},{8,9},{9,8},{10,11... | collective-permute-start | bytes 983048 | tf_op jit(solution)/shard_map/ppermute | solution.py:179
  29.9 0.3 collective-permute-done.8.rest_0_.rest_3_
  30.2 1.5 %collective-permute-start.13 = (bf16[640,256]{1,0:T(8,128)(2,1)}, bf16[640,256]{1,0:T(8,128)(2,1)S(1)}, u32[]{:S(2)}, u32[]{:S(2)}) collective-permute-start(bf16[640,256]{1,0:T(8,128)(2,1)} %collective-permute-done.8.rest_0_.rest_3_), channel_id=1, source_target_pairs={{0,1},{1,0},{2,3},{3,2},{4,5},{5,4},{6,7},{7,6},{8,9},{9,8},{10,11... | collective-permute-start | bytes 983048 | tf_op jit(solution)/shard_map/ppermute | solution.py:179
  31.7 0.1 pad_add_fusion.1.place
  31.8 1.7 %copy-done.1 = bf16[8,256,640]{2,1,0:T(8,128)(2,1)S(1)} copy-done((bf16[8,256,640]{2,1,0:T(8,128)(2,1)S(1)}, bf16[8,256,640]{2,1,0:T(8,128)(2,1)}, u32[]{:S(2)}) %copy-start.1) | copy-done | bytes 2621464
  33.5 3.3 %project.5.rest_3_ = f32[2,512,256]{2,1,0:T(8,128)S(1)} custom-call(s32[3]{0:T(128)S(1)} %pad_add_fusion.1.place, bf16[8,256,640]{2,1,0:T(8,128)(2,1)S(1)} %get-tuple-element.38.own, bf16[8,256,640]{2,1,0:T(8,128)(2,1)S(1)} %copy-done.1, bf16[2,640,256]{2,1,0:T(8,128)(2,1)S(1)} %constant_dynamic-update-slice_fusion.rest_0_, ...), custom_call_target="tpu_custom_call" | custom-call | flops 671088640 | bytes 2621440 | tf_op jit(solution)/shard_map/project/pallas_call | solution.py:254
  36.8 0.8 %mask.1 = (f32[256,512]{1,0:T(8,128)S(1)}, s32[2]{0:T(128)S(1)}) custom-call(bf16[2,640,256]{2,1,0:T(8,128)(2,1)} %collective-permute-done.1.refs_0_.rest_1_, f32[8,128]{1,0:T(8,128)S(1)} %get-tuple-element.33.refs_1_, f32[8,128]{1,0:T(8,128)S(1)} %get-tuple-element.34.refs_2_, s32[2,256]{1,0:T(2,128)S(1)} %pad_add_fusion.refs_3_, ...), custom_call_target="tpu_custom_call" | custom-call | flops 1000000000 | bytes 3333333 | tf_op jit(solution)/shard_map/mask/pallas_call | solution.py:295
  37.7 0.9 %copy-done.2 = bf16[8,256,640]{2,1,0:T(8,128)(2,1)S(1)} copy-done((bf16[8,256,640]{2,1,0:T(8,128)(2,1)S(1)}, bf16[8,256,640]{2,1,0:T(8,128)(2,1)}, u32[]{:S(2)}) %copy-start.2) | copy-done | bytes 2621464
  38.5 2.3 %project.6.rest_5_ = f32[2,512,256]{2,1,0:T(8,128)S(1)} custom-call(s32[3]{0:T(128)S(1)} %pad_add_fusion.1.place, bf16[8,256,640]{2,1,0:T(8,128)(2,1)S(1)} %get-tuple-element.38.own, bf16[8,256,640]{2,1,0:T(8,128)(2,1)S(1)} %copy-done.2, bf16[640,256]{1,0:T(8,128)(2,1)} %collective-permute-done.8.rest_0_.rest_3_, ...), custom_call_target="tpu_custom_call" | custom-call | flops 335544320 | bytes 1310720 | tf_op jit(solution)/shard_map/project/pallas_call | solution.py:254
  40.9 0.0 copy-start.8
  40.9 2.5 %collective-permute-start.10 = (bf16[640,256]{1,0:T(8,128)(2,1)S(1)}, bf16[640,256]{1,0:T(8,128)(2,1)S(1)}, u32[]{:S(2)}, u32[]{:S(2)}) collective-permute-start(bf16[640,256]{1,0:T(8,128)(2,1)S(1)} %collective-permute-done.7.rest_0_), channel_id=1, source_target_pairs={{0,4},{4,0},{1,5},{5,1},{2,6},{6,2},{3,7},{7,3},{8,12},{12,8},{9,1... | collective-permute-start | bytes 983048 | tf_op jit(solution)/shard_map/ppermute | solution.py:179
  43.4 0.5 collective-permute-start.15
  43.9 0.1 collective-permute-start.16
  44.0 0.7 collective-permute-done.13.rest_4_
  44.7 3.1 %project.7.rest_4_ = f32[2,512,256]{2,1,0:T(8,128)S(1)} custom-call(s32[3]{0:T(128)S(1)} %pad_add_fusion.1.place, bf16[8,256,640]{2,1,0:T(8,128)(2,1)S(1)} %get-tuple-element.38.own, bf16[8,256,640]{2,1,0:T(8,128)(2,1)S(1)} %copy-done.2, bf16[640,256]{1,0:T(8,128)(2,1)S(1)} %collective-permute-done.11.rest_0_.rest_2_, ...), custom_call_target="tpu_custom_call" | custom-call | flops 5368709120 | bytes 20971520 | tf_op jit(solution)/shard_map/project/pallas_call | solution.py:254
  47.8 4.2 %collective-permute-done.10.rest_0_ = bf16[640,256]{1,0:T(8,128)(2,1)S(1)} collective-permute-done((bf16[640,256]{1,0:T(8,128)(2,1)S(1)}, bf16[640,256]{1,0:T(8,128)(2,1)S(1)}, u32[]{:S(2)}, u32[]{:S(2)}) %collective-permute-start.10) | collective-permute-done | bytes 327712 | tf_op jit(solution)/shard_map/ppermute | solution.py:179
  52.0 0.5 collective-permute-start.14
  52.5 1.0 %fusion = (f32[512,64]{1,0:T(8,128)S(1)}, f32[512,64]{1,0:T(8,128)S(1)}, f32[512,64]{1,0:T(8,128)S(1)}) fusion(f32[64]{0:T(128)S(1)} %copy-done.8, f32[512]{0:T(512)S(1)} %add_convert_fusion), kind=kLoop, calls=%fused_computation.11 | loop fusion | flops 65536 | bytes 395520 | tf_op jit(solution)/shard_map/neg | solution.py:331
  53.5 0.1 pad_maximum_fusion.1.rest_3_
  53.7 0.1 pad_maximum_fusion.2.rest_4_
  53.8 0.0 copy-start.5
  53.8 2.7 %collective-permute-done.16.rest_3_ = bf16[640,256]{1,0:T(8,128)(2,1)S(1)} collective-permute-done((bf16[640,256]{1,0:T(8,128)(2,1)S(1)}, bf16[640,256]{1,0:T(8,128)(2,1)S(1)}, u32[]{:S(2)}, u32[]{:S(2)}) %collective-permute-start.16) | collective-permute-done | bytes 327712 | tf_op jit(solution)/shard_map/ppermute | solution.py:179
  56.6 2.5 %project.8.rest_2_ = f32[2,512,256]{2,1,0:T(8,128)S(1)} custom-call(s32[3]{0:T(128)S(1)} %pad_add_fusion.1.place, bf16[8,256,640]{2,1,0:T(8,128)(2,1)S(1)} %get-tuple-element.38.own, bf16[8,256,640]{2,1,0:T(8,128)(2,1)S(1)} %copy-done.2, bf16[640,256]{1,0:T(8,128)(2,1)S(1)} %collective-permute-done.7.rest_0_, ...), custom_call_target="tpu_custom_call" | custom-call | flops 671088640 | bytes 2621440 | tf_op jit(solution)/shard_map/project/pallas_call | solution.py:254
  59.1 0.0 copy-start.3
  59.1 2.1 %project.9 = (bf16[256,512]{1,0:T(8,128)(2,1)S(1)}, bf16[256,512]{1,0:T(8,128)(2,1)S(1)}) custom-call(s32[3]{0:T(128)S(1)} %pad_add_fusion.1.place, bf16[8,256,640]{2,1,0:T(8,128)(2,1)S(1)} %get-tuple-element.38.own, bf16[8,256,640]{2,1,0:T(8,128)(2,1)S(1)} %copy-done.2, bf16[640,256]{1,0:T(8,128)(2,1)S(1)} %collective-permute-done.10.rest_0_, ...), custom_call_target="tpu_custom_call" | custom-call | flops 335544320 | bytes 1310720 | tf_op jit(solution)/shard_map/project/pallas_call | solution.py:254
  61.2 0.7 collective-permute-start.19
  61.9 1.5 %collective-permute-start.18 = (bf16[256,512]{1,0:T(8,128)(2,1)S(1)}, bf16[256,512]{1,0:T(8,128)(2,1)S(1)}, u32[]{:S(2)}, u32[]{:S(2)}) collective-permute-start(bf16[256,512]{1,0:T(8,128)(2,1)S(1)} %get-tuple-element.47), channel_id=1, source_target_pairs={{0,3},{1,2},{2,1},{3,0},{4,7},{5,6},{6,5},{7,4},{8,11},{9,10},{10,... | collective-permute-start | bytes 786440 | tf_op jit(solution)/shard_map/ppermute | solution.py:202
  63.4 7.0 %collective-permute-done.19.rest_1_ = bf16[256,512]{1,0:T(8,128)(2,1)S(1)} collective-permute-done((bf16[256,512]{1,0:T(8,128)(2,1)S(1)}, bf16[256,512]{1,0:T(8,128)(2,1)S(1)}, u32[]{:S(2)}, u32[]{:S(2)}) %collective-permute-start.19) | collective-permute-done | bytes 262176 | tf_op jit(solution)/shard_map/ppermute | solution.py:202
  70.4 4.7 %attend.2.rest_2_ = bf16[256,4096]{1,0:T(8,128)(2,1)} custom-call(s32[1]{0:T(128)} %bitcast.place, s32[2]{0:T(128)S(1)} %get-tuple-element.36.needs, bf16[256,4096]{1,0:T(8,128)(2,1)S(1)} %bitcast.22, f32[256,512]{1,0:T(8,128)S(1)} %get-tuple-element.41.bias, bf16[256,512]{1,0:T(8,128)(2,1)S(1)} %get-tuple-element.48.rest_0_, ...), custom_call_target="tpu_custom_call" | custom-call | flops 1073741824 | bytes 2097152 | tf_op jit(solution)/shard_map/attend/pallas_call | solution.py:344
  75.1 4.9 %attend.3 = bf16[256,4096]{1,0:T(8,128)(2,1)} custom-call(s32[1]{0:T(128)} %bitcast.place, s32[2]{0:T(128)S(1)} %get-tuple-element.36.needs, bf16[256,4096]{1,0:T(8,128)(2,1)S(1)} %bitcast.23, f32[256,512]{1,0:T(8,128)S(1)} %get-tuple-element.41.bias, bf16[256,512]{1,0:T(8,128)(2,1)S(1)} %collective-permute-done.17.rest_0_, ...), custom_call_target="tpu_custom_call", output_to_operand_aliasing={{}: (6, {})} | custom-call | flops 1073741824 | bytes 2097152 | tf_op jit(solution)/shard_map/attend/pallas_call | solution.py:344
  (33 shorter events, 0.2 us)
Async XLA Ops:
  0.0 7.8 %copy-start.7 = (s32[1,256]{1,0:T(1,128)S(1)}, s32[1,256]{1,0:T(1,128)}, u32[]{:S(2)}) copy-start(s32[1,256]{1,0:T(1,128)} %param.15) | copy-start | bytes 3076
  0.0 7.8 %copy-start.6 = (s32[1,256]{1,0:T(1,128)S(1)}, s32[1,256]{1,0:T(1,128)}, u32[]{:S(2)}) copy-start(s32[1,256]{1,0:T(1,128)} %param.16) | copy-start | bytes 3076
  0.0 7.9 %copy-start.4 = (f32[5120]{0:T(1024)S(1)}, f32[5120]{0:T(1024)}, u32[]{:S(2)}) copy-start(f32[5120]{0:T(1024)} %param.11) | copy-start | bytes 61444
  1.3 1.8 %collective-permute-start = (bf16[2,320,256]{2,1,0:T(8,128)(2,1)S(1)}, bf16[2,320,256]{2,1,0:T(8,128)(2,1)S(1)}, u32[]{:S(2)}, u32[]{:S(2)}) collective-permute-start(bf16[2,320,256]{2,1,0:T(8,128)(2,1)S(1)} %pad_maximum_fusion), channel_id=1, source_target_pairs={{0,2},{2,0},{1,3},{3,1},{4,6},{6,4},{5,7},{7,5},{8,10},{10,8},{9,1... | collective-permute-start | bytes 983048 | tf_op jit(solution)/shard_map/ppermute | solution.py:179
  3.1 7.5 %collective-permute-start.3 = (bf16[1,256,5120]{2,1,0:T(8,128)(2,1)}, bf16[1,256,5120]{2,1,0:T(8,128)(2,1)}, u32[]{:S(2)}, u32[]{:S(2)}) collective-permute-start(bf16[1,256,5120]{2,1,0:T(8,128)(2,1)} %param.9), channel_id=1, source_target_pairs={{0,2},{2,0},{1,3},{3,1},{4,6},{6,4},{5,7},{7,5},{8,10},{10,8},{9,1... | collective-permute-start | bytes 7864328 | tf_op jit(solution)/shard_map/ppermute | solution.py:179
  3.6 12.1 %collective-permute-start.2 = (bf16[640,256]{1,0:T(8,128)(2,1)S(1)}, bf16[640,256]{1,0:T(8,128)(2,1)}, u32[]{:S(2)}, u32[]{:S(2)}) collective-permute-start(bf16[640,256]{1,0:T(8,128)(2,1)S(1)} %dynamic-slice_bitcast_fusion), channel_id=1, source_target_pairs={{0,8},{8,24},{24,16},{16,0},{1,9},{9,25},{25,17},{17,1},{2,10},{10... | collective-permute-start | bytes 983048 | tf_op jit(solution)/shard_map/ppermute | solution.py:290
  6.3 21.4 %collective-permute-start.1 = (bf16[2,640,256]{2,1,0:T(8,128)(2,1)S(1)}, bf16[2,640,256]{2,1,0:T(8,128)(2,1)}, u32[]{:S(2)}, u32[]{:S(2)}) collective-permute-start(bf16[2,640,256]{2,1,0:T(8,128)(2,1)S(1)} %constant_dynamic-update-slice_fusion.rest_0_), channel_id=1, source_target_pairs={{0,4},{4,0},{1,5},{5,1},{2,6},{6,2},{3,7},{7,3},{8,12},{12,8},{9,1... | collective-permute-start | bytes 1966088 | tf_op jit(solution)/shard_map/ppermute | solution.py:179
  7.9 6.9 %collective-permute-start.4 = (s32[2,256]{1,0:T(2,128)S(1)}, s32[2,256]{1,0:T(2,128)S(1)}, u32[]{:S(2)}, u32[]{:S(2)}) collective-permute-start(s32[2,256]{1,0:T(2,128)S(1)} %pad_add_fusion.refs_3_), channel_id=1, source_target_pairs={{0,2},{2,0},{1,3},{3,1},{4,6},{6,4},{5,7},{7,5},{8,10},{10,8},{9,1... | collective-permute-start | bytes 6152 | tf_op jit(solution)/shard_map/ppermute | solution.py:179
  13.3 1.5 %copy-start = (bf16[8,256,640]{2,1,0:T(8,128)(2,1)}, bf16[8,256,640]{2,1,0:T(8,128)(2,1)S(1)}, u32[]{:S(2)}) copy-start(bf16[8,256,640]{2,1,0:T(8,128)(2,1)S(1)} %get-tuple-element.39.other) | copy-start | bytes 7864324
  15.7 10.6 %collective-permute-start.6 = (bf16[640,256]{1,0:T(8,128)(2,1)}, bf16[640,256]{1,0:T(8,128)(2,1)}, u32[]{:S(2)}, u32[]{:S(2)}) collective-permute-start(bf16[640,256]{1,0:T(8,128)(2,1)} %collective-permute-done.2.rest_1_), channel_id=1, source_target_pairs={{0,8},{8,24},{24,16},{16,0},{1,9},{9,25},{25,17},{17,1},{2,10},{10... | collective-permute-start | bytes 983048 | tf_op jit(solution)/shard_map/ppermute | solution.py:290
  17.3 12.8 %collective-permute-start.8 = (bf16[640,256]{1,0:T(8,128)(2,1)}, bf16[640,256]{1,0:T(8,128)(2,1)}, u32[]{:S(2)}, u32[]{:S(2)}) collective-permute-start(bf16[640,256]{1,0:T(8,128)(2,1)} %collective-permute-done.2.rest_1_), channel_id=1, source_target_pairs={{0,4},{4,0},{1,5},{5,1},{2,6},{6,2},{3,7},{7,3},{8,12},{12,8},{9,1... | collective-permute-start | bytes 983048 | tf_op jit(solution)/shard_map/ppermute | solution.py:179
  17.9 10.5 %collective-permute-start.5 = (s32[2,256]{1,0:T(2,128)S(1)}, s32[2,256]{1,0:T(2,128)S(1)}, u32[]{:S(2)}, u32[]{:S(2)}) collective-permute-start(s32[2,256]{1,0:T(2,128)S(1)} %pad_add_fusion.refs_3_), channel_id=1, source_target_pairs={{0,1},{1,0},{2,3},{3,2},{4,5},{5,4},{6,7},{7,6},{8,9},{9,8},{10,11... | collective-permute-start | bytes 6152 | tf_op jit(solution)/shard_map/ppermute | solution.py:202
  19.4 18.2 %collective-permute-start.9 = (bf16[640,256]{1,0:T(8,128)(2,1)}, bf16[640,256]{1,0:T(8,128)(2,1)S(1)}, u32[]{:S(2)}, u32[]{:S(2)}) collective-permute-start(bf16[640,256]{1,0:T(8,128)(2,1)} %collective-permute-done.2.rest_1_), channel_id=1, source_target_pairs={{0,1},{1,0},{2,3},{3,2},{4,5},{5,4},{6,7},{7,6},{8,9},{9,8},{10,11... | collective-permute-start | bytes 983048 | tf_op jit(solution)/shard_map/ppermute | solution.py:179
  26.3 14.6 %collective-permute-start.7 = (bf16[640,256]{1,0:T(8,128)(2,1)}, bf16[640,256]{1,0:T(8,128)(2,1)S(1)}, u32[]{:S(2)}, u32[]{:S(2)}) collective-permute-start(bf16[640,256]{1,0:T(8,128)(2,1)} %collective-permute-done.6.rest_1_), channel_id=1, source_target_pairs={{0,8},{8,24},{24,16},{16,0},{1,9},{9,25},{25,17},{17,1},{2,10},{10... | collective-permute-start | bytes 983048 | tf_op jit(solution)/shard_map/ppermute | solution.py:290
  27.8 16.2 %collective-permute-start.11 = (bf16[640,256]{1,0:T(8,128)(2,1)}, bf16[640,256]{1,0:T(8,128)(2,1)S(1)}, u32[]{:S(2)}, u32[]{:S(2)}) collective-permute-start(bf16[640,256]{1,0:T(8,128)(2,1)} %collective-permute-done.6.rest_1_), channel_id=1, source_target_pairs={{0,4},{4,0},{1,5},{5,1},{2,6},{6,2},{3,7},{7,3},{8,12},{12,8},{9,1... | collective-permute-start | bytes 983048 | tf_op jit(solution)/shard_map/ppermute | solution.py:179
  28.4 15.5 %collective-permute-start.12 = (bf16[640,256]{1,0:T(8,128)(2,1)}, bf16[640,256]{1,0:T(8,128)(2,1)S(1)}, u32[]{:S(2)}, u32[]{:S(2)}) collective-permute-start(bf16[640,256]{1,0:T(8,128)(2,1)} %collective-permute-done.6.rest_1_), channel_id=1, source_target_pairs={{0,1},{1,0},{2,3},{3,2},{4,5},{5,4},{6,7},{7,6},{8,9},{9,8},{10,11... | collective-permute-start | bytes 983048 | tf_op jit(solution)/shard_map/ppermute | solution.py:179
  30.2 14.5 %collective-permute-start.13 = (bf16[640,256]{1,0:T(8,128)(2,1)}, bf16[640,256]{1,0:T(8,128)(2,1)S(1)}, u32[]{:S(2)}, u32[]{:S(2)}) collective-permute-start(bf16[640,256]{1,0:T(8,128)(2,1)} %collective-permute-done.8.rest_0_.rest_3_), channel_id=1, source_target_pairs={{0,1},{1,0},{2,3},{3,2},{4,5},{5,4},{6,7},{7,6},{8,9},{9,8},{10,11... | collective-permute-start | bytes 983048 | tf_op jit(solution)/shard_map/ppermute | solution.py:179
  31.7 1.7 %copy-start.1 = (bf16[8,256,640]{2,1,0:T(8,128)(2,1)S(1)}, bf16[8,256,640]{2,1,0:T(8,128)(2,1)}, u32[]{:S(2)}) copy-start(bf16[8,256,640]{2,1,0:T(8,128)(2,1)} %copy-done) | copy-start | bytes 7864324
  36.8 1.7 %copy-start.2 = (bf16[8,256,640]{2,1,0:T(8,128)(2,1)S(1)}, bf16[8,256,640]{2,1,0:T(8,128)(2,1)}, u32[]{:S(2)}) copy-start(bf16[8,256,640]{2,1,0:T(8,128)(2,1)} %copy-done) | copy-start | bytes 7864324
  40.9 11.6 %copy-start.8 = (f32[64]{0:T(128)S(1)}, f32[64]{0:T(128)}, u32[]{:S(2)}) copy-start(f32[64]{0:T(128)} %constant.45) | copy-start | bytes 772
  40.9 11.1 %collective-permute-start.10 = (bf16[640,256]{1,0:T(8,128)(2,1)S(1)}, bf16[640,256]{1,0:T(8,128)(2,1)S(1)}, u32[]{:S(2)}, u32[]{:S(2)}) collective-permute-start(bf16[640,256]{1,0:T(8,128)(2,1)S(1)} %collective-permute-done.7.rest_0_), channel_id=1, source_target_pairs={{0,4},{4,0},{1,5},{5,1},{2,6},{6,2},{3,7},{7,3},{8,12},{12,8},{9,1... | collective-permute-start | bytes 983048 | tf_op jit(solution)/shard_map/ppermute | solution.py:179
  43.4 10.5 %collective-permute-start.15 = (bf16[640,256]{1,0:T(8,128)(2,1)S(1)}, bf16[640,256]{1,0:T(8,128)(2,1)S(1)}, u32[]{:S(2)}, u32[]{:S(2)}) collective-permute-start(bf16[640,256]{1,0:T(8,128)(2,1)S(1)} %collective-permute-done.7.rest_0_), channel_id=1, source_target_pairs={{0,1},{1,0},{2,3},{3,2},{4,5},{5,4},{6,7},{7,6},{8,9},{9,8},{10,11... | collective-permute-start | bytes 983048 | tf_op jit(solution)/shard_map/ppermute | solution.py:179
  43.9 12.7 %collective-permute-start.16 = (bf16[640,256]{1,0:T(8,128)(2,1)S(1)}, bf16[640,256]{1,0:T(8,128)(2,1)S(1)}, u32[]{:S(2)}, u32[]{:S(2)}) collective-permute-start(bf16[640,256]{1,0:T(8,128)(2,1)S(1)} %collective-permute-done.12.rest_2_), channel_id=1, source_target_pairs={{0,4},{4,0},{1,5},{5,1},{2,6},{6,2},{3,7},{7,3},{8,12},{12,8},{9,1... | collective-permute-start | bytes 983048 | tf_op jit(solution)/shard_map/ppermute | solution.py:179
  52.0 7.1 %collective-permute-start.14 = (bf16[640,256]{1,0:T(8,128)(2,1)S(1)}, bf16[640,256]{1,0:T(8,128)(2,1)S(1)}, u32[]{:S(2)}, u32[]{:S(2)}) collective-permute-start(bf16[640,256]{1,0:T(8,128)(2,1)S(1)} %collective-permute-done.10.rest_0_), channel_id=1, source_target_pairs={{0,1},{1,0},{2,3},{3,2},{4,5},{5,4},{6,7},{7,6},{8,9},{9,8},{10,11... | collective-permute-start | bytes 983048 | tf_op jit(solution)/shard_map/ppermute | solution.py:179
  53.8 5.3 %copy-start.5 = (f32[128]{0:T(128)S(1)}, f32[128]{0:T(128)}, u32[]{:S(2)}) copy-start(f32[128]{0:T(128)} %param.12) | copy-start | bytes 1540
  59.1 11.3 %copy-start.3 = (bf16[1,256,4096]{2,1,0:T(8,128)(2,1)S(1)}, bf16[1,256,4096]{2,1,0:T(8,128)(2,1)}, u32[]{:S(2)}) copy-start(bf16[1,256,4096]{2,1,0:T(8,128)(2,1)} %param.10) | copy-start | bytes 6291460
  61.2 9.2 %collective-permute-start.19 = (bf16[256,512]{1,0:T(8,128)(2,1)S(1)}, bf16[256,512]{1,0:T(8,128)(2,1)S(1)}, u32[]{:S(2)}, u32[]{:S(2)}) collective-permute-start(bf16[256,512]{1,0:T(8,128)(2,1)S(1)} %get-tuple-element.48.rest_0_), channel_id=1, source_target_pairs={{0,1},{1,0},{2,3},{3,2},{4,5},{5,4},{6,7},{7,6},{8,9},{9,8},{10,11... | collective-permute-start | bytes 786440 | tf_op jit(solution)/shard_map/ppermute | solution.py:202
  61.9 13.2 %collective-permute-start.17 = (bf16[256,512]{1,0:T(8,128)(2,1)S(1)}, bf16[256,512]{1,0:T(8,128)(2,1)S(1)}, u32[]{:S(2)}, u32[]{:S(2)}) collective-permute-start(bf16[256,512]{1,0:T(8,128)(2,1)S(1)} %get-tuple-element.47), channel_id=1, source_target_pairs={{0,2},{1,3},{2,0},{3,1},{4,6},{5,7},{6,4},{7,5},{8,10},{9,11},{10,... | collective-permute-start | bytes 786440 | tf_op jit(solution)/shard_map/ppermute | solution.py:202
  61.9 13.2 %collective-permute-start.18 = (bf16[256,512]{1,0:T(8,128)(2,1)S(1)}, bf16[256,512]{1,0:T(8,128)(2,1)S(1)}, u32[]{:S(2)}, u32[]{:S(2)}) collective-permute-start(bf16[256,512]{1,0:T(8,128)(2,1)S(1)} %get-tuple-element.47), channel_id=1, source_target_pairs={{0,3},{1,2},{2,1},{3,0},{4,7},{5,6},{6,5},{7,4},{8,11},{9,10},{10,... | collective-permute-start | bytes 786440 | tf_op jit(solution)/shard_map/ppermute | solution.py:202

commit v4 on v3

--- a/solution.py
+++ b/solution.py
@@ -99,27 +99,36 @@
 
 
 def mask_kernel(*refs):
-    pieces, (bias, needs) = refs[3:-2], refs[-2:]
-    count = bias.shape[0]
+    pieces, (bias_own, bias_rest, needs) = refs[3:-3], refs[-3:]
+    count = bias_own.shape[0]
     size = count // TILES
     seg_q, pos_q = (
         jnp.transpose(jnp.broadcast_to(pieces[0][i : i + 1, :], (count, count))) for i in range(2)
     )
-    width = len(pieces) * size
-    for tile in range(TILES):
-        for i, piece in enumerate(pieces):
-            at = slice(tile * size, (tile + 1) * size)
-            allowed = (piece[:1, at] == seg_q[:, at]) & (piece[1:, at] <= pos_q[:, at])
-            there = tile * width + i * size
-            bias[:, there : there + size] = jnp.where(allowed, 0.0, MASKED)
+    for bias, some in ((bias_own, pieces[:1]), (bias_rest, pieces[1:])):
+        for tile in range(TILES):
+            for i, piece in enumerate(some):
+                at = slice(tile * size, (tile + 1) * size)
+                allowed = (piece[:1, at] == seg_q[:, at]) & (piece[1:, at] <= pos_q[:, at])
+                there = (tile * len(some) + i) * size
+                bias[:, there : there + size] = jnp.where(allowed, 0.0, MASKED)
     for tile in range(TILES - 1):
         rows = slice(tile * size, (tile + 1) * size)
-        needs[tile] = (jnp.max(bias[rows, (tile + 1) * width :]) == 0.0).astype(jnp.int32)
+        later = [
+            jnp.max(bias[rows, (tile + 1) * bias.shape[1] // TILES :])
+            for bias in (bias_own, bias_rest)
+        ]
+        needs[tile] = (jnp.maximum(later[0], later[1]) == 0.0).astype(jnp.int32)
     needs[TILES - 1] = 0
 
 
-def attend_kernel(pieces, count, place, needs, queries, bias, *rest):
-    sources, (out, keys, values) = rest[:pieces], rest[-3:]
+def attend_kernel(pieces, count, merge, place, needs, queries, bias, *rest):
+    sources, rest = rest[:pieces], rest[pieces:]
+    keys, values = rest[-2:]
+    if merge:
+        top_in, total_in, summed_in, out = *rest[:3], rest[-3]
+    else:
+        top_out, total_out, summed_out = rest[:3]
     step = pl.program_id(0)
     tile_rows = count // TILES
     length = pieces * tile_rows
@@ -142,19 +151,23 @@
         rows = slice(tile * tile_rows, (tile + 1) * tile_rows)
         k, v, b = keys[:high, :], values[:high, :], bias[rows, :high]
 
-        def score(step):
-            heads = range(step * WIDE, (step + 1) * WIDE)
+        def score(part):
+            heads = range(part * WIDE, (part + 1) * WIDE)
             q = jnp.concatenate([queries[rows, g * HD : (g + 1) * HD] for g in heads], axis=0)
             return lax.dot_general(
                 q, k, (((1,), (1,)), ((), ())), preferred_element_type=jnp.float32
             )
 
         ahead = score(0)
-        for step in range(G // WIDE):
+        for part in range(G // WIDE):
+            heads = slice(part * WIDE, (part + 1) * WIDE)
             scores = ahead.reshape(WIDE, tile_rows, high) + b[None]
-            if step + 1 < G // WIDE:
-                ahead = score(step + 1)
+            if part + 1 < G // WIDE:
+                ahead = score(part + 1)
             top = jnp.max(scores, axis=-1, keepdims=True)
+            if merge:
+                before = top_in[0, heads, rows, :]
+                top = jnp.maximum(top, before)
             weights = jnp.exp2((scores - top) * factor)
             total = jnp.sum(weights, axis=-1, keepdims=True)
             summed = jnp.dot(
@@ -162,10 +175,20 @@
                 v,
                 preferred_element_type=jnp.float32,
             ).reshape(WIDE, tile_rows, HD)
-            result = (summed * (1.0 / total)).astype(jnp.bfloat16)
+            if merge:
+                shrink = jnp.exp2((before - top) * factor)
+                over = 1.0 / (total + total_in[0, heads, rows, :] * shrink)
+            else:
+                top_out[0, heads, rows, :] = top
+                total_out[0, heads, rows, :] = total
             for i in range(WIDE):
-                g = step * WIDE + i
-                out[rows, g * HD : (g + 1) * HD] = result[i]
+                g = part * WIDE + i
+                at = slice(g * HD, (g + 1) * HD)
+                if merge:
+                    both = summed[i] + summed_in[rows, at] * shrink[i]
+                    out[rows, at] = (both * over[i]).astype(jnp.bfloat16)
+                else:
+                    summed_out[rows, at] = summed[i]
 
     for tile in range(TILES):
         for need, high in ((0, tile + 1), (1, TILES)):
@@ -292,14 +315,15 @@
             tied = tie((mine[k], token, token_other, ints, ints_other))
             mine[k], token, token_other, ints, ints_other = tied
             ints_all = [ints] + [along_ctx(ints, d) for d in range(1, m)]
-            bias, needs = pl.pallas_call(
+            bias_own, bias_rest, needs = pl.pallas_call(
                 mask_kernel,
                 out_shape=[
-                    jax.ShapeDtypeStruct((count, m * count), jnp.float32),
+                    jax.ShapeDtypeStruct((count, count), jnp.float32),
+                    jax.ShapeDtypeStruct((count, (m - 1) * count), jnp.float32),
                     jax.ShapeDtypeStruct((TILES,), jnp.int32),
                 ],
                 in_specs=[pl.BlockSpec(memory_space=pltpu.HBM)] * 3 + [whole] * m,
-                out_specs=[whole, pl.BlockSpec(memory_space=pltpu.SMEM)],
+                out_specs=[whole, whole, pl.BlockSpec(memory_space=pltpu.SMEM)],
                 compiler_params=params,
                 cost_estimate=pl.CostEstimate(
                     flops=MASK_COST, bytes_accessed=MASK_COST // 300, transcendentals=0
@@ -311,7 +335,7 @@
                 acc = project([(0, True), (0, False)])
             acc = project([(k - 2, True)], acc, also=beside[k - 2])
             if k == 3:
-                mine[k], acc, bias = tie((mine[k], acc, bias))
+                mine[k], acc, bias_own = tie((mine[k], acc, bias_own))
             else:
                 mine[k], acc = tie((mine[k], acc))
         across[k], beside[k] = swap(mine[k], "x"), swap(mine[k], "y")
@@ -333,38 +357,55 @@
     acc = project([(end, True)] + [(k, False) for k in range(2, end)], acc)
     kv_own, kv_other = project([(end, False)], acc, last=True)
 
-    result = None
-    for cross, kv in enumerate((kv_own, kv_other)):
-        sources = [kv if d == 0 and not cross else along_ctx(kv, d, cross) for d in range(m)]
-
-        def block(step, place, needs, cross=cross):
+    beyond = [[along_ctx(kv_own, d) for d in range(1, m)]]
+    local = along_ctx(kv_other, 0, True)
+    beyond.append([along_ctx(kv_other, d, True) for d in range(1, m)])
+    stat_shape = jax.ShapeDtypeStruct((2, G, count, 1), jnp.float32)
+    stat_spec = pl.BlockSpec((1, G, count, 1), lambda step, place, needs: (step, 0, 0, 0))
+    half_shape = jax.ShapeDtypeStruct((count, 2 * G * HD), jnp.float32)
+    half_spec = pl.BlockSpec((count, G * HD), lambda step, place, needs: (0, step))
+
+    def attend(cross, sources, state=None, result=None):
+        def block(step, place, needs):
             return (0, lax.rem(place[0] + cross, 2) * 2 + step)
 
-        earlier = [] if result is None else [result]
-        result = pl.pallas_call(
-            functools.partial(attend_kernel, m, count),
-            out_shape=jax.ShapeDtypeStruct((count, KVH * G * HD), bf16),
+        block_spec = pl.BlockSpec((count, G * HD), block)
+        merge = state is not None
+        extra = [] if result is None else [result]
+        stats = [stat_spec, stat_spec, half_spec]
+        outs = pl.pallas_call(
+            functools.partial(attend_kernel, len(sources), count, merge),
+            out_shape=[jax.ShapeDtypeStruct((count, KVH * G * HD), bf16)]
+            if merge
+            else [stat_shape, stat_shape, half_shape],
             grid_spec=pltpu.PrefetchScalarGridSpec(
                 num_scalar_prefetch=2,
                 grid=(2,),
-                in_specs=[pl.BlockSpec((count, G * HD), block)]
-                + [whole] * (1 + m)
-                + [pl.BlockSpec(memory_space=pl.ANY)] * len(earlier),
-                out_specs=pl.BlockSpec((count, G * HD), block),
-                scratch_shapes=[
-                    pltpu.VMEM((m * count, HD), bf16),
-                    pltpu.VMEM((m * count, HD), bf16),
-                ],
+                in_specs=[block_spec]
+                + [whole] * (1 + len(sources))
+                + (stats if merge else [])
+                + [pl.BlockSpec(memory_space=pl.ANY)] * len(extra),
+                out_specs=[block_spec] if merge else stats,
+                scratch_shapes=[pltpu.VMEM((len(sources) * count, HD), bf16)] * 2,
             ),
-            input_output_aliases={4 + m: 0} if earlier else {},
+            input_output_aliases={4 + len(sources) + 3: 0} if extra else {},
             compiler_params=params,
             cost_estimate=pl.CostEstimate(
-                flops=2 * count * m * count * KVH * G * HD,
+                flops=2 * count * m * count * G * HD * 2,
                 bytes_accessed=2 * count * KVH * G * HD,
-                transcendentals=count * m * count * KVH * G // 2,
+                transcendentals=count * m * count * G,
             ),
             name="attend",
-        )(core.astype(jnp.int32)[None], needs, queries[0], bias, *sources, *earlier)
+        )(
+            core.astype(jnp.int32)[None], needs, queries[0],
+            bias_rest if merge else bias_own, *sources, *(state or ()), *extra,
+        )
+        return outs[0] if merge else outs
+
+    first = attend(0, [kv_own])
+    second = attend(1, [local])
+    result = attend(0, beyond[0], first)
+    result = attend(1, beyond[1], second, result)
     return result[None]
 
 

time: 80.4 us -> 87.9 us (1.093)
  Pallas kernels: 29.1 us -> 42.7 us
  waiting for transfers between devices: 23.3 us -> 17.5 us
    pallas_call x3 -> x5, Pallas kernels: 10.4 us -> 24.1 us  [the longest x4 23.2 us: attend(): pl.pallas_call(functools.partial(attend_kernel, len(sources), count, merg...]
    ppermute x4, waiting for transfers between devices: 6.99 us -> 1.1 us  [along_ctx(): return lax.ppermute(array, ('core', 'ctx', 'x'), pairs)]
  transfers between devices with their start and end apart: 20 -> 20, of which waited for: 8 -> 8; matrix products, arithmetic and copies ran while one was open for 2% -> 2% of each run, Pallas kernels for 28% -> 37%
where the time goes in v4:
time: 87.9 us; the launch traced here: 87.5 us
  Pallas kernels  42.7 us (49%)
  starting transfers between devices  20.2 us (23%)
  waiting for transfers between devices  17.5 us (20%)
  local copies, waits for them, and re-layouts  5.46 us (6%)
  other arithmetic  1.42 us (2%)
    pallas_call x4, Pallas kernels, attend(): pl.pallas_call(functools.partial(attend_kernel, len(sources), count, merg...  23.2 us
    pallas_call x5, Pallas kernels, project(): pl.pallas_call(functools.partial(project_kernel, groups, also is None, ac...  13.3 us
    ppermute x13, starting transfers between devices, swap(): return lax.ppermute(array, axis, [(0, 1), (1, 0)])  10.9 us
    ppermute x13, waiting for transfers between devices, swap(): return lax.ppermute(array, axis, [(0, 1), (1, 0)])  9.07 us
    ppermute x3, waiting for transfers between devices, on_device(): mine[k] = lax.ppermute(mine[k - 1], 'z', ring)  7.29 us
    ppermute x3, starting transfers between devices, on_device(): mine[k] = lax.ppermute(mine[k - 1], 'z', ring)  5.87 us
    pallas_call x2, Pallas kernels, norm(): pl.pallas_call(functools.partial(norm_kernel, chunks), out_shape=[jax.Sha...  5.27 us
    unnamed x18, local copies, waits for them, and re-layouts  4.13 us
  transfers between devices with their start and end apart: 20, of which 8 were waited for; matrix products, arithmetic and copies ran while one was open for 2% of the time, Pallas kernels for 37%

profile of v4, /device:TPU:0, one launch (start us, length us, event | category | flops | bytes accessed | tf_op | source)
XLA Modules:
  0.0 87.5 jit_solution(10743451651385821870)
XLA Ops:
  0.0 1.2 %dynamic-slice_bitcast_fusion.1 = (bf16[1,320,256]{2,1,0:T(8,128)(2,1)S(1)}, bf16[1,320,256]{2,1,0:T(8,128)(2,1)S(1)}, bf16[1,320,256]{2,1,0:T(8,128)(2,1)S(1)}, bf16[1,320,256]{2,1,0:T(8,128)(2,1)S(1)}) fusion(bf16[320,512]{1,0:T(8,128)(2,1)} %param.14, s32[]{:T(128)S(6)} %select_n.31, s32[]{:T(128)S(6)} %select_n.29, bf16[320,512]{1,0:T(8,128)(2,1)} %param.13), kind=kLoop, calls=%fused_computation.7 | loop fusion | bytes 1310728 | tf_op jit(solution)/shard_map/stack | solution.py:229
  1.3 0.5 collective-permute-start
  1.9 1.2 %collective-permute-done = bf16[2,320,256]{2,1,0:T(8,128)(2,1)S(1)} collective-permute-done((bf16[2,320,256]{2,1,0:T(8,128)(2,1)S(1)}, bf16[2,320,256]{2,1,0:T(8,128)(2,1)S(1)}, u32[]{:S(2)}, u32[]{:S(2)}) %collective-permute-start) | collective-permute-done | bytes 327712 | tf_op jit(solution)/shard_map/ppermute | solution.py:202
  3.1 0.4 collective-permute-start.3
  3.6 2.8 %collective-permute-start.2 = (bf16[640,256]{1,0:T(8,128)(2,1)S(1)}, bf16[640,256]{1,0:T(8,128)(2,1)}, u32[]{:S(2)}, u32[]{:S(2)}) collective-permute-start(bf16[640,256]{1,0:T(8,128)(2,1)S(1)} %dynamic-slice_bitcast_fusion), channel_id=1, source_target_pairs={{0,8},{8,24},{24,16},{16,0},{1,9},{9,25},{25,17},{17,1},{2,10},{10... | collective-permute-start | bytes 983048 | tf_op jit(solution)/shard_map/ppermute | solution.py:313
  6.3 1.5 %collective-permute-start.1 = (bf16[2,640,256]{2,1,0:T(8,128)(2,1)S(1)}, bf16[2,640,256]{2,1,0:T(8,128)(2,1)}, u32[]{:S(2)}, u32[]{:S(2)}) collective-permute-start(bf16[2,640,256]{2,1,0:T(8,128)(2,1)S(1)} %constant_dynamic-update-slice_fusion.rest_0_), channel_id=1, source_target_pairs={{0,4},{4,0},{1,5},{5,1},{2,6},{6,2},{3,7},{7,3},{8,12},{12,8},{9,1... | collective-permute-start | bytes 1966088 | tf_op jit(solution)/shard_map/ppermute | solution.py:202
  7.9 0.1 collective-permute-start.4
  8.0 2.6 %norm.2 = (bf16[8,256,640]{2,1,0:T(8,128)(2,1)S(1)}, f32[8,128]{1,0:T(8,128)S(1)}) custom-call(bf16[256,5120]{1,0:T(8,128)(2,1)} %bitcast.6.hidden, f32[1,5120]{1,0:T(1,128)S(1)} %bitcast.26), custom_call_target="tpu_custom_call" | custom-call | flops 5242880 | bytes 5242880 | tf_op jit(solution)/shard_map/norm/pallas_call | solution.py:242
  10.6 2.6 %norm.3 = (bf16[8,256,640]{2,1,0:T(8,128)(2,1)S(1)}, f32[8,128]{1,0:T(8,128)S(1)}) custom-call(bf16[256,5120]{1,0:T(8,128)(2,1)} %bitcast.8.hidden, f32[1,5120]{1,0:T(1,128)S(1)} %bitcast.27), custom_call_target="tpu_custom_call" | custom-call | flops 5242880 | bytes 5242880 | tf_op jit(solution)/shard_map/norm/pallas_call | solution.py:242
  13.3 1.5 %copy-done = bf16[8,256,640]{2,1,0:T(8,128)(2,1)} copy-done((bf16[8,256,640]{2,1,0:T(8,128)(2,1)}, bf16[8,256,640]{2,1,0:T(8,128)(2,1)S(1)}, u32[]{:S(2)}) %copy-start) | copy-done | bytes 2621464
  14.7 0.9 %collective-permute-done.2.rest_1_ = bf16[640,256]{1,0:T(8,128)(2,1)} collective-permute-done((bf16[640,256]{1,0:T(8,128)(2,1)S(1)}, bf16[640,256]{1,0:T(8,128)(2,1)}, u32[]{:S(2)}, u32[]{:S(2)}) %collective-permute-start.2) | collective-permute-done | bytes 327712 | tf_op jit(solution)/shard_map/ppermute | solution.py:313
  15.7 1.7 %collective-permute-start.6 = (bf16[640,256]{1,0:T(8,128)(2,1)}, bf16[640,256]{1,0:T(8,128)(2,1)}, u32[]{:S(2)}, u32[]{:S(2)}) collective-permute-start(bf16[640,256]{1,0:T(8,128)(2,1)} %collective-permute-done.2.rest_1_), channel_id=1, source_target_pairs={{0,8},{8,24},{24,16},{16,0},{1,9},{9,25},{25,17},{17,1},{2,10},{10... | collective-permute-start | bytes 983048 | tf_op jit(solution)/shard_map/ppermute | solution.py:313
  17.3 0.6 collective-permute-start.8
  17.9 1.5 %collective-permute-start.5 = (s32[2,256]{1,0:T(2,128)S(1)}, s32[2,256]{1,0:T(2,128)S(1)}, u32[]{:S(2)}, u32[]{:S(2)}) collective-permute-start(s32[2,256]{1,0:T(2,128)S(1)} %pad_add_fusion.refs_3_), channel_id=1, source_target_pairs={{0,1},{1,0},{2,3},{3,2},{4,5},{5,4},{6,7},{7,6},{8,9},{9,8},{10,11... | collective-permute-start | bytes 6152 | tf_op jit(solution)/shard_map/ppermute | solution.py:225
  19.4 0.5 collective-permute-start.9
  20.0 6.4 %collective-permute-done.6.rest_1_ = bf16[640,256]{1,0:T(8,128)(2,1)} collective-permute-done((bf16[640,256]{1,0:T(8,128)(2,1)}, bf16[640,256]{1,0:T(8,128)(2,1)}, u32[]{:S(2)}, u32[]{:S(2)}) %collective-permute-start.6) | collective-permute-done | bytes 327712 | tf_op jit(solution)/shard_map/ppermute | solution.py:313
  26.3 1.4 %collective-permute-start.7 = (bf16[640,256]{1,0:T(8,128)(2,1)}, bf16[640,256]{1,0:T(8,128)(2,1)S(1)}, u32[]{:S(2)}, u32[]{:S(2)}) collective-permute-start(bf16[640,256]{1,0:T(8,128)(2,1)} %collective-permute-done.6.rest_1_), channel_id=1, source_target_pairs={{0,8},{8,24},{24,16},{16,0},{1,9},{9,25},{25,17},{17,1},{2,10},{10... | collective-permute-start | bytes 983048 | tf_op jit(solution)/shard_map/ppermute | solution.py:313
  27.8 0.7 collective-permute-start.11
  28.4 1.5 %collective-permute-start.12 = (bf16[640,256]{1,0:T(8,128)(2,1)}, bf16[640,256]{1,0:T(8,128)(2,1)S(1)}, u32[]{:S(2)}, u32[]{:S(2)}) collective-permute-start(bf16[640,256]{1,0:T(8,128)(2,1)} %collective-permute-done.6.rest_1_), channel_id=1, source_target_pairs={{0,1},{1,0},{2,3},{3,2},{4,5},{5,4},{6,7},{7,6},{8,9},{9,8},{10,11... | collective-permute-start | bytes 983048 | tf_op jit(solution)/shard_map/ppermute | solution.py:202
  29.9 0.3 collective-permute-done.8.rest_0_.rest_3_
  30.2 1.5 %collective-permute-start.13 = (bf16[640,256]{1,0:T(8,128)(2,1)}, bf16[640,256]{1,0:T(8,128)(2,1)S(1)}, u32[]{:S(2)}, u32[]{:S(2)}) collective-permute-start(bf16[640,256]{1,0:T(8,128)(2,1)} %collective-permute-done.8.rest_0_.rest_3_), channel_id=1, source_target_pairs={{0,1},{1,0},{2,3},{3,2},{4,5},{5,4},{6,7},{7,6},{8,9},{9,8},{10,11... | collective-permute-start | bytes 983048 | tf_op jit(solution)/shard_map/ppermute | solution.py:202
  31.7 0.1 pad_add_fusion.1.place
  31.8 1.7 %copy-done.1 = bf16[8,256,640]{2,1,0:T(8,128)(2,1)S(1)} copy-done((bf16[8,256,640]{2,1,0:T(8,128)(2,1)S(1)}, bf16[8,256,640]{2,1,0:T(8,128)(2,1)}, u32[]{:S(2)}) %copy-start.1) | copy-done | bytes 2621464
  33.5 3.3 %project.5.rest_3_ = f32[2,512,256]{2,1,0:T(8,128)S(1)} custom-call(s32[3]{0:T(128)S(1)} %pad_add_fusion.1.place, bf16[8,256,640]{2,1,0:T(8,128)(2,1)S(1)} %get-tuple-element.45.own, bf16[8,256,640]{2,1,0:T(8,128)(2,1)S(1)} %copy-done.1, bf16[2,640,256]{2,1,0:T(8,128)(2,1)S(1)} %constant_dynamic-update-slice_fusion.rest_0_, ...), custom_call_target="tpu_custom_call" | custom-call | flops 671088640 | bytes 2621440 | tf_op jit(solution)/shard_map/project/pallas_call | solution.py:277
  36.8 0.8 mask.1
  37.7 0.9 %copy-done.2 = bf16[8,256,640]{2,1,0:T(8,128)(2,1)S(1)} copy-done((bf16[8,256,640]{2,1,0:T(8,128)(2,1)S(1)}, bf16[8,256,640]{2,1,0:T(8,128)(2,1)}, u32[]{:S(2)}) %copy-start.2) | copy-done | bytes 2621464
  38.5 2.3 %project.6.rest_5_ = f32[2,512,256]{2,1,0:T(8,128)S(1)} custom-call(s32[3]{0:T(128)S(1)} %pad_add_fusion.1.place, bf16[8,256,640]{2,1,0:T(8,128)(2,1)S(1)} %get-tuple-element.45.own, bf16[8,256,640]{2,1,0:T(8,128)(2,1)S(1)} %copy-done.2, bf16[640,256]{1,0:T(8,128)(2,1)} %collective-permute-done.8.rest_0_.rest_3_, ...), custom_call_target="tpu_custom_call" | custom-call | flops 335544320 | bytes 1310720 | tf_op jit(solution)/shard_map/project/pallas_call | solution.py:277
  40.9 2.4 %collective-permute-start.10 = (bf16[640,256]{1,0:T(8,128)(2,1)S(1)}, bf16[640,256]{1,0:T(8,128)(2,1)S(1)}, u32[]{:S(2)}, u32[]{:S(2)}) collective-permute-start(bf16[640,256]{1,0:T(8,128)(2,1)S(1)} %collective-permute-done.7.rest_0_), channel_id=1, source_target_pairs={{0,4},{4,0},{1,5},{5,1},{2,6},{6,2},{3,7},{7,3},{8,12},{12,8},{9,1... | collective-permute-start | bytes 983048 | tf_op jit(solution)/shard_map/ppermute | solution.py:202
  43.4 0.5 collective-permute-start.15
  43.9 0.1 collective-permute-start.16
  44.0 0.7 collective-permute-done.13.rest_4_
  44.7 3.1 %project.7.rest_4_ = f32[2,512,256]{2,1,0:T(8,128)S(1)} custom-call(s32[3]{0:T(128)S(1)} %pad_add_fusion.1.place, bf16[8,256,640]{2,1,0:T(8,128)(2,1)S(1)} %get-tuple-element.45.own, bf16[8,256,640]{2,1,0:T(8,128)(2,1)S(1)} %copy-done.2, bf16[640,256]{1,0:T(8,128)(2,1)S(1)} %collective-permute-done.11.rest_0_.rest_2_, ...), custom_call_target="tpu_custom_call" | custom-call | flops 5368709120 | bytes 20971520 | tf_op jit(solution)/shard_map/project/pallas_call | solution.py:277
  47.8 4.2 %collective-permute-done.10.rest_0_ = bf16[640,256]{1,0:T(8,128)(2,1)S(1)} collective-permute-done((bf16[640,256]{1,0:T(8,128)(2,1)S(1)}, bf16[640,256]{1,0:T(8,128)(2,1)S(1)}, u32[]{:S(2)}, u32[]{:S(2)}) %collective-permute-start.10) | collective-permute-done | bytes 327712 | tf_op jit(solution)/shard_map/ppermute | solution.py:202
  52.0 0.5 collective-permute-start.14
  52.5 1.0 %fusion = (f32[512,64]{1,0:T(8,128)S(1)}, f32[512,64]{1,0:T(8,128)S(1)}, f32[512,64]{1,0:T(8,128)S(1)}) fusion(f32[64]{0:T(128)S(1)} %copy-done.8, f32[512]{0:T(512)S(1)} %add_convert_fusion), kind=kLoop, calls=%fused_computation.11 | loop fusion | flops 65536 | bytes 395520 | tf_op jit(solution)/shard_map/neg | solution.py:355
  53.5 0.1 pad_maximum_fusion.1.rest_3_
  53.7 0.1 pad_maximum_fusion.2.rest_4_
  53.8 2.7 %collective-permute-done.16.rest_3_ = bf16[640,256]{1,0:T(8,128)(2,1)S(1)} collective-permute-done((bf16[640,256]{1,0:T(8,128)(2,1)S(1)}, bf16[640,256]{1,0:T(8,128)(2,1)S(1)}, u32[]{:S(2)}, u32[]{:S(2)}) %collective-permute-start.16) | collective-permute-done | bytes 327712 | tf_op jit(solution)/shard_map/ppermute | solution.py:202
  56.6 2.5 %project.8.rest_2_ = f32[2,512,256]{2,1,0:T(8,128)S(1)} custom-call(s32[3]{0:T(128)S(1)} %pad_add_fusion.1.place, bf16[8,256,640]{2,1,0:T(8,128)(2,1)S(1)} %get-tuple-element.45.own, bf16[8,256,640]{2,1,0:T(8,128)(2,1)S(1)} %copy-done.2, bf16[640,256]{1,0:T(8,128)(2,1)S(1)} %collective-permute-done.7.rest_0_, ...), custom_call_target="tpu_custom_call" | custom-call | flops 671088640 | bytes 2621440 | tf_op jit(solution)/shard_map/project/pallas_call | solution.py:277
  59.1 2.1 %project.9 = (bf16[256,512]{1,0:T(8,128)(2,1)S(1)}, bf16[256,512]{1,0:T(8,128)(2,1)S(1)}) custom-call(s32[3]{0:T(128)S(1)} %pad_add_fusion.1.place, bf16[8,256,640]{2,1,0:T(8,128)(2,1)S(1)} %get-tuple-element.45.own, bf16[8,256,640]{2,1,0:T(8,128)(2,1)S(1)} %copy-done.2, bf16[640,256]{1,0:T(8,128)(2,1)S(1)} %collective-permute-done.10.rest_0_, ...), custom_call_target="tpu_custom_call" | custom-call | flops 335544320 | bytes 1310720 | tf_op jit(solution)/shard_map/project/pallas_call | solution.py:277
  61.2 0.1 collective-permute-start.18
  61.3 0.7 collective-permute-start.19
  62.0 1.2 %collective-permute-start.17 = (bf16[256,512]{1,0:T(8,128)(2,1)S(1)}, bf16[256,512]{1,0:T(8,128)(2,1)S(1)}, u32[]{:S(2)}, u32[]{:S(2)}) collective-permute-start(bf16[256,512]{1,0:T(8,128)(2,1)S(1)} %get-tuple-element.54), channel_id=1, source_target_pairs={{0,3},{1,2},{2,1},{3,0},{4,7},{5,6},{6,5},{7,4},{8,11},{9,10},{10,... | collective-permute-start | bytes 786440 | tf_op jit(solution)/shard_map/ppermute | solution.py:225
  63.1 3.1 %attend.5 = (f32[2,8,256,1]{3,2,1,0:T(8,128)S(1)}, f32[2,8,256,1]{3,2,1,0:T(8,128)S(1)}, f32[256,2048]{1,0:T(8,128)S(1)}) custom-call(s32[1]{0:T(128)} %bitcast.place, s32[2]{0:T(128)S(1)} %get-tuple-element.43.needs, bf16[256,4096]{1,0:T(8,128)(2,1)S(1)} %bitcast.22, f32[256,256]{1,0:T(8,128)S(1)} %get-tuple-element.55.bias, ...), custom_call_target="tpu_custom_call" | custom-call | flops 536870912 | bytes 2097152 | tf_op jit(solution)/shard_map/attend/pallas_call | solution.py:376
  66.3 3.1 %attend.4 = (f32[2,8,256,1]{3,2,1,0:T(8,128)S(1)}, f32[2,8,256,1]{3,2,1,0:T(8,128)S(1)}, f32[256,2048]{1,0:T(8,128)S(1)}) custom-call(s32[1]{0:T(128)} %bitcast.place, s32[2]{0:T(128)S(1)} %get-tuple-element.43.needs, bf16[256,4096]{1,0:T(8,128)(2,1)S(1)} %bitcast.23, f32[256,256]{1,0:T(8,128)S(1)} %get-tuple-element.55.bias, ...), custom_call_target="tpu_custom_call" | custom-call | flops 536870912 | bytes 2097152 | tf_op jit(solution)/shard_map/attend/pallas_call | solution.py:376
  69.4 1.1 %collective-permute-done.19.rest_0_ = bf16[256,512]{1,0:T(8,128)(2,1)S(1)} collective-permute-done((bf16[256,512]{1,0:T(8,128)(2,1)S(1)}, bf16[256,512]{1,0:T(8,128)(2,1)S(1)}, u32[]{:S(2)}, u32[]{:S(2)}) %collective-permute-start.19) | collective-permute-done | bytes 262176 | tf_op jit(solution)/shard_map/ppermute | solution.py:225
  70.5 8.6 %attend.6.rest_4_ = bf16[256,4096]{1,0:T(8,128)(2,1)} custom-call(s32[1]{0:T(128)} %bitcast.place, s32[2]{0:T(128)S(1)} %get-tuple-element.43.needs, bf16[256,4096]{1,0:T(8,128)(2,1)S(1)} %bitcast.24, f32[256,256]{1,0:T(8,128)S(1)} %get-tuple-element.44.bias, bf16[256,512]{1,0:T(8,128)(2,1)S(1)} %collective-permute-done.19.rest_0_, ...), custom_call_target="tpu_custom_call" | custom-call | flops 536870912 | bytes 2097152 | tf_op jit(solution)/shard_map/attend/pallas_call | solution.py:376
  79.1 8.4 %attend.7 = bf16[256,4096]{1,0:T(8,128)(2,1)} custom-call(s32[1]{0:T(128)} %bitcast.place, s32[2]{0:T(128)S(1)} %get-tuple-element.43.needs, bf16[256,4096]{1,0:T(8,128)(2,1)S(1)} %bitcast.25, f32[256,256]{1,0:T(8,128)S(1)} %get-tuple-element.44.bias, bf16[256,512]{1,0:T(8,128)(2,1)S(1)} %collective-permute-done.17.rest_0_, ...), custom_call_target="tpu_custom_call", output_to_operand_aliasing={{}: (8, {})} | custom-call | flops 536870912 | bytes 2097152 | tf_op jit(solution)/shard_map/attend/pallas_call | solution.py:376
  (35 shorter events, 0.2 us)
Async XLA Ops:
  0.0 7.8 %copy-start.6 = (s32[1,256]{1,0:T(1,128)S(1)}, s32[1,256]{1,0:T(1,128)}, u32[]{:S(2)}) copy-start(s32[1,256]{1,0:T(1,128)} %param.16) | copy-start | bytes 3076
  0.0 7.8 %copy-start.7 = (s32[1,256]{1,0:T(1,128)S(1)}, s32[1,256]{1,0:T(1,128)}, u32[]{:S(2)}) copy-start(s32[1,256]{1,0:T(1,128)} %param.15) | copy-start | bytes 3076
  0.0 7.9 %copy-start.4 = (f32[5120]{0:T(1024)S(1)}, f32[5120]{0:T(1024)}, u32[]{:S(2)}) copy-start(f32[5120]{0:T(1024)} %param.11) | copy-start | bytes 61444
  1.3 1.8 %collective-permute-start = (bf16[2,320,256]{2,1,0:T(8,128)(2,1)S(1)}, bf16[2,320,256]{2,1,0:T(8,128)(2,1)S(1)}, u32[]{:S(2)}, u32[]{:S(2)}) collective-permute-start(bf16[2,320,256]{2,1,0:T(8,128)(2,1)S(1)} %pad_maximum_fusion), channel_id=1, source_target_pairs={{0,2},{2,0},{1,3},{3,1},{4,6},{6,4},{5,7},{7,5},{8,10},{10,8},{9,1... | collective-permute-start | bytes 983048 | tf_op jit(solution)/shard_map/ppermute | solution.py:202
  3.1 7.5 %collective-permute-start.3 = (bf16[1,256,5120]{2,1,0:T(8,128)(2,1)}, bf16[1,256,5120]{2,1,0:T(8,128)(2,1)}, u32[]{:S(2)}, u32[]{:S(2)}) collective-permute-start(bf16[1,256,5120]{2,1,0:T(8,128)(2,1)} %param.9), channel_id=1, source_target_pairs={{0,2},{2,0},{1,3},{3,1},{4,6},{6,4},{5,7},{7,5},{8,10},{10,8},{9,1... | collective-permute-start | bytes 7864328 | tf_op jit(solution)/shard_map/ppermute | solution.py:202
  3.6 12.1 %collective-permute-start.2 = (bf16[640,256]{1,0:T(8,128)(2,1)S(1)}, bf16[640,256]{1,0:T(8,128)(2,1)}, u32[]{:S(2)}, u32[]{:S(2)}) collective-permute-start(bf16[640,256]{1,0:T(8,128)(2,1)S(1)} %dynamic-slice_bitcast_fusion), channel_id=1, source_target_pairs={{0,8},{8,24},{24,16},{16,0},{1,9},{9,25},{25,17},{17,1},{2,10},{10... | collective-permute-start | bytes 983048 | tf_op jit(solution)/shard_map/ppermute | solution.py:313
  6.3 21.4 %collective-permute-start.1 = (bf16[2,640,256]{2,1,0:T(8,128)(2,1)S(1)}, bf16[2,640,256]{2,1,0:T(8,128)(2,1)}, u32[]{:S(2)}, u32[]{:S(2)}) collective-permute-start(bf16[2,640,256]{2,1,0:T(8,128)(2,1)S(1)} %constant_dynamic-update-slice_fusion.rest_0_), channel_id=1, source_target_pairs={{0,4},{4,0},{1,5},{5,1},{2,6},{6,2},{3,7},{7,3},{8,12},{12,8},{9,1... | collective-permute-start | bytes 1966088 | tf_op jit(solution)/shard_map/ppermute | solution.py:202
  7.9 6.9 %collective-permute-start.4 = (s32[2,256]{1,0:T(2,128)S(1)}, s32[2,256]{1,0:T(2,128)S(1)}, u32[]{:S(2)}, u32[]{:S(2)}) collective-permute-start(s32[2,256]{1,0:T(2,128)S(1)} %pad_add_fusion.refs_3_), channel_id=1, source_target_pairs={{0,2},{2,0},{1,3},{3,1},{4,6},{6,4},{5,7},{7,5},{8,10},{10,8},{9,1... | collective-permute-start | bytes 6152 | tf_op jit(solution)/shard_map/ppermute | solution.py:202
  13.3 1.5 %copy-start = (bf16[8,256,640]{2,1,0:T(8,128)(2,1)}, bf16[8,256,640]{2,1,0:T(8,128)(2,1)S(1)}, u32[]{:S(2)}) copy-start(bf16[8,256,640]{2,1,0:T(8,128)(2,1)S(1)} %get-tuple-element.46.other) | copy-start | bytes 7864324
  15.7 10.6 %collective-permute-start.6 = (bf16[640,256]{1,0:T(8,128)(2,1)}, bf16[640,256]{1,0:T(8,128)(2,1)}, u32[]{:S(2)}, u32[]{:S(2)}) collective-permute-start(bf16[640,256]{1,0:T(8,128)(2,1)} %collective-permute-done.2.rest_1_), channel_id=1, source_target_pairs={{0,8},{8,24},{24,16},{16,0},{1,9},{9,25},{25,17},{17,1},{2,10},{10... | collective-permute-start | bytes 983048 | tf_op jit(solution)/shard_map/ppermute | solution.py:313
  17.3 12.8 %collective-permute-start.8 = (bf16[640,256]{1,0:T(8,128)(2,1)}, bf16[640,256]{1,0:T(8,128)(2,1)}, u32[]{:S(2)}, u32[]{:S(2)}) collective-permute-start(bf16[640,256]{1,0:T(8,128)(2,1)} %collective-permute-done.2.rest_1_), channel_id=1, source_target_pairs={{0,4},{4,0},{1,5},{5,1},{2,6},{6,2},{3,7},{7,3},{8,12},{12,8},{9,1... | collective-permute-start | bytes 983048 | tf_op jit(solution)/shard_map/ppermute | solution.py:202
  17.9 10.5 %collective-permute-start.5 = (s32[2,256]{1,0:T(2,128)S(1)}, s32[2,256]{1,0:T(2,128)S(1)}, u32[]{:S(2)}, u32[]{:S(2)}) collective-permute-start(s32[2,256]{1,0:T(2,128)S(1)} %pad_add_fusion.refs_3_), channel_id=1, source_target_pairs={{0,1},{1,0},{2,3},{3,2},{4,5},{5,4},{6,7},{7,6},{8,9},{9,8},{10,11... | collective-permute-start | bytes 6152 | tf_op jit(solution)/shard_map/ppermute | solution.py:225
  19.4 18.2 %collective-permute-start.9 = (bf16[640,256]{1,0:T(8,128)(2,1)}, bf16[640,256]{1,0:T(8,128)(2,1)S(1)}, u32[]{:S(2)}, u32[]{:S(2)}) collective-permute-start(bf16[640,256]{1,0:T(8,128)(2,1)} %collective-permute-done.2.rest_1_), channel_id=1, source_target_pairs={{0,1},{1,0},{2,3},{3,2},{4,5},{5,4},{6,7},{7,6},{8,9},{9,8},{10,11... | collective-permute-start | bytes 983048 | tf_op jit(solution)/shard_map/ppermute | solution.py:202
  26.3 14.6 %collective-permute-start.7 = (bf16[640,256]{1,0:T(8,128)(2,1)}, bf16[640,256]{1,0:T(8,128)(2,1)S(1)}, u32[]{:S(2)}, u32[]{:S(2)}) collective-permute-start(bf16[640,256]{1,0:T(8,128)(2,1)} %collective-permute-done.6.rest_1_), channel_id=1, source_target_pairs={{0,8},{8,24},{24,16},{16,0},{1,9},{9,25},{25,17},{17,1},{2,10},{10... | collective-permute-start | bytes 983048 | tf_op jit(solution)/shard_map/ppermute | solution.py:313
  27.8 16.2 %collective-permute-start.11 = (bf16[640,256]{1,0:T(8,128)(2,1)}, bf16[640,256]{1,0:T(8,128)(2,1)S(1)}, u32[]{:S(2)}, u32[]{:S(2)}) collective-permute-start(bf16[640,256]{1,0:T(8,128)(2,1)} %collective-permute-done.6.rest_1_), channel_id=1, source_target_pairs={{0,4},{4,0},{1,5},{5,1},{2,6},{6,2},{3,7},{7,3},{8,12},{12,8},{9,1... | collective-permute-start | bytes 983048 | tf_op jit(solution)/shard_map/ppermute | solution.py:202
  28.4 15.5 %collective-permute-start.12 = (bf16[640,256]{1,0:T(8,128)(2,1)}, bf16[640,256]{1,0:T(8,128)(2,1)S(1)}, u32[]{:S(2)}, u32[]{:S(2)}) collective-permute-start(bf16[640,256]{1,0:T(8,128)(2,1)} %collective-permute-done.6.rest_1_), channel_id=1, source_target_pairs={{0,1},{1,0},{2,3},{3,2},{4,5},{5,4},{6,7},{7,6},{8,9},{9,8},{10,11... | collective-permute-start | bytes 983048 | tf_op jit(solution)/shard_map/ppermute | solution.py:202
  30.2 14.5 %collective-permute-start.13 = (bf16[640,256]{1,0:T(8,128)(2,1)}, bf16[640,256]{1,0:T(8,128)(2,1)S(1)}, u32[]{:S(2)}, u32[]{:S(2)}) collective-permute-start(bf16[640,256]{1,0:T(8,128)(2,1)} %collective-permute-done.8.rest_0_.rest_3_), channel_id=1, source_target_pairs={{0,1},{1,0},{2,3},{3,2},{4,5},{5,4},{6,7},{7,6},{8,9},{9,8},{10,11... | collective-permute-start | bytes 983048 | tf_op jit(solution)/shard_map/ppermute | solution.py:202
  31.8 1.7 %copy-start.1 = (bf16[8,256,640]{2,1,0:T(8,128)(2,1)S(1)}, bf16[8,256,640]{2,1,0:T(8,128)(2,1)}, u32[]{:S(2)}) copy-start(bf16[8,256,640]{2,1,0:T(8,128)(2,1)} %copy-done) | copy-start | bytes 7864324
  36.8 1.7 %copy-start.2 = (bf16[8,256,640]{2,1,0:T(8,128)(2,1)S(1)}, bf16[8,256,640]{2,1,0:T(8,128)(2,1)}, u32[]{:S(2)}) copy-start(bf16[8,256,640]{2,1,0:T(8,128)(2,1)} %copy-done) | copy-start | bytes 7864324
  40.9 11.6 %copy-start.8 = (f32[64]{0:T(128)S(1)}, f32[64]{0:T(128)}, u32[]{:S(2)}) copy-start(f32[64]{0:T(128)} %constant.45) | copy-start | bytes 772
  40.9 11.1 %collective-permute-start.10 = (bf16[640,256]{1,0:T(8,128)(2,1)S(1)}, bf16[640,256]{1,0:T(8,128)(2,1)S(1)}, u32[]{:S(2)}, u32[]{:S(2)}) collective-permute-start(bf16[640,256]{1,0:T(8,128)(2,1)S(1)} %collective-permute-done.7.rest_0_), channel_id=1, source_target_pairs={{0,4},{4,0},{1,5},{5,1},{2,6},{6,2},{3,7},{7,3},{8,12},{12,8},{9,1... | collective-permute-start | bytes 983048 | tf_op jit(solution)/shard_map/ppermute | solution.py:202
  43.4 10.5 %collective-permute-start.15 = (bf16[640,256]{1,0:T(8,128)(2,1)S(1)}, bf16[640,256]{1,0:T(8,128)(2,1)S(1)}, u32[]{:S(2)}, u32[]{:S(2)}) collective-permute-start(bf16[640,256]{1,0:T(8,128)(2,1)S(1)} %collective-permute-done.7.rest_0_), channel_id=1, source_target_pairs={{0,1},{1,0},{2,3},{3,2},{4,5},{5,4},{6,7},{7,6},{8,9},{9,8},{10,11... | collective-permute-start | bytes 983048 | tf_op jit(solution)/shard_map/ppermute | solution.py:202
  43.9 12.7 %collective-permute-start.16 = (bf16[640,256]{1,0:T(8,128)(2,1)S(1)}, bf16[640,256]{1,0:T(8,128)(2,1)S(1)}, u32[]{:S(2)}, u32[]{:S(2)}) collective-permute-start(bf16[640,256]{1,0:T(8,128)(2,1)S(1)} %collective-permute-done.12.rest_2_), channel_id=1, source_target_pairs={{0,4},{4,0},{1,5},{5,1},{2,6},{6,2},{3,7},{7,3},{8,12},{12,8},{9,1... | collective-permute-start | bytes 983048 | tf_op jit(solution)/shard_map/ppermute | solution.py:202
  52.0 7.1 %collective-permute-start.14 = (bf16[640,256]{1,0:T(8,128)(2,1)S(1)}, bf16[640,256]{1,0:T(8,128)(2,1)S(1)}, u32[]{:S(2)}, u32[]{:S(2)}) collective-permute-start(bf16[640,256]{1,0:T(8,128)(2,1)S(1)} %collective-permute-done.10.rest_0_), channel_id=1, source_target_pairs={{0,1},{1,0},{2,3},{3,2},{4,5},{5,4},{6,7},{7,6},{8,9},{9,8},{10,11... | collective-permute-start | bytes 983048 | tf_op jit(solution)/shard_map/ppermute | solution.py:202
  53.8 5.3 %copy-start.5 = (f32[128]{0:T(128)S(1)}, f32[128]{0:T(128)}, u32[]{:S(2)}) copy-start(f32[128]{0:T(128)} %param.12) | copy-start | bytes 1540
  59.1 4.0 %copy-start.3 = (bf16[1,256,4096]{2,1,0:T(8,128)(2,1)S(1)}, bf16[1,256,4096]{2,1,0:T(8,128)(2,1)}, u32[]{:S(2)}) copy-start(bf16[1,256,4096]{2,1,0:T(8,128)(2,1)} %param.10) | copy-start | bytes 6291460
  61.2 5.0 %collective-permute-start.18 = (bf16[256,512]{1,0:T(8,128)(2,1)S(1)}, bf16[256,512]{1,0:T(8,128)(2,1)S(1)}, u32[]{:S(2)}, u32[]{:S(2)}) collective-permute-start(bf16[256,512]{1,0:T(8,128)(2,1)S(1)} %get-tuple-element.54), channel_id=1, source_target_pairs={{0,2},{1,3},{2,0},{3,1},{4,6},{5,7},{6,4},{7,5},{8,10},{9,11},{10,... | collective-permute-start | bytes 786440 | tf_op jit(solution)/shard_map/ppermute | solution.py:225
  61.3 9.2 %collective-permute-start.19 = (bf16[256,512]{1,0:T(8,128)(2,1)S(1)}, bf16[256,512]{1,0:T(8,128)(2,1)S(1)}, u32[]{:S(2)}, u32[]{:S(2)}) collective-permute-start(bf16[256,512]{1,0:T(8,128)(2,1)S(1)} %get-tuple-element.59.rest_0_), channel_id=1, source_target_pairs={{0,1},{1,0},{2,3},{3,2},{4,5},{5,4},{6,7},{7,6},{8,9},{9,8},{10,11... | collective-permute-start | bytes 786440 | tf_op jit(solution)/shard_map/ppermute | solution.py:225
  62.0 17.1 %collective-permute-start.17 = (bf16[256,512]{1,0:T(8,128)(2,1)S(1)}, bf16[256,512]{1,0:T(8,128)(2,1)S(1)}, u32[]{:S(2)}, u32[]{:S(2)}) collective-permute-start(bf16[256,512]{1,0:T(8,128)(2,1)S(1)} %get-tuple-element.54), channel_id=1, source_target_pairs={{0,3},{1,2},{2,1},{3,0},{4,7},{5,6},{6,5},{7,4},{8,11},{9,10},{10,... | collective-permute-start | bytes 786440 | tf_op jit(solution)/shard_map/ppermute | solution.py:225

commit v5 on v4

--- a/solution.py
+++ b/solution.py
@@ -164,17 +164,19 @@
             scores = ahead.reshape(WIDE, tile_rows, high) + b[None]
             if part + 1 < G // WIDE:
                 ahead = score(part + 1)
-            top = jnp.max(scores, axis=-1, keepdims=True)
+            wide = (WIDE, tile_rows, HD)
+            top = jnp.broadcast_to(jnp.max(scores, axis=-1, keepdims=True), wide)
             if merge:
                 before = top_in[0, heads, rows, :]
                 top = jnp.maximum(top, before)
-            weights = jnp.exp2((scores - top) * factor)
-            total = jnp.sum(weights, axis=-1, keepdims=True)
+            tops = jnp.concatenate([top] * (high // HD), axis=-1)
+            weights = jnp.exp2((scores - tops) * factor)
+            total = jnp.broadcast_to(jnp.sum(weights, axis=-1, keepdims=True), wide)
             summed = jnp.dot(
                 weights.astype(jnp.bfloat16).reshape(WIDE * tile_rows, high),
                 v,
                 preferred_element_type=jnp.float32,
-            ).reshape(WIDE, tile_rows, HD)
+            ).reshape(wide)
             if merge:
                 shrink = jnp.exp2((before - top) * factor)
                 over = 1.0 / (total + total_in[0, heads, rows, :] * shrink)
@@ -360,8 +362,8 @@
     beyond = [[along_ctx(kv_own, d) for d in range(1, m)]]
     local = along_ctx(kv_other, 0, True)
     beyond.append([along_ctx(kv_other, d, True) for d in range(1, m)])
-    stat_shape = jax.ShapeDtypeStruct((2, G, count, 1), jnp.float32)
-    stat_spec = pl.BlockSpec((1, G, count, 1), lambda step, place, needs: (step, 0, 0, 0))
+    stat_shape = jax.ShapeDtypeStruct((2, G, count, HD), jnp.float32)
+    stat_spec = pl.BlockSpec((1, G, count, HD), lambda step, place, needs: (step, 0, 0, 0))
     half_shape = jax.ShapeDtypeStruct((count, 2 * G * HD), jnp.float32)
     half_spec = pl.BlockSpec((count, G * HD), lambda step, place, needs: (0, step))
 

time: 87.9 us -> 80.3 us (0.914)
  Pallas kernels: 42.7 us -> 34.5 us
    pallas_call x4, Pallas kernels: 23.2 us -> 15 us  [attend(): pl.pallas_call(functools.partial(attend_kernel, len(sources), count, merg...]
  transfers between devices with their start and end apart: 20 -> 20, of which waited for: 8 -> 9; matrix products, arithmetic and copies ran while one was open for 2% -> 2% of each run, Pallas kernels for 37% -> 35%
where the time goes in v5:
time: 80.3 us; the launch traced here: 79.5 us
  Pallas kernels  34.5 us (43%)
  starting transfers between devices  20.2 us (25%)
  waiting for transfers between devices  17.6 us (22%)
  local copies, waits for them, and re-layouts  5.46 us (7%)
  other arithmetic  1.42 us (2%)
    pallas_call x4, Pallas kernels, attend(): pl.pallas_call(functools.partial(attend_kernel, len(sources), count, merg...  15 us
    pallas_call x5, Pallas kernels, project(): pl.pallas_call(functools.partial(project_kernel, groups, also is None, ac...  13.3 us
    ppermute x13, starting transfers between devices, swap(): return lax.ppermute(array, axis, [(0, 1), (1, 0)])  10.9 us
    ppermute x13, waiting for transfers between devices, swap(): return lax.ppermute(array, axis, [(0, 1), (1, 0)])  9.07 us
    ppermute x3, waiting for transfers between devices, on_device(): mine[k] = lax.ppermute(mine[k - 1], 'z', ring)  7.29 us
    ppermute x3, starting transfers between devices, on_device(): mine[k] = lax.ppermute(mine[k - 1], 'z', ring)  5.87 us
    pallas_call x2, Pallas kernels, norm(): pl.pallas_call(functools.partial(norm_kernel, chunks), out_shape=[jax.Sha...  5.27 us
    unnamed x18, local copies, waits for them, and re-layouts  4.13 us
  transfers between devices with their start and end apart: 20, of which 9 were waited for; matrix products, arithmetic and copies ran while one was open for 2% of the time, Pallas kernels for 35%

profile of v5, /device:TPU:0, one launch (start us, length us, event | category | flops | bytes accessed | tf_op | source)
XLA Modules:
  0.0 79.5 jit_solution(2818053906564973605)
XLA Ops:
  0.0 1.2 %dynamic-slice_bitcast_fusion.1 = (bf16[1,320,256]{2,1,0:T(8,128)(2,1)S(1)}, bf16[1,320,256]{2,1,0:T(8,128)(2,1)S(1)}, bf16[1,320,256]{2,1,0:T(8,128)(2,1)S(1)}, bf16[1,320,256]{2,1,0:T(8,128)(2,1)S(1)}) fusion(bf16[320,512]{1,0:T(8,128)(2,1)} %param.14, s32[]{:T(128)S(6)} %select_n.31, s32[]{:T(128)S(6)} %select_n.29, bf16[320,512]{1,0:T(8,128)(2,1)} %param.13), kind=kLoop, calls=%fused_computation.7 | loop fusion | bytes 1310728 | tf_op jit(solution)/shard_map/stack | solution.py:231
  1.3 0.5 collective-permute-start
  1.9 1.2 %collective-permute-done = bf16[2,320,256]{2,1,0:T(8,128)(2,1)S(1)} collective-permute-done((bf16[2,320,256]{2,1,0:T(8,128)(2,1)S(1)}, bf16[2,320,256]{2,1,0:T(8,128)(2,1)S(1)}, u32[]{:S(2)}, u32[]{:S(2)}) %collective-permute-start) | collective-permute-done | bytes 327712 | tf_op jit(solution)/shard_map/ppermute | solution.py:204
  3.1 0.4 collective-permute-start.3
  3.6 2.8 %collective-permute-start.2 = (bf16[640,256]{1,0:T(8,128)(2,1)S(1)}, bf16[640,256]{1,0:T(8,128)(2,1)}, u32[]{:S(2)}, u32[]{:S(2)}) collective-permute-start(bf16[640,256]{1,0:T(8,128)(2,1)S(1)} %dynamic-slice_bitcast_fusion), channel_id=1, source_target_pairs={{0,8},{8,24},{24,16},{16,0},{1,9},{9,25},{25,17},{17,1},{2,10},{10... | collective-permute-start | bytes 983048 | tf_op jit(solution)/shard_map/ppermute | solution.py:315
  6.3 1.5 %collective-permute-start.1 = (bf16[2,640,256]{2,1,0:T(8,128)(2,1)S(1)}, bf16[2,640,256]{2,1,0:T(8,128)(2,1)}, u32[]{:S(2)}, u32[]{:S(2)}) collective-permute-start(bf16[2,640,256]{2,1,0:T(8,128)(2,1)S(1)} %constant_dynamic-update-slice_fusion.rest_0_), channel_id=1, source_target_pairs={{0,4},{4,0},{1,5},{5,1},{2,6},{6,2},{3,7},{7,3},{8,12},{12,8},{9,1... | collective-permute-start | bytes 1966088 | tf_op jit(solution)/shard_map/ppermute | solution.py:204
  7.9 0.1 collective-permute-start.4
  8.0 2.6 %norm.2 = (bf16[8,256,640]{2,1,0:T(8,128)(2,1)S(1)}, f32[8,128]{1,0:T(8,128)S(1)}) custom-call(bf16[256,5120]{1,0:T(8,128)(2,1)} %bitcast.6.hidden, f32[1,5120]{1,0:T(1,128)S(1)} %bitcast.26), custom_call_target="tpu_custom_call" | custom-call | flops 5242880 | bytes 5242880 | tf_op jit(solution)/shard_map/norm/pallas_call | solution.py:244
  10.6 2.6 %norm.3 = (bf16[8,256,640]{2,1,0:T(8,128)(2,1)S(1)}, f32[8,128]{1,0:T(8,128)S(1)}) custom-call(bf16[256,5120]{1,0:T(8,128)(2,1)} %bitcast.8.hidden, f32[1,5120]{1,0:T(1,128)S(1)} %bitcast.27), custom_call_target="tpu_custom_call" | custom-call | flops 5242880 | bytes 5242880 | tf_op jit(solution)/shard_map/norm/pallas_call | solution.py:244
  13.3 1.5 %copy-done = bf16[8,256,640]{2,1,0:T(8,128)(2,1)} copy-done((bf16[8,256,640]{2,1,0:T(8,128)(2,1)}, bf16[8,256,640]{2,1,0:T(8,128)(2,1)S(1)}, u32[]{:S(2)}) %copy-start) | copy-done | bytes 2621464
  14.7 0.9 %collective-permute-done.2.rest_1_ = bf16[640,256]{1,0:T(8,128)(2,1)} collective-permute-done((bf16[640,256]{1,0:T(8,128)(2,1)S(1)}, bf16[640,256]{1,0:T(8,128)(2,1)}, u32[]{:S(2)}, u32[]{:S(2)}) %collective-permute-start.2) | collective-permute-done | bytes 327712 | tf_op jit(solution)/shard_map/ppermute | solution.py:315
  15.7 1.7 %collective-permute-start.6 = (bf16[640,256]{1,0:T(8,128)(2,1)}, bf16[640,256]{1,0:T(8,128)(2,1)}, u32[]{:S(2)}, u32[]{:S(2)}) collective-permute-start(bf16[640,256]{1,0:T(8,128)(2,1)} %collective-permute-done.2.rest_1_), channel_id=1, source_target_pairs={{0,8},{8,24},{24,16},{16,0},{1,9},{9,25},{25,17},{17,1},{2,10},{10... | collective-permute-start | bytes 983048 | tf_op jit(solution)/shard_map/ppermute | solution.py:315
  17.3 0.6 collective-permute-start.8
  17.9 1.5 %collective-permute-start.5 = (s32[2,256]{1,0:T(2,128)S(1)}, s32[2,256]{1,0:T(2,128)S(1)}, u32[]{:S(2)}, u32[]{:S(2)}) collective-permute-start(s32[2,256]{1,0:T(2,128)S(1)} %pad_add_fusion.refs_3_), channel_id=1, source_target_pairs={{0,1},{1,0},{2,3},{3,2},{4,5},{5,4},{6,7},{7,6},{8,9},{9,8},{10,11... | collective-permute-start | bytes 6152 | tf_op jit(solution)/shard_map/ppermute | solution.py:227
  19.4 0.5 collective-permute-start.9
  20.0 6.4 %collective-permute-done.6.rest_1_ = bf16[640,256]{1,0:T(8,128)(2,1)} collective-permute-done((bf16[640,256]{1,0:T(8,128)(2,1)}, bf16[640,256]{1,0:T(8,128)(2,1)}, u32[]{:S(2)}, u32[]{:S(2)}) %collective-permute-start.6) | collective-permute-done | bytes 327712 | tf_op jit(solution)/shard_map/ppermute | solution.py:315
  26.3 1.4 %collective-permute-start.7 = (bf16[640,256]{1,0:T(8,128)(2,1)}, bf16[640,256]{1,0:T(8,128)(2,1)S(1)}, u32[]{:S(2)}, u32[]{:S(2)}) collective-permute-start(bf16[640,256]{1,0:T(8,128)(2,1)} %collective-permute-done.6.rest_1_), channel_id=1, source_target_pairs={{0,8},{8,24},{24,16},{16,0},{1,9},{9,25},{25,17},{17,1},{2,10},{10... | collective-permute-start | bytes 983048 | tf_op jit(solution)/shard_map/ppermute | solution.py:315
  27.8 0.7 collective-permute-start.11
  28.4 1.5 %collective-permute-start.12 = (bf16[640,256]{1,0:T(8,128)(2,1)}, bf16[640,256]{1,0:T(8,128)(2,1)S(1)}, u32[]{:S(2)}, u32[]{:S(2)}) collective-permute-start(bf16[640,256]{1,0:T(8,128)(2,1)} %collective-permute-done.6.rest_1_), channel_id=1, source_target_pairs={{0,1},{1,0},{2,3},{3,2},{4,5},{5,4},{6,7},{7,6},{8,9},{9,8},{10,11... | collective-permute-start | bytes 983048 | tf_op jit(solution)/shard_map/ppermute | solution.py:204
  29.9 0.3 collective-permute-done.8.rest_0_.rest_3_
  30.2 1.5 %collective-permute-start.13 = (bf16[640,256]{1,0:T(8,128)(2,1)}, bf16[640,256]{1,0:T(8,128)(2,1)S(1)}, u32[]{:S(2)}, u32[]{:S(2)}) collective-permute-start(bf16[640,256]{1,0:T(8,128)(2,1)} %collective-permute-done.8.rest_0_.rest_3_), channel_id=1, source_target_pairs={{0,1},{1,0},{2,3},{3,2},{4,5},{5,4},{6,7},{7,6},{8,9},{9,8},{10,11... | collective-permute-start | bytes 983048 | tf_op jit(solution)/shard_map/ppermute | solution.py:204
  31.7 0.1 pad_add_fusion.1.place
  31.8 1.7 %copy-done.1 = bf16[8,256,640]{2,1,0:T(8,128)(2,1)S(1)} copy-done((bf16[8,256,640]{2,1,0:T(8,128)(2,1)S(1)}, bf16[8,256,640]{2,1,0:T(8,128)(2,1)}, u32[]{:S(2)}) %copy-start.1) | copy-done | bytes 2621464
  33.5 3.3 %project.5.rest_3_ = f32[2,512,256]{2,1,0:T(8,128)S(1)} custom-call(s32[3]{0:T(128)S(1)} %pad_add_fusion.1.place, bf16[8,256,640]{2,1,0:T(8,128)(2,1)S(1)} %get-tuple-element.45.own, bf16[8,256,640]{2,1,0:T(8,128)(2,1)S(1)} %copy-done.1, bf16[2,640,256]{2,1,0:T(8,128)(2,1)S(1)} %constant_dynamic-update-slice_fusion.rest_0_, ...), custom_call_target="tpu_custom_call" | custom-call | flops 671088640 | bytes 2621440 | tf_op jit(solution)/shard_map/project/pallas_call | solution.py:279
  36.8 0.8 %mask.1 = (f32[256,256]{1,0:T(8,128)S(1)}, f32[256,256]{1,0:T(8,128)S(1)}, s32[2]{0:T(128)S(1)}) custom-call(bf16[2,640,256]{2,1,0:T(8,128)(2,1)} %collective-permute-done.1.refs_0_.rest_1_, f32[8,128]{1,0:T(8,128)S(1)} %get-tuple-element.40.refs_1_, f32[8,128]{1,0:T(8,128)S(1)} %get-tuple-element.41.refs_2_, s32[2,256]{1,0:T(2,128)S(1)} %pad_add_fusion.refs_3_, ...), custom_call_target="tpu_custom_call" | custom-call | flops 1000000000 | bytes 3333333 | tf_op jit(solution)/shard_map/mask/pallas_call | solution.py:320
  37.7 0.9 %copy-done.2 = bf16[8,256,640]{2,1,0:T(8,128)(2,1)S(1)} copy-done((bf16[8,256,640]{2,1,0:T(8,128)(2,1)S(1)}, bf16[8,256,640]{2,1,0:T(8,128)(2,1)}, u32[]{:S(2)}) %copy-start.2) | copy-done | bytes 2621464
  38.5 2.3 %project.6.rest_5_ = f32[2,512,256]{2,1,0:T(8,128)S(1)} custom-call(s32[3]{0:T(128)S(1)} %pad_add_fusion.1.place, bf16[8,256,640]{2,1,0:T(8,128)(2,1)S(1)} %get-tuple-element.45.own, bf16[8,256,640]{2,1,0:T(8,128)(2,1)S(1)} %copy-done.2, bf16[640,256]{1,0:T(8,128)(2,1)} %collective-permute-done.8.rest_0_.rest_3_, ...), custom_call_target="tpu_custom_call" | custom-call | flops 335544320 | bytes 1310720 | tf_op jit(solution)/shard_map/project/pallas_call | solution.py:279
  40.9 2.4 %collective-permute-start.10 = (bf16[640,256]{1,0:T(8,128)(2,1)S(1)}, bf16[640,256]{1,0:T(8,128)(2,1)S(1)}, u32[]{:S(2)}, u32[]{:S(2)}) collective-permute-start(bf16[640,256]{1,0:T(8,128)(2,1)S(1)} %collective-permute-done.7.rest_0_), channel_id=1, source_target_pairs={{0,4},{4,0},{1,5},{5,1},{2,6},{6,2},{3,7},{7,3},{8,12},{12,8},{9,1... | collective-permute-start | bytes 983048 | tf_op jit(solution)/shard_map/ppermute | solution.py:204
  43.4 0.5 collective-permute-start.15
  43.9 0.1 collective-permute-start.16
  44.0 0.7 collective-permute-done.13.rest_4_
  44.7 3.1 %project.7.rest_4_ = f32[2,512,256]{2,1,0:T(8,128)S(1)} custom-call(s32[3]{0:T(128)S(1)} %pad_add_fusion.1.place, bf16[8,256,640]{2,1,0:T(8,128)(2,1)S(1)} %get-tuple-element.45.own, bf16[8,256,640]{2,1,0:T(8,128)(2,1)S(1)} %copy-done.2, bf16[640,256]{1,0:T(8,128)(2,1)S(1)} %collective-permute-done.11.rest_0_.rest_2_, ...), custom_call_target="tpu_custom_call" | custom-call | flops 5368709120 | bytes 20971520 | tf_op jit(solution)/shard_map/project/pallas_call | solution.py:279
  47.8 4.2 %collective-permute-done.10.rest_0_ = bf16[640,256]{1,0:T(8,128)(2,1)S(1)} collective-permute-done((bf16[640,256]{1,0:T(8,128)(2,1)S(1)}, bf16[640,256]{1,0:T(8,128)(2,1)S(1)}, u32[]{:S(2)}, u32[]{:S(2)}) %collective-permute-start.10) | collective-permute-done | bytes 327712 | tf_op jit(solution)/shard_map/ppermute | solution.py:204
  52.0 0.5 collective-permute-start.14
  52.5 1.0 %fusion = (f32[512,64]{1,0:T(8,128)S(1)}, f32[512,64]{1,0:T(8,128)S(1)}, f32[512,64]{1,0:T(8,128)S(1)}) fusion(f32[64]{0:T(128)S(1)} %copy-done.8, f32[512]{0:T(512)S(1)} %add_convert_fusion), kind=kLoop, calls=%fused_computation.11 | loop fusion | flops 65536 | bytes 395520 | tf_op jit(solution)/shard_map/neg | solution.py:357
  53.5 0.1 pad_maximum_fusion.1.rest_3_
  53.7 0.1 pad_maximum_fusion.2.rest_4_
  53.8 2.7 %collective-permute-done.16.rest_3_ = bf16[640,256]{1,0:T(8,128)(2,1)S(1)} collective-permute-done((bf16[640,256]{1,0:T(8,128)(2,1)S(1)}, bf16[640,256]{1,0:T(8,128)(2,1)S(1)}, u32[]{:S(2)}, u32[]{:S(2)}) %collective-permute-start.16) | collective-permute-done | bytes 327712 | tf_op jit(solution)/shard_map/ppermute | solution.py:204
  56.6 2.5 %project.8.rest_2_ = f32[2,512,256]{2,1,0:T(8,128)S(1)} custom-call(s32[3]{0:T(128)S(1)} %pad_add_fusion.1.place, bf16[8,256,640]{2,1,0:T(8,128)(2,1)S(1)} %get-tuple-element.45.own, bf16[8,256,640]{2,1,0:T(8,128)(2,1)S(1)} %copy-done.2, bf16[640,256]{1,0:T(8,128)(2,1)S(1)} %collective-permute-done.7.rest_0_, ...), custom_call_target="tpu_custom_call" | custom-call | flops 671088640 | bytes 2621440 | tf_op jit(solution)/shard_map/project/pallas_call | solution.py:279
  59.1 2.1 %project.9 = (bf16[256,512]{1,0:T(8,128)(2,1)S(1)}, bf16[256,512]{1,0:T(8,128)(2,1)S(1)}) custom-call(s32[3]{0:T(128)S(1)} %pad_add_fusion.1.place, bf16[8,256,640]{2,1,0:T(8,128)(2,1)S(1)} %get-tuple-element.45.own, bf16[8,256,640]{2,1,0:T(8,128)(2,1)S(1)} %copy-done.2, bf16[640,256]{1,0:T(8,128)(2,1)S(1)} %collective-permute-done.10.rest_0_, ...), custom_call_target="tpu_custom_call" | custom-call | flops 335544320 | bytes 1310720 | tf_op jit(solution)/shard_map/project/pallas_call | solution.py:279
  61.3 0.7 collective-permute-start.19
  62.0 1.2 %collective-permute-start.17 = (bf16[256,512]{1,0:T(8,128)(2,1)S(1)}, bf16[256,512]{1,0:T(8,128)(2,1)S(1)}, u32[]{:S(2)}, u32[]{:S(2)}) collective-permute-start(bf16[256,512]{1,0:T(8,128)(2,1)S(1)} %get-tuple-element.54), channel_id=1, source_target_pairs={{0,3},{1,2},{2,1},{3,0},{4,7},{5,6},{6,5},{7,4},{8,11},{9,10},{10,... | collective-permute-start | bytes 786440 | tf_op jit(solution)/shard_map/ppermute | solution.py:227
  63.1 3.1 %attend.5 = (f32[2,8,256,128]{3,2,1,0:T(8,128)S(1)}, f32[2,8,256,128]{3,2,1,0:T(8,128)S(1)}, f32[256,2048]{1,0:T(8,128)S(1)}) custom-call(s32[1]{0:T(128)} %bitcast.place, s32[2]{0:T(128)S(1)} %get-tuple-element.43.needs, bf16[256,4096]{1,0:T(8,128)(2,1)S(1)} %bitcast.22, f32[256,256]{1,0:T(8,128)S(1)} %get-tuple-element.55.bias, ...), custom_call_target="tpu_custom_call" | custom-call | flops 536870912 | bytes 2097152 | tf_op jit(solution)/shard_map/attend/pallas_call | solution.py:378
  66.3 3.1 %attend.4 = (f32[2,8,256,128]{3,2,1,0:T(8,128)S(1)}, f32[2,8,256,128]{3,2,1,0:T(8,128)S(1)}, f32[256,2048]{1,0:T(8,128)S(1)}) custom-call(s32[1]{0:T(128)} %bitcast.place, s32[2]{0:T(128)S(1)} %get-tuple-element.43.needs, bf16[256,4096]{1,0:T(8,128)(2,1)S(1)} %bitcast.23, f32[256,256]{1,0:T(8,128)S(1)} %get-tuple-element.55.bias, ...), custom_call_target="tpu_custom_call" | custom-call | flops 536870912 | bytes 2097152 | tf_op jit(solution)/shard_map/attend/pallas_call | solution.py:378
  69.4 1.1 %collective-permute-done.19.rest_0_ = bf16[256,512]{1,0:T(8,128)(2,1)S(1)} collective-permute-done((bf16[256,512]{1,0:T(8,128)(2,1)S(1)}, bf16[256,512]{1,0:T(8,128)(2,1)S(1)}, u32[]{:S(2)}, u32[]{:S(2)}) %collective-permute-start.19) | collective-permute-done | bytes 262176 | tf_op jit(solution)/shard_map/ppermute | solution.py:227
  70.5 4.5 %attend.6.rest_4_ = bf16[256,4096]{1,0:T(8,128)(2,1)} custom-call(s32[1]{0:T(128)} %bitcast.place, s32[2]{0:T(128)S(1)} %get-tuple-element.43.needs, bf16[256,4096]{1,0:T(8,128)(2,1)S(1)} %bitcast.24, f32[256,256]{1,0:T(8,128)S(1)} %get-tuple-element.44.bias, bf16[256,512]{1,0:T(8,128)(2,1)S(1)} %collective-permute-done.19.rest_0_, ...), custom_call_target="tpu_custom_call" | custom-call | flops 536870912 | bytes 2097152 | tf_op jit(solution)/shard_map/attend/pallas_call | solution.py:378
  75.0 0.2 collective-permute-done.17.rest_0_
  75.2 4.3 %attend.7 = bf16[256,4096]{1,0:T(8,128)(2,1)} custom-call(s32[1]{0:T(128)} %bitcast.place, s32[2]{0:T(128)S(1)} %get-tuple-element.43.needs, bf16[256,4096]{1,0:T(8,128)(2,1)S(1)} %bitcast.25, f32[256,256]{1,0:T(8,128)S(1)} %get-tuple-element.44.bias, bf16[256,512]{1,0:T(8,128)(2,1)S(1)} %collective-permute-done.17.rest_0_, ...), custom_call_target="tpu_custom_call", output_to_operand_aliasing={{}: (8, {})} | custom-call | flops 536870912 | bytes 2097152 | tf_op jit(solution)/shard_map/attend/pallas_call | solution.py:378
  (35 shorter events, 0.3 us)
Async XLA Ops:
  0.0 7.8 %copy-start.6 = (s32[1,256]{1,0:T(1,128)S(1)}, s32[1,256]{1,0:T(1,128)}, u32[]{:S(2)}) copy-start(s32[1,256]{1,0:T(1,128)} %param.16) | copy-start | bytes 3076
  0.0 7.8 %copy-start.7 = (s32[1,256]{1,0:T(1,128)S(1)}, s32[1,256]{1,0:T(1,128)}, u32[]{:S(2)}) copy-start(s32[1,256]{1,0:T(1,128)} %param.15) | copy-start | bytes 3076
  0.0 7.9 %copy-start.4 = (f32[5120]{0:T(1024)S(1)}, f32[5120]{0:T(1024)}, u32[]{:S(2)}) copy-start(f32[5120]{0:T(1024)} %param.11) | copy-start | bytes 61444
  1.3 1.8 %collective-permute-start = (bf16[2,320,256]{2,1,0:T(8,128)(2,1)S(1)}, bf16[2,320,256]{2,1,0:T(8,128)(2,1)S(1)}, u32[]{:S(2)}, u32[]{:S(2)}) collective-permute-start(bf16[2,320,256]{2,1,0:T(8,128)(2,1)S(1)} %pad_maximum_fusion), channel_id=1, source_target_pairs={{0,2},{2,0},{1,3},{3,1},{4,6},{6,4},{5,7},{7,5},{8,10},{10,8},{9,1... | collective-permute-start | bytes 983048 | tf_op jit(solution)/shard_map/ppermute | solution.py:204
  3.1 7.5 %collective-permute-start.3 = (bf16[1,256,5120]{2,1,0:T(8,128)(2,1)}, bf16[1,256,5120]{2,1,0:T(8,128)(2,1)}, u32[]{:S(2)}, u32[]{:S(2)}) collective-permute-start(bf16[1,256,5120]{2,1,0:T(8,128)(2,1)} %param.9), channel_id=1, source_target_pairs={{0,2},{2,0},{1,3},{3,1},{4,6},{6,4},{5,7},{7,5},{8,10},{10,8},{9,1... | collective-permute-start | bytes 7864328 | tf_op jit(solution)/shard_map/ppermute | solution.py:204
  3.6 12.1 %collective-permute-start.2 = (bf16[640,256]{1,0:T(8,128)(2,1)S(1)}, bf16[640,256]{1,0:T(8,128)(2,1)}, u32[]{:S(2)}, u32[]{:S(2)}) collective-permute-start(bf16[640,256]{1,0:T(8,128)(2,1)S(1)} %dynamic-slice_bitcast_fusion), channel_id=1, source_target_pairs={{0,8},{8,24},{24,16},{16,0},{1,9},{9,25},{25,17},{17,1},{2,10},{10... | collective-permute-start | bytes 983048 | tf_op jit(solution)/shard_map/ppermute | solution.py:315
  6.3 21.4 %collective-permute-start.1 = (bf16[2,640,256]{2,1,0:T(8,128)(2,1)S(1)}, bf16[2,640,256]{2,1,0:T(8,128)(2,1)}, u32[]{:S(2)}, u32[]{:S(2)}) collective-permute-start(bf16[2,640,256]{2,1,0:T(8,128)(2,1)S(1)} %constant_dynamic-update-slice_fusion.rest_0_), channel_id=1, source_target_pairs={{0,4},{4,0},{1,5},{5,1},{2,6},{6,2},{3,7},{7,3},{8,12},{12,8},{9,1... | collective-permute-start | bytes 1966088 | tf_op jit(solution)/shard_map/ppermute | solution.py:204
  7.9 6.9 %collective-permute-start.4 = (s32[2,256]{1,0:T(2,128)S(1)}, s32[2,256]{1,0:T(2,128)S(1)}, u32[]{:S(2)}, u32[]{:S(2)}) collective-permute-start(s32[2,256]{1,0:T(2,128)S(1)} %pad_add_fusion.refs_3_), channel_id=1, source_target_pairs={{0,2},{2,0},{1,3},{3,1},{4,6},{6,4},{5,7},{7,5},{8,10},{10,8},{9,1... | collective-permute-start | bytes 6152 | tf_op jit(solution)/shard_map/ppermute | solution.py:204
  13.3 1.5 %copy-start = (bf16[8,256,640]{2,1,0:T(8,128)(2,1)}, bf16[8,256,640]{2,1,0:T(8,128)(2,1)S(1)}, u32[]{:S(2)}) copy-start(bf16[8,256,640]{2,1,0:T(8,128)(2,1)S(1)} %get-tuple-element.46.other) | copy-start | bytes 7864324
  15.7 10.6 %collective-permute-start.6 = (bf16[640,256]{1,0:T(8,128)(2,1)}, bf16[640,256]{1,0:T(8,128)(2,1)}, u32[]{:S(2)}, u32[]{:S(2)}) collective-permute-start(bf16[640,256]{1,0:T(8,128)(2,1)} %collective-permute-done.2.rest_1_), channel_id=1, source_target_pairs={{0,8},{8,24},{24,16},{16,0},{1,9},{9,25},{25,17},{17,1},{2,10},{10... | collective-permute-start | bytes 983048 | tf_op jit(solution)/shard_map/ppermute | solution.py:315
  17.3 12.8 %collective-permute-start.8 = (bf16[640,256]{1,0:T(8,128)(2,1)}, bf16[640,256]{1,0:T(8,128)(2,1)}, u32[]{:S(2)}, u32[]{:S(2)}) collective-permute-start(bf16[640,256]{1,0:T(8,128)(2,1)} %collective-permute-done.2.rest_1_), channel_id=1, source_target_pairs={{0,4},{4,0},{1,5},{5,1},{2,6},{6,2},{3,7},{7,3},{8,12},{12,8},{9,1... | collective-permute-start | bytes 983048 | tf_op jit(solution)/shard_map/ppermute | solution.py:204
  17.9 10.5 %collective-permute-start.5 = (s32[2,256]{1,0:T(2,128)S(1)}, s32[2,256]{1,0:T(2,128)S(1)}, u32[]{:S(2)}, u32[]{:S(2)}) collective-permute-start(s32[2,256]{1,0:T(2,128)S(1)} %pad_add_fusion.refs_3_), channel_id=1, source_target_pairs={{0,1},{1,0},{2,3},{3,2},{4,5},{5,4},{6,7},{7,6},{8,9},{9,8},{10,11... | collective-permute-start | bytes 6152 | tf_op jit(solution)/shard_map/ppermute | solution.py:227
  19.4 18.2 %collective-permute-start.9 = (bf16[640,256]{1,0:T(8,128)(2,1)}, bf16[640,256]{1,0:T(8,128)(2,1)S(1)}, u32[]{:S(2)}, u32[]{:S(2)}) collective-permute-start(bf16[640,256]{1,0:T(8,128)(2,1)} %collective-permute-done.2.rest_1_), channel_id=1, source_target_pairs={{0,1},{1,0},{2,3},{3,2},{4,5},{5,4},{6,7},{7,6},{8,9},{9,8},{10,11... | collective-permute-start | bytes 983048 | tf_op jit(solution)/shard_map/ppermute | solution.py:204
  26.3 14.6 %collective-permute-start.7 = (bf16[640,256]{1,0:T(8,128)(2,1)}, bf16[640,256]{1,0:T(8,128)(2,1)S(1)}, u32[]{:S(2)}, u32[]{:S(2)}) collective-permute-start(bf16[640,256]{1,0:T(8,128)(2,1)} %collective-permute-done.6.rest_1_), channel_id=1, source_target_pairs={{0,8},{8,24},{24,16},{16,0},{1,9},{9,25},{25,17},{17,1},{2,10},{10... | collective-permute-start | bytes 983048 | tf_op jit(solution)/shard_map/ppermute | solution.py:315
  27.8 16.2 %collective-permute-start.11 = (bf16[640,256]{1,0:T(8,128)(2,1)}, bf16[640,256]{1,0:T(8,128)(2,1)S(1)}, u32[]{:S(2)}, u32[]{:S(2)}) collective-permute-start(bf16[640,256]{1,0:T(8,128)(2,1)} %collective-permute-done.6.rest_1_), channel_id=1, source_target_pairs={{0,4},{4,0},{1,5},{5,1},{2,6},{6,2},{3,7},{7,3},{8,12},{12,8},{9,1... | collective-permute-start | bytes 983048 | tf_op jit(solution)/shard_map/ppermute | solution.py:204
  28.4 15.5 %collective-permute-start.12 = (bf16[640,256]{1,0:T(8,128)(2,1)}, bf16[640,256]{1,0:T(8,128)(2,1)S(1)}, u32[]{:S(2)}, u32[]{:S(2)}) collective-permute-start(bf16[640,256]{1,0:T(8,128)(2,1)} %collective-permute-done.6.rest_1_), channel_id=1, source_target_pairs={{0,1},{1,0},{2,3},{3,2},{4,5},{5,4},{6,7},{7,6},{8,9},{9,8},{10,11... | collective-permute-start | bytes 983048 | tf_op jit(solution)/shard_map/ppermute | solution.py:204
  30.2 14.5 %collective-permute-start.13 = (bf16[640,256]{1,0:T(8,128)(2,1)}, bf16[640,256]{1,0:T(8,128)(2,1)S(1)}, u32[]{:S(2)}, u32[]{:S(2)}) collective-permute-start(bf16[640,256]{1,0:T(8,128)(2,1)} %collective-permute-done.8.rest_0_.rest_3_), channel_id=1, source_target_pairs={{0,1},{1,0},{2,3},{3,2},{4,5},{5,4},{6,7},{7,6},{8,9},{9,8},{10,11... | collective-permute-start | bytes 983048 | tf_op jit(solution)/shard_map/ppermute | solution.py:204
  31.8 1.7 %copy-start.1 = (bf16[8,256,640]{2,1,0:T(8,128)(2,1)S(1)}, bf16[8,256,640]{2,1,0:T(8,128)(2,1)}, u32[]{:S(2)}) copy-start(bf16[8,256,640]{2,1,0:T(8,128)(2,1)} %copy-done) | copy-start | bytes 7864324
  36.8 1.7 %copy-start.2 = (bf16[8,256,640]{2,1,0:T(8,128)(2,1)S(1)}, bf16[8,256,640]{2,1,0:T(8,128)(2,1)}, u32[]{:S(2)}) copy-start(bf16[8,256,640]{2,1,0:T(8,128)(2,1)} %copy-done) | copy-start | bytes 7864324
  40.9 11.6 %copy-start.8 = (f32[64]{0:T(128)S(1)}, f32[64]{0:T(128)}, u32[]{:S(2)}) copy-start(f32[64]{0:T(128)} %constant.45) | copy-start | bytes 772
  40.9 11.1 %collective-permute-start.10 = (bf16[640,256]{1,0:T(8,128)(2,1)S(1)}, bf16[640,256]{1,0:T(8,128)(2,1)S(1)}, u32[]{:S(2)}, u32[]{:S(2)}) collective-permute-start(bf16[640,256]{1,0:T(8,128)(2,1)S(1)} %collective-permute-done.7.rest_0_), channel_id=1, source_target_pairs={{0,4},{4,0},{1,5},{5,1},{2,6},{6,2},{3,7},{7,3},{8,12},{12,8},{9,1... | collective-permute-start | bytes 983048 | tf_op jit(solution)/shard_map/ppermute | solution.py:204
  43.4 10.5 %collective-permute-start.15 = (bf16[640,256]{1,0:T(8,128)(2,1)S(1)}, bf16[640,256]{1,0:T(8,128)(2,1)S(1)}, u32[]{:S(2)}, u32[]{:S(2)}) collective-permute-start(bf16[640,256]{1,0:T(8,128)(2,1)S(1)} %collective-permute-done.7.rest_0_), channel_id=1, source_target_pairs={{0,1},{1,0},{2,3},{3,2},{4,5},{5,4},{6,7},{7,6},{8,9},{9,8},{10,11... | collective-permute-start | bytes 983048 | tf_op jit(solution)/shard_map/ppermute | solution.py:204
  43.9 12.7 %collective-permute-start.16 = (bf16[640,256]{1,0:T(8,128)(2,1)S(1)}, bf16[640,256]{1,0:T(8,128)(2,1)S(1)}, u32[]{:S(2)}, u32[]{:S(2)}) collective-permute-start(bf16[640,256]{1,0:T(8,128)(2,1)S(1)} %collective-permute-done.12.rest_2_), channel_id=1, source_target_pairs={{0,4},{4,0},{1,5},{5,1},{2,6},{6,2},{3,7},{7,3},{8,12},{12,8},{9,1... | collective-permute-start | bytes 983048 | tf_op jit(solution)/shard_map/ppermute | solution.py:204
  52.0 7.1 %collective-permute-start.14 = (bf16[640,256]{1,0:T(8,128)(2,1)S(1)}, bf16[640,256]{1,0:T(8,128)(2,1)S(1)}, u32[]{:S(2)}, u32[]{:S(2)}) collective-permute-start(bf16[640,256]{1,0:T(8,128)(2,1)S(1)} %collective-permute-done.10.rest_0_), channel_id=1, source_target_pairs={{0,1},{1,0},{2,3},{3,2},{4,5},{5,4},{6,7},{7,6},{8,9},{9,8},{10,11... | collective-permute-start | bytes 983048 | tf_op jit(solution)/shard_map/ppermute | solution.py:204
  53.8 5.3 %copy-start.5 = (f32[128]{0:T(128)S(1)}, f32[128]{0:T(128)}, u32[]{:S(2)}) copy-start(f32[128]{0:T(128)} %param.12) | copy-start | bytes 1540
  59.1 4.0 %copy-start.3 = (bf16[1,256,4096]{2,1,0:T(8,128)(2,1)S(1)}, bf16[1,256,4096]{2,1,0:T(8,128)(2,1)}, u32[]{:S(2)}) copy-start(bf16[1,256,4096]{2,1,0:T(8,128)(2,1)} %param.10) | copy-start | bytes 6291460
  61.2 5.1 %collective-permute-start.18 = (bf16[256,512]{1,0:T(8,128)(2,1)S(1)}, bf16[256,512]{1,0:T(8,128)(2,1)S(1)}, u32[]{:S(2)}, u32[]{:S(2)}) collective-permute-start(bf16[256,512]{1,0:T(8,128)(2,1)S(1)} %get-tuple-element.54), channel_id=1, source_target_pairs={{0,2},{1,3},{2,0},{3,1},{4,6},{5,7},{6,4},{7,5},{8,10},{9,11},{10,... | collective-permute-start | bytes 786440 | tf_op jit(solution)/shard_map/ppermute | solution.py:227
  61.3 9.2 %collective-permute-start.19 = (bf16[256,512]{1,0:T(8,128)(2,1)S(1)}, bf16[256,512]{1,0:T(8,128)(2,1)S(1)}, u32[]{:S(2)}, u32[]{:S(2)}) collective-permute-start(bf16[256,512]{1,0:T(8,128)(2,1)S(1)} %get-tuple-element.59.rest_0_), channel_id=1, source_target_pairs={{0,1},{1,0},{2,3},{3,2},{4,5},{5,4},{6,7},{7,6},{8,9},{9,8},{10,11... | collective-permute-start | bytes 786440 | tf_op jit(solution)/shard_map/ppermute | solution.py:227
  62.0 13.2 %collective-permute-start.17 = (bf16[256,512]{1,0:T(8,128)(2,1)S(1)}, bf16[256,512]{1,0:T(8,128)(2,1)S(1)}, u32[]{:S(2)}, u32[]{:S(2)}) collective-permute-start(bf16[256,512]{1,0:T(8,128)(2,1)S(1)} %get-tuple-element.54), channel_id=1, source_target_pairs={{0,3},{1,2},{2,1},{3,0},{4,7},{5,6},{6,5},{7,4},{8,11},{9,10},{10,... | collective-permute-start | bytes 786440 | tf_op jit(solution)/shard_map/ppermute | solution.py:227

commit v6 on v3

--- a/solution.py
+++ b/solution.py
@@ -118,9 +118,10 @@
     needs[TILES - 1] = 0
 
 
-def attend_kernel(pieces, count, place, needs, queries, bias, *rest):
+def attend_kernel(pieces, count, cross, place, needs, queries, bias, *rest):
     sources, (out, keys, values) = rest[:pieces], rest[-3:]
     step = pl.program_id(0)
+    base = (lax.rem(place[0] + cross, 2) * 2 + step) * G * HD
     tile_rows = count // TILES
     length = pieces * tile_rows
 
@@ -142,9 +143,12 @@
         rows = slice(tile * tile_rows, (tile + 1) * tile_rows)
         k, v, b = keys[:high, :], values[:high, :], bias[rows, :high]
 
-        def score(step):
-            heads = range(step * WIDE, (step + 1) * WIDE)
-            q = jnp.concatenate([queries[rows, g * HD : (g + 1) * HD] for g in heads], axis=0)
+        def score(part):
+            columns = [
+                pl.ds(pl.multiple_of(base + g * HD, HD), HD)
+                for g in range(part * WIDE, (part + 1) * WIDE)
+            ]
+            q = jnp.concatenate([queries[rows, at] for at in columns], axis=0)
             return lax.dot_general(
                 q, k, (((1,), (1,)), ((), ())), preferred_element_type=jnp.float32
             )
@@ -342,13 +346,12 @@
 
         earlier = [] if result is None else [result]
         result = pl.pallas_call(
-            functools.partial(attend_kernel, m, count),
+            functools.partial(attend_kernel, m, count, cross),
             out_shape=jax.ShapeDtypeStruct((count, KVH * G * HD), bf16),
             grid_spec=pltpu.PrefetchScalarGridSpec(
                 num_scalar_prefetch=2,
                 grid=(2,),
-                in_specs=[pl.BlockSpec((count, G * HD), block)]
-                + [whole] * (1 + m)
+                in_specs=[whole] * (2 + m)
                 + [pl.BlockSpec(memory_space=pl.ANY)] * len(earlier),
                 out_specs=pl.BlockSpec((count, G * HD), block),
                 scratch_shapes=[

time: 80.4 us -> 80.2 us (level)
  no operation moved by 1% of the time
where the time goes in v6:
time: 80.2 us; the launch traced here: 79.8 us
  Pallas kernels  28.9 us (36%)
  waiting for transfers between devices  23.3 us (29%)
  starting transfers between devices  20.5 us (26%)
  local copies, waits for them, and re-layouts  5.46 us (7%)
  other arithmetic  1.42 us (2%)
    pallas_call x5, Pallas kernels, project(): pl.pallas_call(functools.partial(project_kernel, groups, also is None, ac...  13.3 us
    ppermute x13, starting transfers between devices, swap(): return lax.ppermute(array, axis, [(0, 1), (1, 0)])  10.9 us
    pallas_call x2, Pallas kernels, on_device(): pl.pallas_call(functools.partial(attend_kernel, m, count, cross), out_sha...  9.43 us
    ppermute x13, waiting for transfers between devices, swap(): return lax.ppermute(array, axis, [(0, 1), (1, 0)])  9.06 us
    ppermute x3, waiting for transfers between devices, on_device(): mine[k] = lax.ppermute(mine[k - 1], 'z', ring)  7.28 us
    ppermute x4, waiting for transfers between devices, along_ctx(): return lax.ppermute(array, ('core', 'ctx', 'x'), pairs)  6.99 us
    ppermute x3, starting transfers between devices, on_device(): mine[k] = lax.ppermute(mine[k - 1], 'z', ring)  5.89 us
    pallas_call x2, Pallas kernels, norm(): pl.pallas_call(functools.partial(norm_kernel, chunks), out_shape=[jax.Sha...  5.27 us
  transfers between devices with their start and end apart: 20, of which 8 were waited for; matrix products, arithmetic and copies ran while one was open for 2% of the time, Pallas kernels for 28%

profile of v6, /device:TPU:0, one launch (start us, length us, event | category | flops | bytes accessed | tf_op | source)
XLA Modules:
  0.0 79.8 jit_solution(9625760943097780362)
XLA Ops:
  0.0 1.2 %dynamic-slice_bitcast_fusion.1 = (bf16[1,320,256]{2,1,0:T(8,128)(2,1)S(1)}, bf16[1,320,256]{2,1,0:T(8,128)(2,1)S(1)}, bf16[1,320,256]{2,1,0:T(8,128)(2,1)S(1)}, bf16[1,320,256]{2,1,0:T(8,128)(2,1)S(1)}) fusion(bf16[320,512]{1,0:T(8,128)(2,1)} %param.14, s32[]{:T(128)S(6)} %select_n.31, s32[]{:T(128)S(6)} %select_n.29, bf16[320,512]{1,0:T(8,128)(2,1)} %param.13), kind=kLoop, calls=%fused_computation.7 | loop fusion | bytes 1310728 | tf_op jit(solution)/shard_map/stack | solution.py:210
  1.3 0.5 collective-permute-start
  1.9 1.2 %collective-permute-done = bf16[2,320,256]{2,1,0:T(8,128)(2,1)S(1)} collective-permute-done((bf16[2,320,256]{2,1,0:T(8,128)(2,1)S(1)}, bf16[2,320,256]{2,1,0:T(8,128)(2,1)S(1)}, u32[]{:S(2)}, u32[]{:S(2)}) %collective-permute-start) | collective-permute-done | bytes 327712 | tf_op jit(solution)/shard_map/ppermute | solution.py:183
  3.1 0.4 collective-permute-start.3
  3.6 2.8 %collective-permute-start.2 = (bf16[640,256]{1,0:T(8,128)(2,1)S(1)}, bf16[640,256]{1,0:T(8,128)(2,1)}, u32[]{:S(2)}, u32[]{:S(2)}) collective-permute-start(bf16[640,256]{1,0:T(8,128)(2,1)S(1)} %dynamic-slice_bitcast_fusion), channel_id=1, source_target_pairs={{0,8},{8,24},{24,16},{16,0},{1,9},{9,25},{25,17},{17,1},{2,10},{10... | collective-permute-start | bytes 983048 | tf_op jit(solution)/shard_map/ppermute | solution.py:294
  6.3 1.5 %collective-permute-start.1 = (bf16[2,640,256]{2,1,0:T(8,128)(2,1)S(1)}, bf16[2,640,256]{2,1,0:T(8,128)(2,1)}, u32[]{:S(2)}, u32[]{:S(2)}) collective-permute-start(bf16[2,640,256]{2,1,0:T(8,128)(2,1)S(1)} %constant_dynamic-update-slice_fusion.rest_0_), channel_id=1, source_target_pairs={{0,4},{4,0},{1,5},{5,1},{2,6},{6,2},{3,7},{7,3},{8,12},{12,8},{9,1... | collective-permute-start | bytes 1966088 | tf_op jit(solution)/shard_map/ppermute | solution.py:183
  7.9 0.1 collective-permute-start.4
  8.0 2.6 %norm.2 = (bf16[8,256,640]{2,1,0:T(8,128)(2,1)S(1)}, f32[8,128]{1,0:T(8,128)S(1)}) custom-call(bf16[256,5120]{1,0:T(8,128)(2,1)} %bitcast.6.hidden, f32[1,5120]{1,0:T(1,128)S(1)} %bitcast.24), custom_call_target="tpu_custom_call" | custom-call | flops 5242880 | bytes 5242880 | tf_op jit(solution)/shard_map/norm/pallas_call | solution.py:223
  10.6 2.6 %norm.3 = (bf16[8,256,640]{2,1,0:T(8,128)(2,1)S(1)}, f32[8,128]{1,0:T(8,128)S(1)}) custom-call(bf16[256,5120]{1,0:T(8,128)(2,1)} %bitcast.8.hidden, f32[1,5120]{1,0:T(1,128)S(1)} %bitcast.25), custom_call_target="tpu_custom_call" | custom-call | flops 5242880 | bytes 5242880 | tf_op jit(solution)/shard_map/norm/pallas_call | solution.py:223
  13.3 1.5 %copy-done = bf16[8,256,640]{2,1,0:T(8,128)(2,1)} copy-done((bf16[8,256,640]{2,1,0:T(8,128)(2,1)}, bf16[8,256,640]{2,1,0:T(8,128)(2,1)S(1)}, u32[]{:S(2)}) %copy-start) | copy-done | bytes 2621464
  14.8 0.9 %collective-permute-done.2.rest_1_ = bf16[640,256]{1,0:T(8,128)(2,1)} collective-permute-done((bf16[640,256]{1,0:T(8,128)(2,1)S(1)}, bf16[640,256]{1,0:T(8,128)(2,1)}, u32[]{:S(2)}, u32[]{:S(2)}) %collective-permute-start.2) | collective-permute-done | bytes 327712 | tf_op jit(solution)/shard_map/ppermute | solution.py:294
  15.7 1.7 %collective-permute-start.6 = (bf16[640,256]{1,0:T(8,128)(2,1)}, bf16[640,256]{1,0:T(8,128)(2,1)}, u32[]{:S(2)}, u32[]{:S(2)}) collective-permute-start(bf16[640,256]{1,0:T(8,128)(2,1)} %collective-permute-done.2.rest_1_), channel_id=1, source_target_pairs={{0,8},{8,24},{24,16},{16,0},{1,9},{9,25},{25,17},{17,1},{2,10},{10... | collective-permute-start | bytes 983048 | tf_op jit(solution)/shard_map/ppermute | solution.py:294
  17.3 0.6 collective-permute-start.8
  17.9 1.5 %collective-permute-start.5 = (s32[2,256]{1,0:T(2,128)S(1)}, s32[2,256]{1,0:T(2,128)S(1)}, u32[]{:S(2)}, u32[]{:S(2)}) collective-permute-start(s32[2,256]{1,0:T(2,128)S(1)} %pad_add_fusion.refs_3_), channel_id=1, source_target_pairs={{0,1},{1,0},{2,3},{3,2},{4,5},{5,4},{6,7},{7,6},{8,9},{9,8},{10,11... | collective-permute-start | bytes 6152 | tf_op jit(solution)/shard_map/ppermute | solution.py:206
  19.4 0.5 collective-permute-start.9
  20.0 6.4 %collective-permute-done.6.rest_1_ = bf16[640,256]{1,0:T(8,128)(2,1)} collective-permute-done((bf16[640,256]{1,0:T(8,128)(2,1)}, bf16[640,256]{1,0:T(8,128)(2,1)}, u32[]{:S(2)}, u32[]{:S(2)}) %collective-permute-start.6) | collective-permute-done | bytes 327712 | tf_op jit(solution)/shard_map/ppermute | solution.py:294
  26.3 1.5 %collective-permute-start.7 = (bf16[640,256]{1,0:T(8,128)(2,1)}, bf16[640,256]{1,0:T(8,128)(2,1)S(1)}, u32[]{:S(2)}, u32[]{:S(2)}) collective-permute-start(bf16[640,256]{1,0:T(8,128)(2,1)} %collective-permute-done.6.rest_1_), channel_id=1, source_target_pairs={{0,8},{8,24},{24,16},{16,0},{1,9},{9,25},{25,17},{17,1},{2,10},{10... | collective-permute-start | bytes 983048 | tf_op jit(solution)/shard_map/ppermute | solution.py:294
  27.8 0.7 collective-permute-start.11
  28.4 1.5 %collective-permute-start.12 = (bf16[640,256]{1,0:T(8,128)(2,1)}, bf16[640,256]{1,0:T(8,128)(2,1)S(1)}, u32[]{:S(2)}, u32[]{:S(2)}) collective-permute-start(bf16[640,256]{1,0:T(8,128)(2,1)} %collective-permute-done.6.rest_1_), channel_id=1, source_target_pairs={{0,1},{1,0},{2,3},{3,2},{4,5},{5,4},{6,7},{7,6},{8,9},{9,8},{10,11... | collective-permute-start | bytes 983048 | tf_op jit(solution)/shard_map/ppermute | solution.py:183
  29.9 0.3 collective-permute-done.8.rest_0_.rest_3_
  30.2 1.5 %collective-permute-start.13 = (bf16[640,256]{1,0:T(8,128)(2,1)}, bf16[640,256]{1,0:T(8,128)(2,1)S(1)}, u32[]{:S(2)}, u32[]{:S(2)}) collective-permute-start(bf16[640,256]{1,0:T(8,128)(2,1)} %collective-permute-done.8.rest_0_.rest_3_), channel_id=1, source_target_pairs={{0,1},{1,0},{2,3},{3,2},{4,5},{5,4},{6,7},{7,6},{8,9},{9,8},{10,11... | collective-permute-start | bytes 983048 | tf_op jit(solution)/shard_map/ppermute | solution.py:183
  31.7 0.1 pad_add_fusion.1.place
  31.8 1.7 %copy-done.1 = bf16[8,256,640]{2,1,0:T(8,128)(2,1)S(1)} copy-done((bf16[8,256,640]{2,1,0:T(8,128)(2,1)S(1)}, bf16[8,256,640]{2,1,0:T(8,128)(2,1)}, u32[]{:S(2)}) %copy-start.1) | copy-done | bytes 2621464
  33.5 3.3 %project.5.rest_3_ = f32[2,512,256]{2,1,0:T(8,128)S(1)} custom-call(s32[3]{0:T(128)S(1)} %pad_add_fusion.1.place, bf16[8,256,640]{2,1,0:T(8,128)(2,1)S(1)} %get-tuple-element.38.own, bf16[8,256,640]{2,1,0:T(8,128)(2,1)S(1)} %copy-done.1, bf16[2,640,256]{2,1,0:T(8,128)(2,1)S(1)} %constant_dynamic-update-slice_fusion.rest_0_, ...), custom_call_target="tpu_custom_call" | custom-call | flops 671088640 | bytes 2621440 | tf_op jit(solution)/shard_map/project/pallas_call | solution.py:258
  36.8 0.8 %mask.1 = (f32[256,512]{1,0:T(8,128)S(1)}, s32[2]{0:T(128)S(1)}) custom-call(bf16[2,640,256]{2,1,0:T(8,128)(2,1)} %collective-permute-done.1.refs_0_.rest_1_, f32[8,128]{1,0:T(8,128)S(1)} %get-tuple-element.33.refs_1_, f32[8,128]{1,0:T(8,128)S(1)} %get-tuple-element.34.refs_2_, s32[2,256]{1,0:T(2,128)S(1)} %pad_add_fusion.refs_3_, ...), custom_call_target="tpu_custom_call" | custom-call | flops 1000000000 | bytes 3333333 | tf_op jit(solution)/shard_map/mask/pallas_call | solution.py:299
  37.7 0.9 %copy-done.2 = bf16[8,256,640]{2,1,0:T(8,128)(2,1)S(1)} copy-done((bf16[8,256,640]{2,1,0:T(8,128)(2,1)S(1)}, bf16[8,256,640]{2,1,0:T(8,128)(2,1)}, u32[]{:S(2)}) %copy-start.2) | copy-done | bytes 2621464
  38.5 2.3 %project.6.rest_5_ = f32[2,512,256]{2,1,0:T(8,128)S(1)} custom-call(s32[3]{0:T(128)S(1)} %pad_add_fusion.1.place, bf16[8,256,640]{2,1,0:T(8,128)(2,1)S(1)} %get-tuple-element.38.own, bf16[8,256,640]{2,1,0:T(8,128)(2,1)S(1)} %copy-done.2, bf16[640,256]{1,0:T(8,128)(2,1)} %collective-permute-done.8.rest_0_.rest_3_, ...), custom_call_target="tpu_custom_call" | custom-call | flops 335544320 | bytes 1310720 | tf_op jit(solution)/shard_map/project/pallas_call | solution.py:258
  40.9 0.0 copy-start.8
  40.9 2.5 %collective-permute-start.10 = (bf16[640,256]{1,0:T(8,128)(2,1)S(1)}, bf16[640,256]{1,0:T(8,128)(2,1)S(1)}, u32[]{:S(2)}, u32[]{:S(2)}) collective-permute-start(bf16[640,256]{1,0:T(8,128)(2,1)S(1)} %collective-permute-done.7.rest_0_), channel_id=1, source_target_pairs={{0,4},{4,0},{1,5},{5,1},{2,6},{6,2},{3,7},{7,3},{8,12},{12,8},{9,1... | collective-permute-start | bytes 983048 | tf_op jit(solution)/shard_map/ppermute | solution.py:183
  43.4 0.5 collective-permute-start.15
  43.9 0.1 collective-permute-start.16
  44.0 0.7 collective-permute-done.13.rest_4_
  44.7 3.1 %project.7.rest_4_ = f32[2,512,256]{2,1,0:T(8,128)S(1)} custom-call(s32[3]{0:T(128)S(1)} %pad_add_fusion.1.place, bf16[8,256,640]{2,1,0:T(8,128)(2,1)S(1)} %get-tuple-element.38.own, bf16[8,256,640]{2,1,0:T(8,128)(2,1)S(1)} %copy-done.2, bf16[640,256]{1,0:T(8,128)(2,1)S(1)} %collective-permute-done.11.rest_0_.rest_2_, ...), custom_call_target="tpu_custom_call" | custom-call | flops 5368709120 | bytes 20971520 | tf_op jit(solution)/shard_map/project/pallas_call | solution.py:258
  47.8 4.2 %collective-permute-done.10.rest_0_ = bf16[640,256]{1,0:T(8,128)(2,1)S(1)} collective-permute-done((bf16[640,256]{1,0:T(8,128)(2,1)S(1)}, bf16[640,256]{1,0:T(8,128)(2,1)S(1)}, u32[]{:S(2)}, u32[]{:S(2)}) %collective-permute-start.10) | collective-permute-done | bytes 327712 | tf_op jit(solution)/shard_map/ppermute | solution.py:183
  52.0 0.5 collective-permute-start.14
  52.5 1.0 %fusion = (f32[512,64]{1,0:T(8,128)S(1)}, f32[512,64]{1,0:T(8,128)S(1)}, f32[512,64]{1,0:T(8,128)S(1)}) fusion(f32[64]{0:T(128)S(1)} %copy-done.8, f32[512]{0:T(512)S(1)} %add_convert_fusion), kind=kLoop, calls=%fused_computation.11 | loop fusion | flops 65536 | bytes 395520 | tf_op jit(solution)/shard_map/neg | solution.py:335
  53.5 0.1 pad_maximum_fusion.1.rest_3_
  53.7 0.1 pad_maximum_fusion.2.rest_4_
  53.8 0.0 copy-start.5
  53.8 2.7 %collective-permute-done.16.rest_3_ = bf16[640,256]{1,0:T(8,128)(2,1)S(1)} collective-permute-done((bf16[640,256]{1,0:T(8,128)(2,1)S(1)}, bf16[640,256]{1,0:T(8,128)(2,1)S(1)}, u32[]{:S(2)}, u32[]{:S(2)}) %collective-permute-start.16) | collective-permute-done | bytes 327712 | tf_op jit(solution)/shard_map/ppermute | solution.py:183
  56.6 2.5 %project.8.rest_2_ = f32[2,512,256]{2,1,0:T(8,128)S(1)} custom-call(s32[3]{0:T(128)S(1)} %pad_add_fusion.1.place, bf16[8,256,640]{2,1,0:T(8,128)(2,1)S(1)} %get-tuple-element.38.own, bf16[8,256,640]{2,1,0:T(8,128)(2,1)S(1)} %copy-done.2, bf16[640,256]{1,0:T(8,128)(2,1)S(1)} %collective-permute-done.7.rest_0_, ...), custom_call_target="tpu_custom_call" | custom-call | flops 671088640 | bytes 2621440 | tf_op jit(solution)/shard_map/project/pallas_call | solution.py:258
  59.1 0.0 copy-start.3
  59.1 2.1 %project.9 = (bf16[256,512]{1,0:T(8,128)(2,1)S(1)}, bf16[256,512]{1,0:T(8,128)(2,1)S(1)}) custom-call(s32[3]{0:T(128)S(1)} %pad_add_fusion.1.place, bf16[8,256,640]{2,1,0:T(8,128)(2,1)S(1)} %get-tuple-element.38.own, bf16[8,256,640]{2,1,0:T(8,128)(2,1)S(1)} %copy-done.2, bf16[640,256]{1,0:T(8,128)(2,1)S(1)} %collective-permute-done.10.rest_0_, ...), custom_call_target="tpu_custom_call" | custom-call | flops 335544320 | bytes 1310720 | tf_op jit(solution)/shard_map/project/pallas_call | solution.py:258
  61.2 0.7 collective-permute-start.19
  61.9 1.5 %collective-permute-start.18 = (bf16[256,512]{1,0:T(8,128)(2,1)S(1)}, bf16[256,512]{1,0:T(8,128)(2,1)S(1)}, u32[]{:S(2)}, u32[]{:S(2)}) collective-permute-start(bf16[256,512]{1,0:T(8,128)(2,1)S(1)} %get-tuple-element.47), channel_id=1, source_target_pairs={{0,3},{1,2},{2,1},{3,0},{4,7},{5,6},{6,5},{7,4},{8,11},{9,10},{10,... | collective-permute-start | bytes 786440 | tf_op jit(solution)/shard_map/ppermute | solution.py:206
  63.4 7.0 %collective-permute-done.19.rest_1_ = bf16[256,512]{1,0:T(8,128)(2,1)S(1)} collective-permute-done((bf16[256,512]{1,0:T(8,128)(2,1)S(1)}, bf16[256,512]{1,0:T(8,128)(2,1)S(1)}, u32[]{:S(2)}, u32[]{:S(2)}) %collective-permute-start.19) | collective-permute-done | bytes 262176 | tf_op jit(solution)/shard_map/ppermute | solution.py:206
  70.4 4.6 %attend.2.rest_2_ = bf16[256,4096]{1,0:T(8,128)(2,1)} custom-call(s32[1]{0:T(128)} %bitcast.place, s32[2]{0:T(128)S(1)} %get-tuple-element.36.needs, bf16[256,4096]{1,0:T(8,128)(2,1)S(1)} %bitcast.22, f32[256,512]{1,0:T(8,128)S(1)} %get-tuple-element.41.bias, bf16[256,512]{1,0:T(8,128)(2,1)S(1)} %get-tuple-element.48.rest_0_, ...), custom_call_target="tpu_custom_call" | custom-call | flops 1073741824 | bytes 2097152 | tf_op jit(solution)/shard_map/attend/pallas_call | solution.py:348
  75.0 4.8 %attend.3 = bf16[256,4096]{1,0:T(8,128)(2,1)} custom-call(s32[1]{0:T(128)} %bitcast.place, s32[2]{0:T(128)S(1)} %get-tuple-element.36.needs, bf16[256,4096]{1,0:T(8,128)(2,1)S(1)} %bitcast.23, f32[256,512]{1,0:T(8,128)S(1)} %get-tuple-element.41.bias, bf16[256,512]{1,0:T(8,128)(2,1)S(1)} %collective-permute-done.17.rest_0_, ...), custom_call_target="tpu_custom_call", output_to_operand_aliasing={{}: (6, {})} | custom-call | flops 1073741824 | bytes 2097152 | tf_op jit(solution)/shard_map/attend/pallas_call | solution.py:348
  (33 shorter events, 0.2 us)
Async XLA Ops:
  0.0 7.8 %copy-start.7 = (s32[1,256]{1,0:T(1,128)S(1)}, s32[1,256]{1,0:T(1,128)}, u32[]{:S(2)}) copy-start(s32[1,256]{1,0:T(1,128)} %param.15) | copy-start | bytes 3076
  0.0 7.8 %copy-start.6 = (s32[1,256]{1,0:T(1,128)S(1)}, s32[1,256]{1,0:T(1,128)}, u32[]{:S(2)}) copy-start(s32[1,256]{1,0:T(1,128)} %param.16) | copy-start | bytes 3076
  0.0 7.9 %copy-start.4 = (f32[5120]{0:T(1024)S(1)}, f32[5120]{0:T(1024)}, u32[]{:S(2)}) copy-start(f32[5120]{0:T(1024)} %param.11) | copy-start | bytes 61444
  1.3 1.8 %collective-permute-start = (bf16[2,320,256]{2,1,0:T(8,128)(2,1)S(1)}, bf16[2,320,256]{2,1,0:T(8,128)(2,1)S(1)}, u32[]{:S(2)}, u32[]{:S(2)}) collective-permute-start(bf16[2,320,256]{2,1,0:T(8,128)(2,1)S(1)} %pad_maximum_fusion), channel_id=1, source_target_pairs={{0,2},{2,0},{1,3},{3,1},{4,6},{6,4},{5,7},{7,5},{8,10},{10,8},{9,1... | collective-permute-start | bytes 983048 | tf_op jit(solution)/shard_map/ppermute | solution.py:183
  3.1 7.5 %collective-permute-start.3 = (bf16[1,256,5120]{2,1,0:T(8,128)(2,1)}, bf16[1,256,5120]{2,1,0:T(8,128)(2,1)}, u32[]{:S(2)}, u32[]{:S(2)}) collective-permute-start(bf16[1,256,5120]{2,1,0:T(8,128)(2,1)} %param.9), channel_id=1, source_target_pairs={{0,2},{2,0},{1,3},{3,1},{4,6},{6,4},{5,7},{7,5},{8,10},{10,8},{9,1... | collective-permute-start | bytes 7864328 | tf_op jit(solution)/shard_map/ppermute | solution.py:183
  3.6 12.1 %collective-permute-start.2 = (bf16[640,256]{1,0:T(8,128)(2,1)S(1)}, bf16[640,256]{1,0:T(8,128)(2,1)}, u32[]{:S(2)}, u32[]{:S(2)}) collective-permute-start(bf16[640,256]{1,0:T(8,128)(2,1)S(1)} %dynamic-slice_bitcast_fusion), channel_id=1, source_target_pairs={{0,8},{8,24},{24,16},{16,0},{1,9},{9,25},{25,17},{17,1},{2,10},{10... | collective-permute-start | bytes 983048 | tf_op jit(solution)/shard_map/ppermute | solution.py:294
  6.3 21.4 %collective-permute-start.1 = (bf16[2,640,256]{2,1,0:T(8,128)(2,1)S(1)}, bf16[2,640,256]{2,1,0:T(8,128)(2,1)}, u32[]{:S(2)}, u32[]{:S(2)}) collective-permute-start(bf16[2,640,256]{2,1,0:T(8,128)(2,1)S(1)} %constant_dynamic-update-slice_fusion.rest_0_), channel_id=1, source_target_pairs={{0,4},{4,0},{1,5},{5,1},{2,6},{6,2},{3,7},{7,3},{8,12},{12,8},{9,1... | collective-permute-start | bytes 1966088 | tf_op jit(solution)/shard_map/ppermute | solution.py:183
  7.9 6.9 %collective-permute-start.4 = (s32[2,256]{1,0:T(2,128)S(1)}, s32[2,256]{1,0:T(2,128)S(1)}, u32[]{:S(2)}, u32[]{:S(2)}) collective-permute-start(s32[2,256]{1,0:T(2,128)S(1)} %pad_add_fusion.refs_3_), channel_id=1, source_target_pairs={{0,2},{2,0},{1,3},{3,1},{4,6},{6,4},{5,7},{7,5},{8,10},{10,8},{9,1... | collective-permute-start | bytes 6152 | tf_op jit(solution)/shard_map/ppermute | solution.py:183
  13.3 1.5 %copy-start = (bf16[8,256,640]{2,1,0:T(8,128)(2,1)}, bf16[8,256,640]{2,1,0:T(8,128)(2,1)S(1)}, u32[]{:S(2)}) copy-start(bf16[8,256,640]{2,1,0:T(8,128)(2,1)S(1)} %get-tuple-element.39.other) | copy-start | bytes 7864324
  15.7 10.6 %collective-permute-start.6 = (bf16[640,256]{1,0:T(8,128)(2,1)}, bf16[640,256]{1,0:T(8,128)(2,1)}, u32[]{:S(2)}, u32[]{:S(2)}) collective-permute-start(bf16[640,256]{1,0:T(8,128)(2,1)} %collective-permute-done.2.rest_1_), channel_id=1, source_target_pairs={{0,8},{8,24},{24,16},{16,0},{1,9},{9,25},{25,17},{17,1},{2,10},{10... | collective-permute-start | bytes 983048 | tf_op jit(solution)/shard_map/ppermute | solution.py:294
  17.3 12.8 %collective-permute-start.8 = (bf16[640,256]{1,0:T(8,128)(2,1)}, bf16[640,256]{1,0:T(8,128)(2,1)}, u32[]{:S(2)}, u32[]{:S(2)}) collective-permute-start(bf16[640,256]{1,0:T(8,128)(2,1)} %collective-permute-done.2.rest_1_), channel_id=1, source_target_pairs={{0,4},{4,0},{1,5},{5,1},{2,6},{6,2},{3,7},{7,3},{8,12},{12,8},{9,1... | collective-permute-start | bytes 983048 | tf_op jit(solution)/shard_map/ppermute | solution.py:183
  17.9 10.5 %collective-permute-start.5 = (s32[2,256]{1,0:T(2,128)S(1)}, s32[2,256]{1,0:T(2,128)S(1)}, u32[]{:S(2)}, u32[]{:S(2)}) collective-permute-start(s32[2,256]{1,0:T(2,128)S(1)} %pad_add_fusion.refs_3_), channel_id=1, source_target_pairs={{0,1},{1,0},{2,3},{3,2},{4,5},{5,4},{6,7},{7,6},{8,9},{9,8},{10,11... | collective-permute-start | bytes 6152 | tf_op jit(solution)/shard_map/ppermute | solution.py:206
  19.4 18.2 %collective-permute-start.9 = (bf16[640,256]{1,0:T(8,128)(2,1)}, bf16[640,256]{1,0:T(8,128)(2,1)S(1)}, u32[]{:S(2)}, u32[]{:S(2)}) collective-permute-start(bf16[640,256]{1,0:T(8,128)(2,1)} %collective-permute-done.2.rest_1_), channel_id=1, source_target_pairs={{0,1},{1,0},{2,3},{3,2},{4,5},{5,4},{6,7},{7,6},{8,9},{9,8},{10,11... | collective-permute-start | bytes 983048 | tf_op jit(solution)/shard_map/ppermute | solution.py:183
  26.3 14.6 %collective-permute-start.7 = (bf16[640,256]{1,0:T(8,128)(2,1)}, bf16[640,256]{1,0:T(8,128)(2,1)S(1)}, u32[]{:S(2)}, u32[]{:S(2)}) collective-permute-start(bf16[640,256]{1,0:T(8,128)(2,1)} %collective-permute-done.6.rest_1_), channel_id=1, source_target_pairs={{0,8},{8,24},{24,16},{16,0},{1,9},{9,25},{25,17},{17,1},{2,10},{10... | collective-permute-start | bytes 983048 | tf_op jit(solution)/shard_map/ppermute | solution.py:294
  27.8 16.2 %collective-permute-start.11 = (bf16[640,256]{1,0:T(8,128)(2,1)}, bf16[640,256]{1,0:T(8,128)(2,1)S(1)}, u32[]{:S(2)}, u32[]{:S(2)}) collective-permute-start(bf16[640,256]{1,0:T(8,128)(2,1)} %collective-permute-done.6.rest_1_), channel_id=1, source_target_pairs={{0,4},{4,0},{1,5},{5,1},{2,6},{6,2},{3,7},{7,3},{8,12},{12,8},{9,1... | collective-permute-start | bytes 983048 | tf_op jit(solution)/shard_map/ppermute | solution.py:183
  28.4 15.5 %collective-permute-start.12 = (bf16[640,256]{1,0:T(8,128)(2,1)}, bf16[640,256]{1,0:T(8,128)(2,1)S(1)}, u32[]{:S(2)}, u32[]{:S(2)}) collective-permute-start(bf16[640,256]{1,0:T(8,128)(2,1)} %collective-permute-done.6.rest_1_), channel_id=1, source_target_pairs={{0,1},{1,0},{2,3},{3,2},{4,5},{5,4},{6,7},{7,6},{8,9},{9,8},{10,11... | collective-permute-start | bytes 983048 | tf_op jit(solution)/shard_map/ppermute | solution.py:183
  30.2 14.5 %collective-permute-start.13 = (bf16[640,256]{1,0:T(8,128)(2,1)}, bf16[640,256]{1,0:T(8,128)(2,1)S(1)}, u32[]{:S(2)}, u32[]{:S(2)}) collective-permute-start(bf16[640,256]{1,0:T(8,128)(2,1)} %collective-permute-done.8.rest_0_.rest_3_), channel_id=1, source_target_pairs={{0,1},{1,0},{2,3},{3,2},{4,5},{5,4},{6,7},{7,6},{8,9},{9,8},{10,11... | collective-permute-start | bytes 983048 | tf_op jit(solution)/shard_map/ppermute | solution.py:183
  31.7 1.7 %copy-start.1 = (bf16[8,256,640]{2,1,0:T(8,128)(2,1)S(1)}, bf16[8,256,640]{2,1,0:T(8,128)(2,1)}, u32[]{:S(2)}) copy-start(bf16[8,256,640]{2,1,0:T(8,128)(2,1)} %copy-done) | copy-start | bytes 7864324
  36.8 1.7 %copy-start.2 = (bf16[8,256,640]{2,1,0:T(8,128)(2,1)S(1)}, bf16[8,256,640]{2,1,0:T(8,128)(2,1)}, u32[]{:S(2)}) copy-start(bf16[8,256,640]{2,1,0:T(8,128)(2,1)} %copy-done) | copy-start | bytes 7864324
  40.9 11.6 %copy-start.8 = (f32[64]{0:T(128)S(1)}, f32[64]{0:T(128)}, u32[]{:S(2)}) copy-start(f32[64]{0:T(128)} %constant.45) | copy-start | bytes 772
  40.9 11.1 %collective-permute-start.10 = (bf16[640,256]{1,0:T(8,128)(2,1)S(1)}, bf16[640,256]{1,0:T(8,128)(2,1)S(1)}, u32[]{:S(2)}, u32[]{:S(2)}) collective-permute-start(bf16[640,256]{1,0:T(8,128)(2,1)S(1)} %collective-permute-done.7.rest_0_), channel_id=1, source_target_pairs={{0,4},{4,0},{1,5},{5,1},{2,6},{6,2},{3,7},{7,3},{8,12},{12,8},{9,1... | collective-permute-start | bytes 983048 | tf_op jit(solution)/shard_map/ppermute | solution.py:183
  43.4 10.5 %collective-permute-start.15 = (bf16[640,256]{1,0:T(8,128)(2,1)S(1)}, bf16[640,256]{1,0:T(8,128)(2,1)S(1)}, u32[]{:S(2)}, u32[]{:S(2)}) collective-permute-start(bf16[640,256]{1,0:T(8,128)(2,1)S(1)} %collective-permute-done.7.rest_0_), channel_id=1, source_target_pairs={{0,1},{1,0},{2,3},{3,2},{4,5},{5,4},{6,7},{7,6},{8,9},{9,8},{10,11... | collective-permute-start | bytes 983048 | tf_op jit(solution)/shard_map/ppermute | solution.py:183
  43.9 12.7 %collective-permute-start.16 = (bf16[640,256]{1,0:T(8,128)(2,1)S(1)}, bf16[640,256]{1,0:T(8,128)(2,1)S(1)}, u32[]{:S(2)}, u32[]{:S(2)}) collective-permute-start(bf16[640,256]{1,0:T(8,128)(2,1)S(1)} %collective-permute-done.12.rest_2_), channel_id=1, source_target_pairs={{0,4},{4,0},{1,5},{5,1},{2,6},{6,2},{3,7},{7,3},{8,12},{12,8},{9,1... | collective-permute-start | bytes 983048 | tf_op jit(solution)/shard_map/ppermute | solution.py:183
  52.0 7.1 %collective-permute-start.14 = (bf16[640,256]{1,0:T(8,128)(2,1)S(1)}, bf16[640,256]{1,0:T(8,128)(2,1)S(1)}, u32[]{:S(2)}, u32[]{:S(2)}) collective-permute-start(bf16[640,256]{1,0:T(8,128)(2,1)S(1)} %collective-permute-done.10.rest_0_), channel_id=1, source_target_pairs={{0,1},{1,0},{2,3},{3,2},{4,5},{5,4},{6,7},{7,6},{8,9},{9,8},{10,11... | collective-permute-start | bytes 983048 | tf_op jit(solution)/shard_map/ppermute | solution.py:183
  53.8 5.3 %copy-start.5 = (f32[128]{0:T(128)S(1)}, f32[128]{0:T(128)}, u32[]{:S(2)}) copy-start(f32[128]{0:T(128)} %param.12) | copy-start | bytes 1540
  59.1 11.3 %copy-start.3 = (bf16[1,256,4096]{2,1,0:T(8,128)(2,1)S(1)}, bf16[1,256,4096]{2,1,0:T(8,128)(2,1)}, u32[]{:S(2)}) copy-start(bf16[1,256,4096]{2,1,0:T(8,128)(2,1)} %param.10) | copy-start | bytes 6291460
  61.2 9.2 %collective-permute-start.19 = (bf16[256,512]{1,0:T(8,128)(2,1)S(1)}, bf16[256,512]{1,0:T(8,128)(2,1)S(1)}, u32[]{:S(2)}, u32[]{:S(2)}) collective-permute-start(bf16[256,512]{1,0:T(8,128)(2,1)S(1)} %get-tuple-element.48.rest_0_), channel_id=1, source_target_pairs={{0,1},{1,0},{2,3},{3,2},{4,5},{5,4},{6,7},{7,6},{8,9},{9,8},{10,11... | collective-permute-start | bytes 786440 | tf_op jit(solution)/shard_map/ppermute | solution.py:206
  61.9 13.1 %collective-permute-start.17 = (bf16[256,512]{1,0:T(8,128)(2,1)S(1)}, bf16[256,512]{1,0:T(8,128)(2,1)S(1)}, u32[]{:S(2)}, u32[]{:S(2)}) collective-permute-start(bf16[256,512]{1,0:T(8,128)(2,1)S(1)} %get-tuple-element.47), channel_id=1, source_target_pairs={{0,2},{1,3},{2,0},{3,1},{4,6},{5,7},{6,4},{7,5},{8,10},{9,11},{10,... | collective-permute-start | bytes 786440 | tf_op jit(solution)/shard_map/ppermute | solution.py:206
  61.9 13.1 %collective-permute-start.18 = (bf16[256,512]{1,0:T(8,128)(2,1)S(1)}, bf16[256,512]{1,0:T(8,128)(2,1)S(1)}, u32[]{:S(2)}, u32[]{:S(2)}) collective-permute-start(bf16[256,512]{1,0:T(8,128)(2,1)S(1)} %get-tuple-element.47), channel_id=1, source_target_pairs={{0,3},{1,2},{2,1},{3,0},{4,7},{5,6},{6,5},{7,4},{8,11},{9,10},{10,... | collective-permute-start | bytes 786440 | tf_op jit(solution)/shard_map/ppermute | solution.py:206

commit v7 on v6

--- a/solution.py
+++ b/solution.py
@@ -313,11 +313,11 @@
         elif k > 2:
             if acc is None:
                 acc = project([(0, True), (0, False)])
-            acc = project([(k - 2, True)], acc, also=beside[k - 2])
             if k == 3:
                 mine[k], acc, bias = tie((mine[k], acc, bias))
             else:
                 mine[k], acc = tie((mine[k], acc))
+            acc = project([(k - 2, True)], acc, also=beside[k - 2])
         across[k], beside[k] = swap(mine[k], "x"), swap(mine[k], "y")
     for k in range(1, chips_z):
         if k < end:

time: 80.2 us -> 78.9 us (0.984)
  waiting for transfers between devices: 23.3 us -> 22.4 us
  local copies, waits for them, and re-layouts: 5.46 us -> 4.59 us
    unnamed x18, local copies, waits for them, and re-layouts: 4.14 us -> 3.26 us
  transfers between devices with their start and end apart: 20 -> 20, of which waited for: 8 -> 9; matrix products, arithmetic and copies ran while one was open for 2% -> 2% of each run, Pallas kernels for 28% -> 28%
where the time goes in v7:
time: 78.9 us; the launch traced here: 78.6 us
  Pallas kernels  28.9 us (37%)
  waiting for transfers between devices  22.4 us (28%)
  starting transfers between devices  21.1 us (27%)
  local copies, waits for them, and re-layouts  4.59 us (6%)
  other arithmetic  1.42 us (2%)
    pallas_call x5, Pallas kernels, project(): pl.pallas_call(functools.partial(project_kernel, groups, also is None, ac...  13.3 us
    ppermute x13, starting transfers between devices, swap(): return lax.ppermute(array, axis, [(0, 1), (1, 0)])  11.5 us
    pallas_call x2, Pallas kernels, on_device(): pl.pallas_call(functools.partial(attend_kernel, m, count, cross), out_sha...  9.44 us
    ppermute x13, waiting for transfers between devices, swap(): return lax.ppermute(array, axis, [(0, 1), (1, 0)])  8.34 us
    ppermute x3, waiting for transfers between devices, on_device(): mine[k] = lax.ppermute(mine[k - 1], 'z', ring)  7.28 us
    ppermute x4, waiting for transfers between devices, along_ctx(): return lax.ppermute(array, ('core', 'ctx', 'x'), pairs)  6.82 us
    ppermute x3, starting transfers between devices, on_device(): mine[k] = lax.ppermute(mine[k - 1], 'z', ring)  5.89 us
    pallas_call x2, Pallas kernels, norm(): pl.pallas_call(functools.partial(norm_kernel, chunks), out_shape=[jax.Sha...  5.27 us
  transfers between devices with their start and end apart: 20, of which 9 were waited for; matrix products, arithmetic and copies ran while one was open for 2% of the time, Pallas kernels for 28%

profile of v7, /device:TPU:0, one launch (start us, length us, event | category | flops | bytes accessed | tf_op | source)
XLA Modules:
  0.0 78.6 jit_solution(5635551083821561984)
XLA Ops:
  0.0 1.2 %dynamic-slice_bitcast_fusion.1 = (bf16[1,320,256]{2,1,0:T(8,128)(2,1)S(1)}, bf16[1,320,256]{2,1,0:T(8,128)(2,1)S(1)}, bf16[1,320,256]{2,1,0:T(8,128)(2,1)S(1)}, bf16[1,320,256]{2,1,0:T(8,128)(2,1)S(1)}) fusion(bf16[320,512]{1,0:T(8,128)(2,1)} %param.14, s32[]{:T(128)S(6)} %select_n.31, s32[]{:T(128)S(6)} %select_n.29, bf16[320,512]{1,0:T(8,128)(2,1)} %param.13), kind=kLoop, calls=%fused_computation.7 | loop fusion | bytes 1310728 | tf_op jit(solution)/shard_map/stack | solution.py:210
  1.3 0.5 collective-permute-start
  1.9 1.2 %collective-permute-done = bf16[2,320,256]{2,1,0:T(8,128)(2,1)S(1)} collective-permute-done((bf16[2,320,256]{2,1,0:T(8,128)(2,1)S(1)}, bf16[2,320,256]{2,1,0:T(8,128)(2,1)S(1)}, u32[]{:S(2)}, u32[]{:S(2)}) %collective-permute-start) | collective-permute-done | bytes 327712 | tf_op jit(solution)/shard_map/ppermute | solution.py:183
  3.1 0.4 collective-permute-start.3
  3.6 2.8 %collective-permute-start.2 = (bf16[640,256]{1,0:T(8,128)(2,1)S(1)}, bf16[640,256]{1,0:T(8,128)(2,1)}, u32[]{:S(2)}, u32[]{:S(2)}) collective-permute-start(bf16[640,256]{1,0:T(8,128)(2,1)S(1)} %dynamic-slice_bitcast_fusion), channel_id=1, source_target_pairs={{0,8},{8,24},{24,16},{16,0},{1,9},{9,25},{25,17},{17,1},{2,10},{10... | collective-permute-start | bytes 983048 | tf_op jit(solution)/shard_map/ppermute | solution.py:294
  6.3 1.5 %collective-permute-start.1 = (bf16[2,640,256]{2,1,0:T(8,128)(2,1)S(1)}, bf16[2,640,256]{2,1,0:T(8,128)(2,1)}, u32[]{:S(2)}, u32[]{:S(2)}) collective-permute-start(bf16[2,640,256]{2,1,0:T(8,128)(2,1)S(1)} %constant_dynamic-update-slice_fusion.rest_0_), channel_id=1, source_target_pairs={{0,4},{4,0},{1,5},{5,1},{2,6},{6,2},{3,7},{7,3},{8,12},{12,8},{9,1... | collective-permute-start | bytes 1966088 | tf_op jit(solution)/shard_map/ppermute | solution.py:183
  7.9 0.1 collective-permute-start.4
  8.0 2.6 %norm.2 = (bf16[8,256,640]{2,1,0:T(8,128)(2,1)S(1)}, f32[8,128]{1,0:T(8,128)S(1)}) custom-call(bf16[256,5120]{1,0:T(8,128)(2,1)} %bitcast.6.hidden, f32[1,5120]{1,0:T(1,128)S(1)} %bitcast.24), custom_call_target="tpu_custom_call" | custom-call | flops 5242880 | bytes 5242880 | tf_op jit(solution)/shard_map/norm/pallas_call | solution.py:223
  10.6 0.0 collective-permute-done.3
  10.6 2.6 %norm.3 = (bf16[8,256,640]{2,1,0:T(8,128)(2,1)S(1)}, f32[8,128]{1,0:T(8,128)S(1)}) custom-call(bf16[256,5120]{1,0:T(8,128)(2,1)} %bitcast.8.hidden, f32[1,5120]{1,0:T(1,128)S(1)} %bitcast.25), custom_call_target="tpu_custom_call" | custom-call | flops 5242880 | bytes 5242880 | tf_op jit(solution)/shard_map/norm/pallas_call | solution.py:223
  13.3 1.5 %copy-done = bf16[8,256,640]{2,1,0:T(8,128)(2,1)} copy-done((bf16[8,256,640]{2,1,0:T(8,128)(2,1)}, bf16[8,256,640]{2,1,0:T(8,128)(2,1)S(1)}, u32[]{:S(2)}) %copy-start) | copy-done | bytes 2621464
  14.8 0.9 %collective-permute-done.2.rest_1_ = bf16[640,256]{1,0:T(8,128)(2,1)} collective-permute-done((bf16[640,256]{1,0:T(8,128)(2,1)S(1)}, bf16[640,256]{1,0:T(8,128)(2,1)}, u32[]{:S(2)}, u32[]{:S(2)}) %collective-permute-start.2) | collective-permute-done | bytes 327712 | tf_op jit(solution)/shard_map/ppermute | solution.py:294
  15.7 1.7 %collective-permute-start.6 = (bf16[640,256]{1,0:T(8,128)(2,1)}, bf16[640,256]{1,0:T(8,128)(2,1)}, u32[]{:S(2)}, u32[]{:S(2)}) collective-permute-start(bf16[640,256]{1,0:T(8,128)(2,1)} %collective-permute-done.2.rest_1_), channel_id=1, source_target_pairs={{0,8},{8,24},{24,16},{16,0},{1,9},{9,25},{25,17},{17,1},{2,10},{10... | collective-permute-start | bytes 983048 | tf_op jit(solution)/shard_map/ppermute | solution.py:294
  17.3 0.6 collective-permute-start.11
  17.9 1.5 %collective-permute-start.5 = (s32[2,256]{1,0:T(2,128)S(1)}, s32[2,256]{1,0:T(2,128)S(1)}, u32[]{:S(2)}, u32[]{:S(2)}) collective-permute-start(s32[2,256]{1,0:T(2,128)S(1)} %pad_add_fusion.refs_3_), channel_id=1, source_target_pairs={{0,1},{1,0},{2,3},{3,2},{4,5},{5,4},{6,7},{7,6},{8,9},{9,8},{10,11... | collective-permute-start | bytes 6152 | tf_op jit(solution)/shard_map/ppermute | solution.py:206
  19.4 0.5 collective-permute-start.13
  20.0 6.4 %collective-permute-done.6.rest_1_ = bf16[640,256]{1,0:T(8,128)(2,1)} collective-permute-done((bf16[640,256]{1,0:T(8,128)(2,1)}, bf16[640,256]{1,0:T(8,128)(2,1)}, u32[]{:S(2)}, u32[]{:S(2)}) %collective-permute-start.6) | collective-permute-done | bytes 327712 | tf_op jit(solution)/shard_map/ppermute | solution.py:294
  26.3 1.5 %collective-permute-start.7 = (bf16[640,256]{1,0:T(8,128)(2,1)}, bf16[640,256]{1,0:T(8,128)(2,1)S(1)}, u32[]{:S(2)}, u32[]{:S(2)}) collective-permute-start(bf16[640,256]{1,0:T(8,128)(2,1)} %collective-permute-done.6.rest_1_), channel_id=1, source_target_pairs={{0,8},{8,24},{24,16},{16,0},{1,9},{9,25},{25,17},{17,1},{2,10},{10... | collective-permute-start | bytes 983048 | tf_op jit(solution)/shard_map/ppermute | solution.py:294
  27.8 1.5 %collective-permute-start.10 = (bf16[640,256]{1,0:T(8,128)(2,1)}, bf16[640,256]{1,0:T(8,128)(2,1)S(1)}, u32[]{:S(2)}, u32[]{:S(2)}) collective-permute-start(bf16[640,256]{1,0:T(8,128)(2,1)} %collective-permute-done.6.rest_1_), channel_id=1, source_target_pairs={{0,1},{1,0},{2,3},{3,2},{4,5},{5,4},{6,7},{7,6},{8,9},{9,8},{10,11... | collective-permute-start | bytes 983048 | tf_op jit(solution)/shard_map/ppermute | solution.py:183
  29.3 0.7 collective-permute-start.9
  29.9 0.2 collective-permute-done.11.rest_0_.rest_3_
  30.2 1.5 %collective-permute-start.12 = (bf16[640,256]{1,0:T(8,128)(2,1)}, bf16[640,256]{1,0:T(8,128)(2,1)S(1)}, u32[]{:S(2)}, u32[]{:S(2)}) collective-permute-start(bf16[640,256]{1,0:T(8,128)(2,1)} %collective-permute-done.11.rest_0_.rest_3_), channel_id=1, source_target_pairs={{0,1},{1,0},{2,3},{3,2},{4,5},{5,4},{6,7},{7,6},{8,9},{9,8},{10,11... | collective-permute-start | bytes 983048 | tf_op jit(solution)/shard_map/ppermute | solution.py:183
  31.7 0.1 pad_add_fusion.1.place
  31.7 1.7 %copy-done.1 = bf16[8,256,640]{2,1,0:T(8,128)(2,1)S(1)} copy-done((bf16[8,256,640]{2,1,0:T(8,128)(2,1)S(1)}, bf16[8,256,640]{2,1,0:T(8,128)(2,1)}, u32[]{:S(2)}) %copy-start.1) | copy-done | bytes 2621464
  33.5 3.3 %project.5.rest_3_ = f32[2,512,256]{2,1,0:T(8,128)S(1)} custom-call(s32[3]{0:T(128)S(1)} %pad_add_fusion.1.place, bf16[8,256,640]{2,1,0:T(8,128)(2,1)S(1)} %get-tuple-element.38.own, bf16[8,256,640]{2,1,0:T(8,128)(2,1)S(1)} %copy-done.1, bf16[2,640,256]{2,1,0:T(8,128)(2,1)S(1)} %constant_dynamic-update-slice_fusion.rest_0_, ...), custom_call_target="tpu_custom_call" | custom-call | flops 671088640 | bytes 2621440 | tf_op jit(solution)/shard_map/project/pallas_call | solution.py:258
  36.8 0.8 %mask.1 = (f32[256,512]{1,0:T(8,128)S(1)}, s32[2]{0:T(128)S(1)}) custom-call(bf16[2,640,256]{2,1,0:T(8,128)(2,1)} %collective-permute-done.1.refs_0_.rest_1_, f32[8,128]{1,0:T(8,128)S(1)} %get-tuple-element.33.refs_1_, f32[8,128]{1,0:T(8,128)S(1)} %get-tuple-element.34.refs_2_, s32[2,256]{1,0:T(2,128)S(1)} %pad_add_fusion.refs_3_, ...), custom_call_target="tpu_custom_call" | custom-call | flops 1000000000 | bytes 3333333 | tf_op jit(solution)/shard_map/mask/pallas_call | solution.py:299
  37.7 2.4 %collective-permute-start.8 = (bf16[640,256]{1,0:T(8,128)(2,1)S(1)}, bf16[640,256]{1,0:T(8,128)(2,1)S(1)}, u32[]{:S(2)}, u32[]{:S(2)}) collective-permute-start(bf16[640,256]{1,0:T(8,128)(2,1)S(1)} %collective-permute-done.7.rest_0_), channel_id=1, source_target_pairs={{0,4},{4,0},{1,5},{5,1},{2,6},{6,2},{3,7},{7,3},{8,12},{12,8},{9,1... | collective-permute-start | bytes 983048 | tf_op jit(solution)/shard_map/ppermute | solution.py:183
  40.0 0.0 collective-permute-start.15
  40.1 0.2 collective-permute-start.16
  40.3 2.3 %project.6.rest_5_ = f32[2,512,256]{2,1,0:T(8,128)S(1)} custom-call(s32[3]{0:T(128)S(1)} %pad_add_fusion.1.place, bf16[8,256,640]{2,1,0:T(8,128)(2,1)S(1)} %get-tuple-element.38.own, bf16[8,256,640]{2,1,0:T(8,128)(2,1)S(1)} %copy-done.2, bf16[640,256]{1,0:T(8,128)(2,1)} %collective-permute-done.11.rest_0_.rest_3_, ...), custom_call_target="tpu_custom_call" | custom-call | flops 335544320 | bytes 1310720 | tf_op jit(solution)/shard_map/project/pallas_call | solution.py:258
  42.6 0.0 copy-start.8
  42.7 3.0 %collective-permute-done.12.rest_4_ = bf16[640,256]{1,0:T(8,128)(2,1)S(1)} collective-permute-done((bf16[640,256]{1,0:T(8,128)(2,1)}, bf16[640,256]{1,0:T(8,128)(2,1)S(1)}, u32[]{:S(2)}, u32[]{:S(2)}) %collective-permute-start.12) | collective-permute-done | bytes 327712 | tf_op jit(solution)/shard_map/ppermute | solution.py:183
  45.6 3.1 %project.7.rest_4_ = f32[2,512,256]{2,1,0:T(8,128)S(1)} custom-call(s32[3]{0:T(128)S(1)} %pad_add_fusion.1.place, bf16[8,256,640]{2,1,0:T(8,128)(2,1)S(1)} %get-tuple-element.38.own, bf16[8,256,640]{2,1,0:T(8,128)(2,1)S(1)} %copy-done.2, bf16[640,256]{1,0:T(8,128)(2,1)S(1)} %collective-permute-done.9.rest_0_.rest_2_, ...), custom_call_target="tpu_custom_call" | custom-call | flops 5368709120 | bytes 20971520 | tf_op jit(solution)/shard_map/project/pallas_call | solution.py:258
  48.8 1.6 %collective-permute-start.14 = (bf16[640,256]{1,0:T(8,128)(2,1)S(1)}, bf16[640,256]{1,0:T(8,128)(2,1)S(1)}, u32[]{:S(2)}, u32[]{:S(2)}) collective-permute-start(bf16[640,256]{1,0:T(8,128)(2,1)S(1)} %collective-permute-done.8.rest_0_), channel_id=1, source_target_pairs={{0,1},{1,0},{2,3},{3,2},{4,5},{5,4},{6,7},{7,6},{8,9},{9,8},{10,11... | collective-permute-start | bytes 983048 | tf_op jit(solution)/shard_map/ppermute | solution.py:183
  50.3 1.0 %fusion = (f32[512,64]{1,0:T(8,128)S(1)}, f32[512,64]{1,0:T(8,128)S(1)}, f32[512,64]{1,0:T(8,128)S(1)}) fusion(f32[64]{0:T(128)S(1)} %copy-done.8, f32[512]{0:T(512)S(1)} %add_convert_fusion), kind=kLoop, calls=%fused_computation.11 | loop fusion | flops 65536 | bytes 395520 | tf_op jit(solution)/shard_map/neg | solution.py:335
  51.3 0.1 pad_maximum_fusion.1.rest_3_
  51.5 0.1 pad_maximum_fusion.2.rest_4_
  51.6 0.0 copy-start.5
  51.6 1.0 %collective-permute-done.15.rest_1_ = bf16[640,256]{1,0:T(8,128)(2,1)S(1)} collective-permute-done((bf16[640,256]{1,0:T(8,128)(2,1)S(1)}, bf16[640,256]{1,0:T(8,128)(2,1)S(1)}, u32[]{:S(2)}, u32[]{:S(2)}) %collective-permute-start.15) | collective-permute-done | bytes 327712 | tf_op jit(solution)/shard_map/ppermute | solution.py:183
  52.7 0.7 collective-permute-done.16.rest_3_
  53.3 2.5 %project.8.rest_2_ = f32[2,512,256]{2,1,0:T(8,128)S(1)} custom-call(s32[3]{0:T(128)S(1)} %pad_add_fusion.1.place, bf16[8,256,640]{2,1,0:T(8,128)(2,1)S(1)} %get-tuple-element.38.own, bf16[8,256,640]{2,1,0:T(8,128)(2,1)S(1)} %copy-done.2, bf16[640,256]{1,0:T(8,128)(2,1)S(1)} %collective-permute-done.7.rest_0_, ...), custom_call_target="tpu_custom_call" | custom-call | flops 671088640 | bytes 2621440 | tf_op jit(solution)/shard_map/project/pallas_call | solution.py:258
  55.9 2.2 %collective-permute-done.14.rest_1_ = bf16[640,256]{1,0:T(8,128)(2,1)S(1)} collective-permute-done((bf16[640,256]{1,0:T(8,128)(2,1)S(1)}, bf16[640,256]{1,0:T(8,128)(2,1)S(1)}, u32[]{:S(2)}, u32[]{:S(2)}) %collective-permute-start.14) | collective-permute-done | bytes 327712 | tf_op jit(solution)/shard_map/ppermute | solution.py:183
  58.1 2.1 %project.9 = (bf16[256,512]{1,0:T(8,128)(2,1)S(1)}, bf16[256,512]{1,0:T(8,128)(2,1)S(1)}) custom-call(s32[3]{0:T(128)S(1)} %pad_add_fusion.1.place, bf16[8,256,640]{2,1,0:T(8,128)(2,1)S(1)} %get-tuple-element.38.own, bf16[8,256,640]{2,1,0:T(8,128)(2,1)S(1)} %copy-done.2, bf16[640,256]{1,0:T(8,128)(2,1)S(1)} %collective-permute-done.8.rest_0_, ...), custom_call_target="tpu_custom_call" | custom-call | flops 335544320 | bytes 1310720 | tf_op jit(solution)/shard_map/project/pallas_call | solution.py:258
  60.1 1.6 %collective-permute-start.19 = (bf16[256,512]{1,0:T(8,128)(2,1)S(1)}, bf16[256,512]{1,0:T(8,128)(2,1)S(1)}, u32[]{:S(2)}, u32[]{:S(2)}) collective-permute-start(bf16[256,512]{1,0:T(8,128)(2,1)S(1)} %get-tuple-element.48.rest_0_), channel_id=1, source_target_pairs={{0,1},{1,0},{2,3},{3,2},{4,5},{5,4},{6,7},{7,6},{8,9},{9,8},{10,11... | collective-permute-start | bytes 786440 | tf_op jit(solution)/shard_map/ppermute | solution.py:206
  61.7 0.6 collective-permute-start.18
  62.4 6.8 %collective-permute-done.19.rest_1_ = bf16[256,512]{1,0:T(8,128)(2,1)S(1)} collective-permute-done((bf16[256,512]{1,0:T(8,128)(2,1)S(1)}, bf16[256,512]{1,0:T(8,128)(2,1)S(1)}, u32[]{:S(2)}, u32[]{:S(2)}) %collective-permute-start.19) | collective-permute-done | bytes 262176 | tf_op jit(solution)/shard_map/ppermute | solution.py:206
  69.2 4.6 %attend.2.rest_2_ = bf16[256,4096]{1,0:T(8,128)(2,1)} custom-call(s32[1]{0:T(128)} %bitcast.place, s32[2]{0:T(128)S(1)} %get-tuple-element.36.needs, bf16[256,4096]{1,0:T(8,128)(2,1)S(1)} %bitcast.22, f32[256,512]{1,0:T(8,128)S(1)} %get-tuple-element.41.bias, bf16[256,512]{1,0:T(8,128)(2,1)S(1)} %get-tuple-element.48.rest_0_, ...), custom_call_target="tpu_custom_call" | custom-call | flops 1073741824 | bytes 2097152 | tf_op jit(solution)/shard_map/attend/pallas_call | solution.py:348
  73.8 4.8 %attend.3 = bf16[256,4096]{1,0:T(8,128)(2,1)} custom-call(s32[1]{0:T(128)} %bitcast.place, s32[2]{0:T(128)S(1)} %get-tuple-element.36.needs, bf16[256,4096]{1,0:T(8,128)(2,1)S(1)} %bitcast.23, f32[256,512]{1,0:T(8,128)S(1)} %get-tuple-element.41.bias, bf16[256,512]{1,0:T(8,128)(2,1)S(1)} %collective-permute-done.17.rest_0_, ...), custom_call_target="tpu_custom_call", output_to_operand_aliasing={{}: (6, {})} | custom-call | flops 1073741824 | bytes 2097152 | tf_op jit(solution)/shard_map/attend/pallas_call | solution.py:348
  (33 shorter events, 0.2 us)
Async XLA Ops:
  0.0 7.8 %copy-start.7 = (s32[1,256]{1,0:T(1,128)S(1)}, s32[1,256]{1,0:T(1,128)}, u32[]{:S(2)}) copy-start(s32[1,256]{1,0:T(1,128)} %param.15) | copy-start | bytes 3076
  0.0 7.8 %copy-start.6 = (s32[1,256]{1,0:T(1,128)S(1)}, s32[1,256]{1,0:T(1,128)}, u32[]{:S(2)}) copy-start(s32[1,256]{1,0:T(1,128)} %param.16) | copy-start | bytes 3076
  0.0 7.9 %copy-start.4 = (f32[5120]{0:T(1024)S(1)}, f32[5120]{0:T(1024)}, u32[]{:S(2)}) copy-start(f32[5120]{0:T(1024)} %param.11) | copy-start | bytes 61444
  1.3 1.8 %collective-permute-start = (bf16[2,320,256]{2,1,0:T(8,128)(2,1)S(1)}, bf16[2,320,256]{2,1,0:T(8,128)(2,1)S(1)}, u32[]{:S(2)}, u32[]{:S(2)}) collective-permute-start(bf16[2,320,256]{2,1,0:T(8,128)(2,1)S(1)} %pad_maximum_fusion), channel_id=1, source_target_pairs={{0,2},{2,0},{1,3},{3,1},{4,6},{6,4},{5,7},{7,5},{8,10},{10,8},{9,1... | collective-permute-start | bytes 983048 | tf_op jit(solution)/shard_map/ppermute | solution.py:183
  3.1 7.5 %collective-permute-start.3 = (bf16[1,256,5120]{2,1,0:T(8,128)(2,1)}, bf16[1,256,5120]{2,1,0:T(8,128)(2,1)}, u32[]{:S(2)}, u32[]{:S(2)}) collective-permute-start(bf16[1,256,5120]{2,1,0:T(8,128)(2,1)} %param.9), channel_id=1, source_target_pairs={{0,2},{2,0},{1,3},{3,1},{4,6},{6,4},{5,7},{7,5},{8,10},{10,8},{9,1... | collective-permute-start | bytes 7864328 | tf_op jit(solution)/shard_map/ppermute | solution.py:183
  3.6 12.1 %collective-permute-start.2 = (bf16[640,256]{1,0:T(8,128)(2,1)S(1)}, bf16[640,256]{1,0:T(8,128)(2,1)}, u32[]{:S(2)}, u32[]{:S(2)}) collective-permute-start(bf16[640,256]{1,0:T(8,128)(2,1)S(1)} %dynamic-slice_bitcast_fusion), channel_id=1, source_target_pairs={{0,8},{8,24},{24,16},{16,0},{1,9},{9,25},{25,17},{17,1},{2,10},{10... | collective-permute-start | bytes 983048 | tf_op jit(solution)/shard_map/ppermute | solution.py:294
  6.3 21.4 %collective-permute-start.1 = (bf16[2,640,256]{2,1,0:T(8,128)(2,1)S(1)}, bf16[2,640,256]{2,1,0:T(8,128)(2,1)}, u32[]{:S(2)}, u32[]{:S(2)}) collective-permute-start(bf16[2,640,256]{2,1,0:T(8,128)(2,1)S(1)} %constant_dynamic-update-slice_fusion.rest_0_), channel_id=1, source_target_pairs={{0,4},{4,0},{1,5},{5,1},{2,6},{6,2},{3,7},{7,3},{8,12},{12,8},{9,1... | collective-permute-start | bytes 1966088 | tf_op jit(solution)/shard_map/ppermute | solution.py:183
  7.9 6.9 %collective-permute-start.4 = (s32[2,256]{1,0:T(2,128)S(1)}, s32[2,256]{1,0:T(2,128)S(1)}, u32[]{:S(2)}, u32[]{:S(2)}) collective-permute-start(s32[2,256]{1,0:T(2,128)S(1)} %pad_add_fusion.refs_3_), channel_id=1, source_target_pairs={{0,2},{2,0},{1,3},{3,1},{4,6},{6,4},{5,7},{7,5},{8,10},{10,8},{9,1... | collective-permute-start | bytes 6152 | tf_op jit(solution)/shard_map/ppermute | solution.py:183
  13.3 1.5 %copy-start = (bf16[8,256,640]{2,1,0:T(8,128)(2,1)}, bf16[8,256,640]{2,1,0:T(8,128)(2,1)S(1)}, u32[]{:S(2)}) copy-start(bf16[8,256,640]{2,1,0:T(8,128)(2,1)S(1)} %get-tuple-element.39.other) | copy-start | bytes 7864324
  15.7 10.6 %collective-permute-start.6 = (bf16[640,256]{1,0:T(8,128)(2,1)}, bf16[640,256]{1,0:T(8,128)(2,1)}, u32[]{:S(2)}, u32[]{:S(2)}) collective-permute-start(bf16[640,256]{1,0:T(8,128)(2,1)} %collective-permute-done.2.rest_1_), channel_id=1, source_target_pairs={{0,8},{8,24},{24,16},{16,0},{1,9},{9,25},{25,17},{17,1},{2,10},{10... | collective-permute-start | bytes 983048 | tf_op jit(solution)/shard_map/ppermute | solution.py:294
  17.3 12.8 %collective-permute-start.11 = (bf16[640,256]{1,0:T(8,128)(2,1)}, bf16[640,256]{1,0:T(8,128)(2,1)}, u32[]{:S(2)}, u32[]{:S(2)}) collective-permute-start(bf16[640,256]{1,0:T(8,128)(2,1)} %collective-permute-done.2.rest_1_), channel_id=1, source_target_pairs={{0,4},{4,0},{1,5},{5,1},{2,6},{6,2},{3,7},{7,3},{8,12},{12,8},{9,1... | collective-permute-start | bytes 983048 | tf_op jit(solution)/shard_map/ppermute | solution.py:183
  17.9 11.3 %collective-permute-start.5 = (s32[2,256]{1,0:T(2,128)S(1)}, s32[2,256]{1,0:T(2,128)S(1)}, u32[]{:S(2)}, u32[]{:S(2)}) collective-permute-start(s32[2,256]{1,0:T(2,128)S(1)} %pad_add_fusion.refs_3_), channel_id=1, source_target_pairs={{0,1},{1,0},{2,3},{3,2},{4,5},{5,4},{6,7},{7,6},{8,9},{9,8},{10,11... | collective-permute-start | bytes 6152 | tf_op jit(solution)/shard_map/ppermute | solution.py:206
  19.4 20.6 %collective-permute-start.13 = (bf16[640,256]{1,0:T(8,128)(2,1)}, bf16[640,256]{1,0:T(8,128)(2,1)S(1)}, u32[]{:S(2)}, u32[]{:S(2)}) collective-permute-start(bf16[640,256]{1,0:T(8,128)(2,1)} %collective-permute-done.2.rest_1_), channel_id=1, source_target_pairs={{0,1},{1,0},{2,3},{3,2},{4,5},{5,4},{6,7},{7,6},{8,9},{9,8},{10,11... | collective-permute-start | bytes 983048 | tf_op jit(solution)/shard_map/ppermute | solution.py:183
  26.3 11.3 %collective-permute-start.7 = (bf16[640,256]{1,0:T(8,128)(2,1)}, bf16[640,256]{1,0:T(8,128)(2,1)S(1)}, u32[]{:S(2)}, u32[]{:S(2)}) collective-permute-start(bf16[640,256]{1,0:T(8,128)(2,1)} %collective-permute-done.6.rest_1_), channel_id=1, source_target_pairs={{0,8},{8,24},{24,16},{16,0},{1,9},{9,25},{25,17},{17,1},{2,10},{10... | collective-permute-start | bytes 983048 | tf_op jit(solution)/shard_map/ppermute | solution.py:294
  27.8 12.3 %collective-permute-start.10 = (bf16[640,256]{1,0:T(8,128)(2,1)}, bf16[640,256]{1,0:T(8,128)(2,1)S(1)}, u32[]{:S(2)}, u32[]{:S(2)}) collective-permute-start(bf16[640,256]{1,0:T(8,128)(2,1)} %collective-permute-done.6.rest_1_), channel_id=1, source_target_pairs={{0,1},{1,0},{2,3},{3,2},{4,5},{5,4},{6,7},{7,6},{8,9},{9,8},{10,11... | collective-permute-start | bytes 983048 | tf_op jit(solution)/shard_map/ppermute | solution.py:183
  29.3 16.4 %collective-permute-start.9 = (bf16[640,256]{1,0:T(8,128)(2,1)}, bf16[640,256]{1,0:T(8,128)(2,1)S(1)}, u32[]{:S(2)}, u32[]{:S(2)}) collective-permute-start(bf16[640,256]{1,0:T(8,128)(2,1)} %collective-permute-done.6.rest_1_), channel_id=1, source_target_pairs={{0,4},{4,0},{1,5},{5,1},{2,6},{6,2},{3,7},{7,3},{8,12},{12,8},{9,1... | collective-permute-start | bytes 983048 | tf_op jit(solution)/shard_map/ppermute | solution.py:183
  30.2 15.5 %collective-permute-start.12 = (bf16[640,256]{1,0:T(8,128)(2,1)}, bf16[640,256]{1,0:T(8,128)(2,1)S(1)}, u32[]{:S(2)}, u32[]{:S(2)}) collective-permute-start(bf16[640,256]{1,0:T(8,128)(2,1)} %collective-permute-done.11.rest_0_.rest_3_), channel_id=1, source_target_pairs={{0,1},{1,0},{2,3},{3,2},{4,5},{5,4},{6,7},{7,6},{8,9},{9,8},{10,11... | collective-permute-start | bytes 983048 | tf_op jit(solution)/shard_map/ppermute | solution.py:183
  31.7 1.7 %copy-start.1 = (bf16[8,256,640]{2,1,0:T(8,128)(2,1)S(1)}, bf16[8,256,640]{2,1,0:T(8,128)(2,1)}, u32[]{:S(2)}) copy-start(bf16[8,256,640]{2,1,0:T(8,128)(2,1)} %copy-done) | copy-start | bytes 7864324
  36.8 3.5 %copy-start.2 = (bf16[8,256,640]{2,1,0:T(8,128)(2,1)S(1)}, bf16[8,256,640]{2,1,0:T(8,128)(2,1)}, u32[]{:S(2)}) copy-start(bf16[8,256,640]{2,1,0:T(8,128)(2,1)} %copy-done) | copy-start | bytes 7864324
  37.7 11.1 %collective-permute-start.8 = (bf16[640,256]{1,0:T(8,128)(2,1)S(1)}, bf16[640,256]{1,0:T(8,128)(2,1)S(1)}, u32[]{:S(2)}, u32[]{:S(2)}) collective-permute-start(bf16[640,256]{1,0:T(8,128)(2,1)S(1)} %collective-permute-done.7.rest_0_), channel_id=1, source_target_pairs={{0,4},{4,0},{1,5},{5,1},{2,6},{6,2},{3,7},{7,3},{8,12},{12,8},{9,1... | collective-permute-start | bytes 983048 | tf_op jit(solution)/shard_map/ppermute | solution.py:183
  40.0 12.6 %collective-permute-start.15 = (bf16[640,256]{1,0:T(8,128)(2,1)S(1)}, bf16[640,256]{1,0:T(8,128)(2,1)S(1)}, u32[]{:S(2)}, u32[]{:S(2)}) collective-permute-start(bf16[640,256]{1,0:T(8,128)(2,1)S(1)} %collective-permute-done.7.rest_0_), channel_id=1, source_target_pairs={{0,1},{1,0},{2,3},{3,2},{4,5},{5,4},{6,7},{7,6},{8,9},{9,8},{10,11... | collective-permute-start | bytes 983048 | tf_op jit(solution)/shard_map/ppermute | solution.py:183
  40.1 13.3 %collective-permute-start.16 = (bf16[640,256]{1,0:T(8,128)(2,1)S(1)}, bf16[640,256]{1,0:T(8,128)(2,1)S(1)}, u32[]{:S(2)}, u32[]{:S(2)}) collective-permute-start(bf16[640,256]{1,0:T(8,128)(2,1)S(1)} %collective-permute-done.10.rest_2_), channel_id=1, source_target_pairs={{0,4},{4,0},{1,5},{5,1},{2,6},{6,2},{3,7},{7,3},{8,12},{12,8},{9,1... | collective-permute-start | bytes 983048 | tf_op jit(solution)/shard_map/ppermute | solution.py:183
  42.6 7.7 %copy-start.8 = (f32[64]{0:T(128)S(1)}, f32[64]{0:T(128)}, u32[]{:S(2)}) copy-start(f32[64]{0:T(128)} %constant.45) | copy-start | bytes 772
  48.8 9.3 %collective-permute-start.14 = (bf16[640,256]{1,0:T(8,128)(2,1)S(1)}, bf16[640,256]{1,0:T(8,128)(2,1)S(1)}, u32[]{:S(2)}, u32[]{:S(2)}) collective-permute-start(bf16[640,256]{1,0:T(8,128)(2,1)S(1)} %collective-permute-done.8.rest_0_), channel_id=1, source_target_pairs={{0,1},{1,0},{2,3},{3,2},{4,5},{5,4},{6,7},{7,6},{8,9},{9,8},{10,11... | collective-permute-start | bytes 983048 | tf_op jit(solution)/shard_map/ppermute | solution.py:183
  51.6 6.5 %copy-start.5 = (f32[128]{0:T(128)S(1)}, f32[128]{0:T(128)}, u32[]{:S(2)}) copy-start(f32[128]{0:T(128)} %param.12) | copy-start | bytes 1540
  58.1 11.1 %copy-start.3 = (bf16[1,256,4096]{2,1,0:T(8,128)(2,1)S(1)}, bf16[1,256,4096]{2,1,0:T(8,128)(2,1)}, u32[]{:S(2)}) copy-start(bf16[1,256,4096]{2,1,0:T(8,128)(2,1)} %param.10) | copy-start | bytes 6291460
  60.1 9.0 %collective-permute-start.19 = (bf16[256,512]{1,0:T(8,128)(2,1)S(1)}, bf16[256,512]{1,0:T(8,128)(2,1)S(1)}, u32[]{:S(2)}, u32[]{:S(2)}) collective-permute-start(bf16[256,512]{1,0:T(8,128)(2,1)S(1)} %get-tuple-element.48.rest_0_), channel_id=1, source_target_pairs={{0,1},{1,0},{2,3},{3,2},{4,5},{5,4},{6,7},{7,6},{8,9},{9,8},{10,11... | collective-permute-start | bytes 786440 | tf_op jit(solution)/shard_map/ppermute | solution.py:206
  61.7 12.1 %collective-permute-start.17 = (bf16[256,512]{1,0:T(8,128)(2,1)S(1)}, bf16[256,512]{1,0:T(8,128)(2,1)S(1)}, u32[]{:S(2)}, u32[]{:S(2)}) collective-permute-start(bf16[256,512]{1,0:T(8,128)(2,1)S(1)} %get-tuple-element.47), channel_id=1, source_target_pairs={{0,2},{1,3},{2,0},{3,1},{4,6},{5,7},{6,4},{7,5},{8,10},{9,11},{10,... | collective-permute-start | bytes 786440 | tf_op jit(solution)/shard_map/ppermute | solution.py:206
  61.7 12.1 %collective-permute-start.18 = (bf16[256,512]{1,0:T(8,128)(2,1)S(1)}, bf16[256,512]{1,0:T(8,128)(2,1)S(1)}, u32[]{:S(2)}, u32[]{:S(2)}) collective-permute-start(bf16[256,512]{1,0:T(8,128)(2,1)S(1)} %get-tuple-element.47), channel_id=1, source_target_pairs={{0,3},{1,2},{2,1},{3,0},{4,7},{5,6},{6,5},{7,4},{8,11},{9,10},{10,... | collective-permute-start | bytes 786440 | tf_op jit(solution)/shard_map/ppermute | solution.py:206

commit v8 on v7

--- a/solution.py
+++ b/solution.py
@@ -135,7 +135,11 @@
                     here = slice(tile * tile_rows, (tile + 1) * tile_rows)
                     there = tile * length + i * tile_rows
                     keys[there : there + tile_rows, :] = source[here, left : left + HD]
-                    values[there : there + tile_rows, :] = source[here, left + HD : left + 2 * HD]
+                    values[there : there + tile_rows, :HD] = source[here, left + HD : left + 2 * HD]
+
+    @pl.when(step == 0)
+    def _():
+        values[:, HD:] = jnp.ones((pieces * count, HD), jnp.bfloat16)
 
     factor = math.log2(math.e) / math.sqrt(HD)
 
@@ -160,16 +164,15 @@
                 ahead = score(step + 1)
             top = jnp.max(scores, axis=-1, keepdims=True)
             weights = jnp.exp2((scores - top) * factor)
-            total = jnp.sum(weights, axis=-1, keepdims=True)
             summed = jnp.dot(
                 weights.astype(jnp.bfloat16).reshape(WIDE * tile_rows, high),
                 v,
                 preferred_element_type=jnp.float32,
-            ).reshape(WIDE, tile_rows, HD)
-            result = (summed * (1.0 / total)).astype(jnp.bfloat16)
+            )
+            result = (summed[:, :HD] / summed[:, HD:]).astype(jnp.bfloat16)
             for i in range(WIDE):
                 g = step * WIDE + i
-                out[rows, g * HD : (g + 1) * HD] = result[i]
+                out[rows, g * HD : (g + 1) * HD] = result[i * tile_rows : (i + 1) * tile_rows]
 
     for tile in range(TILES):
         for need, high in ((0, tile + 1), (1, TILES)):
@@ -356,7 +359,7 @@
                 out_specs=pl.BlockSpec((count, G * HD), block),
                 scratch_shapes=[
                     pltpu.VMEM((m * count, HD), bf16),
-                    pltpu.VMEM((m * count, HD), bf16),
+                    pltpu.VMEM((m * count, 2 * HD), bf16),
                 ],
             ),
             input_output_aliases={4 + m: 0} if earlier else {},

time: 78.9 us -> 78.6 us (level)
  no operation moved by 1% of the time
where the time goes in v8:
time: 78.6 us; the launch traced here: 78.3 us
  Pallas kernels  28.6 us (36%)
  waiting for transfers between devices  22.4 us (28%)
  starting transfers between devices  21.1 us (27%)
  local copies, waits for them, and re-layouts  4.59 us (6%)
  other arithmetic  1.42 us (2%)
    pallas_call x5, Pallas kernels, project(): pl.pallas_call(functools.partial(project_kernel, groups, also is None, ac...  13.3 us
    ppermute x13, starting transfers between devices, swap(): return lax.ppermute(array, axis, [(0, 1), (1, 0)])  11.5 us
    pallas_call x2, Pallas kernels, on_device(): pl.pallas_call(functools.partial(attend_kernel, m, count, cross), out_sha...  9.12 us
    ppermute x13, waiting for transfers between devices, swap(): return lax.ppermute(array, axis, [(0, 1), (1, 0)])  8.34 us
    ppermute x3, waiting for transfers between devices, on_device(): mine[k] = lax.ppermute(mine[k - 1], 'z', ring)  7.28 us
    ppermute x4, waiting for transfers between devices, along_ctx(): return lax.ppermute(array, ('core', 'ctx', 'x'), pairs)  6.82 us
    ppermute x3, starting transfers between devices, on_device(): mine[k] = lax.ppermute(mine[k - 1], 'z', ring)  5.89 us
    pallas_call x2, Pallas kernels, norm(): pl.pallas_call(functools.partial(norm_kernel, chunks), out_shape=[jax.Sha...  5.27 us
  transfers between devices with their start and end apart: 20, of which 9 were waited for; matrix products, arithmetic and copies ran while one was open for 2% of the time, Pallas kernels for 28%

profile of v8, /device:TPU:0, one launch (start us, length us, event | category | flops | bytes accessed | tf_op | source)
XLA Modules:
  0.0 78.3 jit_solution(11235030957537772872)
XLA Ops:
  0.0 1.2 %dynamic-slice_bitcast_fusion.1 = (bf16[1,320,256]{2,1,0:T(8,128)(2,1)S(1)}, bf16[1,320,256]{2,1,0:T(8,128)(2,1)S(1)}, bf16[1,320,256]{2,1,0:T(8,128)(2,1)S(1)}, bf16[1,320,256]{2,1,0:T(8,128)(2,1)S(1)}) fusion(bf16[320,512]{1,0:T(8,128)(2,1)} %param.14, s32[]{:T(128)S(6)} %select_n.31, s32[]{:T(128)S(6)} %select_n.29, bf16[320,512]{1,0:T(8,128)(2,1)} %param.13), kind=kLoop, calls=%fused_computation.7 | loop fusion | bytes 1310728 | tf_op jit(solution)/shard_map/stack | solution.py:213
  1.3 0.5 collective-permute-start
  1.9 1.2 %collective-permute-done = bf16[2,320,256]{2,1,0:T(8,128)(2,1)S(1)} collective-permute-done((bf16[2,320,256]{2,1,0:T(8,128)(2,1)S(1)}, bf16[2,320,256]{2,1,0:T(8,128)(2,1)S(1)}, u32[]{:S(2)}, u32[]{:S(2)}) %collective-permute-start) | collective-permute-done | bytes 327712 | tf_op jit(solution)/shard_map/ppermute | solution.py:186
  3.1 0.4 collective-permute-start.3
  3.6 2.8 %collective-permute-start.2 = (bf16[640,256]{1,0:T(8,128)(2,1)S(1)}, bf16[640,256]{1,0:T(8,128)(2,1)}, u32[]{:S(2)}, u32[]{:S(2)}) collective-permute-start(bf16[640,256]{1,0:T(8,128)(2,1)S(1)} %dynamic-slice_bitcast_fusion), channel_id=1, source_target_pairs={{0,8},{8,24},{24,16},{16,0},{1,9},{9,25},{25,17},{17,1},{2,10},{10... | collective-permute-start | bytes 983048 | tf_op jit(solution)/shard_map/ppermute | solution.py:297
  6.3 1.5 %collective-permute-start.1 = (bf16[2,640,256]{2,1,0:T(8,128)(2,1)S(1)}, bf16[2,640,256]{2,1,0:T(8,128)(2,1)}, u32[]{:S(2)}, u32[]{:S(2)}) collective-permute-start(bf16[2,640,256]{2,1,0:T(8,128)(2,1)S(1)} %constant_dynamic-update-slice_fusion.rest_0_), channel_id=1, source_target_pairs={{0,4},{4,0},{1,5},{5,1},{2,6},{6,2},{3,7},{7,3},{8,12},{12,8},{9,1... | collective-permute-start | bytes 1966088 | tf_op jit(solution)/shard_map/ppermute | solution.py:186
  7.9 0.1 collective-permute-start.4
  8.0 2.6 %norm.2 = (bf16[8,256,640]{2,1,0:T(8,128)(2,1)S(1)}, f32[8,128]{1,0:T(8,128)S(1)}) custom-call(bf16[256,5120]{1,0:T(8,128)(2,1)} %bitcast.6.hidden, f32[1,5120]{1,0:T(1,128)S(1)} %bitcast.24), custom_call_target="tpu_custom_call" | custom-call | flops 5242880 | bytes 5242880 | tf_op jit(solution)/shard_map/norm/pallas_call | solution.py:226
  10.6 0.0 collective-permute-done.3
  10.6 2.6 %norm.3 = (bf16[8,256,640]{2,1,0:T(8,128)(2,1)S(1)}, f32[8,128]{1,0:T(8,128)S(1)}) custom-call(bf16[256,5120]{1,0:T(8,128)(2,1)} %bitcast.8.hidden, f32[1,5120]{1,0:T(1,128)S(1)} %bitcast.25), custom_call_target="tpu_custom_call" | custom-call | flops 5242880 | bytes 5242880 | tf_op jit(solution)/shard_map/norm/pallas_call | solution.py:226
  13.3 1.5 %copy-done = bf16[8,256,640]{2,1,0:T(8,128)(2,1)} copy-done((bf16[8,256,640]{2,1,0:T(8,128)(2,1)}, bf16[8,256,640]{2,1,0:T(8,128)(2,1)S(1)}, u32[]{:S(2)}) %copy-start) | copy-done | bytes 2621464
  14.8 0.9 %collective-permute-done.2.rest_1_ = bf16[640,256]{1,0:T(8,128)(2,1)} collective-permute-done((bf16[640,256]{1,0:T(8,128)(2,1)S(1)}, bf16[640,256]{1,0:T(8,128)(2,1)}, u32[]{:S(2)}, u32[]{:S(2)}) %collective-permute-start.2) | collective-permute-done | bytes 327712 | tf_op jit(solution)/shard_map/ppermute | solution.py:297
  15.7 1.7 %collective-permute-start.6 = (bf16[640,256]{1,0:T(8,128)(2,1)}, bf16[640,256]{1,0:T(8,128)(2,1)}, u32[]{:S(2)}, u32[]{:S(2)}) collective-permute-start(bf16[640,256]{1,0:T(8,128)(2,1)} %collective-permute-done.2.rest_1_), channel_id=1, source_target_pairs={{0,8},{8,24},{24,16},{16,0},{1,9},{9,25},{25,17},{17,1},{2,10},{10... | collective-permute-start | bytes 983048 | tf_op jit(solution)/shard_map/ppermute | solution.py:297
  17.3 0.6 collective-permute-start.11
  17.9 1.5 %collective-permute-start.5 = (s32[2,256]{1,0:T(2,128)S(1)}, s32[2,256]{1,0:T(2,128)S(1)}, u32[]{:S(2)}, u32[]{:S(2)}) collective-permute-start(s32[2,256]{1,0:T(2,128)S(1)} %pad_add_fusion.refs_3_), channel_id=1, source_target_pairs={{0,1},{1,0},{2,3},{3,2},{4,5},{5,4},{6,7},{7,6},{8,9},{9,8},{10,11... | collective-permute-start | bytes 6152 | tf_op jit(solution)/shard_map/ppermute | solution.py:209
  19.4 0.5 collective-permute-start.13
  20.0 6.4 %collective-permute-done.6.rest_1_ = bf16[640,256]{1,0:T(8,128)(2,1)} collective-permute-done((bf16[640,256]{1,0:T(8,128)(2,1)}, bf16[640,256]{1,0:T(8,128)(2,1)}, u32[]{:S(2)}, u32[]{:S(2)}) %collective-permute-start.6) | collective-permute-done | bytes 327712 | tf_op jit(solution)/shard_map/ppermute | solution.py:297
  26.3 1.5 %collective-permute-start.7 = (bf16[640,256]{1,0:T(8,128)(2,1)}, bf16[640,256]{1,0:T(8,128)(2,1)S(1)}, u32[]{:S(2)}, u32[]{:S(2)}) collective-permute-start(bf16[640,256]{1,0:T(8,128)(2,1)} %collective-permute-done.6.rest_1_), channel_id=1, source_target_pairs={{0,8},{8,24},{24,16},{16,0},{1,9},{9,25},{25,17},{17,1},{2,10},{10... | collective-permute-start | bytes 983048 | tf_op jit(solution)/shard_map/ppermute | solution.py:297
  27.8 1.5 %collective-permute-start.10 = (bf16[640,256]{1,0:T(8,128)(2,1)}, bf16[640,256]{1,0:T(8,128)(2,1)S(1)}, u32[]{:S(2)}, u32[]{:S(2)}) collective-permute-start(bf16[640,256]{1,0:T(8,128)(2,1)} %collective-permute-done.6.rest_1_), channel_id=1, source_target_pairs={{0,1},{1,0},{2,3},{3,2},{4,5},{5,4},{6,7},{7,6},{8,9},{9,8},{10,11... | collective-permute-start | bytes 983048 | tf_op jit(solution)/shard_map/ppermute | solution.py:186
  29.3 0.7 collective-permute-start.9
  29.9 0.2 collective-permute-done.11.rest_0_.rest_3_
  30.2 1.5 %collective-permute-start.12 = (bf16[640,256]{1,0:T(8,128)(2,1)}, bf16[640,256]{1,0:T(8,128)(2,1)S(1)}, u32[]{:S(2)}, u32[]{:S(2)}) collective-permute-start(bf16[640,256]{1,0:T(8,128)(2,1)} %collective-permute-done.11.rest_0_.rest_3_), channel_id=1, source_target_pairs={{0,1},{1,0},{2,3},{3,2},{4,5},{5,4},{6,7},{7,6},{8,9},{9,8},{10,11... | collective-permute-start | bytes 983048 | tf_op jit(solution)/shard_map/ppermute | solution.py:186
  31.7 0.1 pad_add_fusion.1.place
  31.7 1.7 %copy-done.1 = bf16[8,256,640]{2,1,0:T(8,128)(2,1)S(1)} copy-done((bf16[8,256,640]{2,1,0:T(8,128)(2,1)S(1)}, bf16[8,256,640]{2,1,0:T(8,128)(2,1)}, u32[]{:S(2)}) %copy-start.1) | copy-done | bytes 2621464
  33.5 3.3 %project.5.rest_3_ = f32[2,512,256]{2,1,0:T(8,128)S(1)} custom-call(s32[3]{0:T(128)S(1)} %pad_add_fusion.1.place, bf16[8,256,640]{2,1,0:T(8,128)(2,1)S(1)} %get-tuple-element.38.own, bf16[8,256,640]{2,1,0:T(8,128)(2,1)S(1)} %copy-done.1, bf16[2,640,256]{2,1,0:T(8,128)(2,1)S(1)} %constant_dynamic-update-slice_fusion.rest_0_, ...), custom_call_target="tpu_custom_call" | custom-call | flops 671088640 | bytes 2621440 | tf_op jit(solution)/shard_map/project/pallas_call | solution.py:261
  36.8 0.8 %mask.1 = (f32[256,512]{1,0:T(8,128)S(1)}, s32[2]{0:T(128)S(1)}) custom-call(bf16[2,640,256]{2,1,0:T(8,128)(2,1)} %collective-permute-done.1.refs_0_.rest_1_, f32[8,128]{1,0:T(8,128)S(1)} %get-tuple-element.33.refs_1_, f32[8,128]{1,0:T(8,128)S(1)} %get-tuple-element.34.refs_2_, s32[2,256]{1,0:T(2,128)S(1)} %pad_add_fusion.refs_3_, ...), custom_call_target="tpu_custom_call" | custom-call | flops 1000000000 | bytes 3333333 | tf_op jit(solution)/shard_map/mask/pallas_call | solution.py:302
  37.7 2.4 %collective-permute-start.8 = (bf16[640,256]{1,0:T(8,128)(2,1)S(1)}, bf16[640,256]{1,0:T(8,128)(2,1)S(1)}, u32[]{:S(2)}, u32[]{:S(2)}) collective-permute-start(bf16[640,256]{1,0:T(8,128)(2,1)S(1)} %collective-permute-done.7.rest_0_), channel_id=1, source_target_pairs={{0,4},{4,0},{1,5},{5,1},{2,6},{6,2},{3,7},{7,3},{8,12},{12,8},{9,1... | collective-permute-start | bytes 983048 | tf_op jit(solution)/shard_map/ppermute | solution.py:186
  40.0 0.0 collective-permute-start.15
  40.1 0.2 collective-permute-start.16
  40.3 2.3 %project.6.rest_5_ = f32[2,512,256]{2,1,0:T(8,128)S(1)} custom-call(s32[3]{0:T(128)S(1)} %pad_add_fusion.1.place, bf16[8,256,640]{2,1,0:T(8,128)(2,1)S(1)} %get-tuple-element.38.own, bf16[8,256,640]{2,1,0:T(8,128)(2,1)S(1)} %copy-done.2, bf16[640,256]{1,0:T(8,128)(2,1)} %collective-permute-done.11.rest_0_.rest_3_, ...), custom_call_target="tpu_custom_call" | custom-call | flops 335544320 | bytes 1310720 | tf_op jit(solution)/shard_map/project/pallas_call | solution.py:261
  42.6 0.0 copy-start.8
  42.7 3.0 %collective-permute-done.12.rest_4_ = bf16[640,256]{1,0:T(8,128)(2,1)S(1)} collective-permute-done((bf16[640,256]{1,0:T(8,128)(2,1)}, bf16[640,256]{1,0:T(8,128)(2,1)S(1)}, u32[]{:S(2)}, u32[]{:S(2)}) %collective-permute-start.12) | collective-permute-done | bytes 327712 | tf_op jit(solution)/shard_map/ppermute | solution.py:186
  45.6 3.1 %project.7.rest_4_ = f32[2,512,256]{2,1,0:T(8,128)S(1)} custom-call(s32[3]{0:T(128)S(1)} %pad_add_fusion.1.place, bf16[8,256,640]{2,1,0:T(8,128)(2,1)S(1)} %get-tuple-element.38.own, bf16[8,256,640]{2,1,0:T(8,128)(2,1)S(1)} %copy-done.2, bf16[640,256]{1,0:T(8,128)(2,1)S(1)} %collective-permute-done.9.rest_0_.rest_2_, ...), custom_call_target="tpu_custom_call" | custom-call | flops 5368709120 | bytes 20971520 | tf_op jit(solution)/shard_map/project/pallas_call | solution.py:261
  48.8 1.6 %collective-permute-start.14 = (bf16[640,256]{1,0:T(8,128)(2,1)S(1)}, bf16[640,256]{1,0:T(8,128)(2,1)S(1)}, u32[]{:S(2)}, u32[]{:S(2)}) collective-permute-start(bf16[640,256]{1,0:T(8,128)(2,1)S(1)} %collective-permute-done.8.rest_0_), channel_id=1, source_target_pairs={{0,1},{1,0},{2,3},{3,2},{4,5},{5,4},{6,7},{7,6},{8,9},{9,8},{10,11... | collective-permute-start | bytes 983048 | tf_op jit(solution)/shard_map/ppermute | solution.py:186
  50.3 1.0 %fusion = (f32[512,64]{1,0:T(8,128)S(1)}, f32[512,64]{1,0:T(8,128)S(1)}, f32[512,64]{1,0:T(8,128)S(1)}) fusion(f32[64]{0:T(128)S(1)} %copy-done.8, f32[512]{0:T(512)S(1)} %add_convert_fusion), kind=kLoop, calls=%fused_computation.11 | loop fusion | flops 65536 | bytes 395520 | tf_op jit(solution)/shard_map/neg | solution.py:338
  51.3 0.1 pad_maximum_fusion.1.rest_3_
  51.5 0.1 pad_maximum_fusion.2.rest_4_
  51.6 0.0 copy-start.5
  51.6 1.0 %collective-permute-done.15.rest_1_ = bf16[640,256]{1,0:T(8,128)(2,1)S(1)} collective-permute-done((bf16[640,256]{1,0:T(8,128)(2,1)S(1)}, bf16[640,256]{1,0:T(8,128)(2,1)S(1)}, u32[]{:S(2)}, u32[]{:S(2)}) %collective-permute-start.15) | collective-permute-done | bytes 327712 | tf_op jit(solution)/shard_map/ppermute | solution.py:186
  52.7 0.7 collective-permute-done.16.rest_3_
  53.3 2.5 %project.8.rest_2_ = f32[2,512,256]{2,1,0:T(8,128)S(1)} custom-call(s32[3]{0:T(128)S(1)} %pad_add_fusion.1.place, bf16[8,256,640]{2,1,0:T(8,128)(2,1)S(1)} %get-tuple-element.38.own, bf16[8,256,640]{2,1,0:T(8,128)(2,1)S(1)} %copy-done.2, bf16[640,256]{1,0:T(8,128)(2,1)S(1)} %collective-permute-done.7.rest_0_, ...), custom_call_target="tpu_custom_call" | custom-call | flops 671088640 | bytes 2621440 | tf_op jit(solution)/shard_map/project/pallas_call | solution.py:261
  55.9 2.2 %collective-permute-done.14.rest_1_ = bf16[640,256]{1,0:T(8,128)(2,1)S(1)} collective-permute-done((bf16[640,256]{1,0:T(8,128)(2,1)S(1)}, bf16[640,256]{1,0:T(8,128)(2,1)S(1)}, u32[]{:S(2)}, u32[]{:S(2)}) %collective-permute-start.14) | collective-permute-done | bytes 327712 | tf_op jit(solution)/shard_map/ppermute | solution.py:186
  58.1 2.1 %project.9 = (bf16[256,512]{1,0:T(8,128)(2,1)S(1)}, bf16[256,512]{1,0:T(8,128)(2,1)S(1)}) custom-call(s32[3]{0:T(128)S(1)} %pad_add_fusion.1.place, bf16[8,256,640]{2,1,0:T(8,128)(2,1)S(1)} %get-tuple-element.38.own, bf16[8,256,640]{2,1,0:T(8,128)(2,1)S(1)} %copy-done.2, bf16[640,256]{1,0:T(8,128)(2,1)S(1)} %collective-permute-done.8.rest_0_, ...), custom_call_target="tpu_custom_call" | custom-call | flops 335544320 | bytes 1310720 | tf_op jit(solution)/shard_map/project/pallas_call | solution.py:261
  60.1 1.6 %collective-permute-start.19 = (bf16[256,512]{1,0:T(8,128)(2,1)S(1)}, bf16[256,512]{1,0:T(8,128)(2,1)S(1)}, u32[]{:S(2)}, u32[]{:S(2)}) collective-permute-start(bf16[256,512]{1,0:T(8,128)(2,1)S(1)} %get-tuple-element.48.rest_0_), channel_id=1, source_target_pairs={{0,1},{1,0},{2,3},{3,2},{4,5},{5,4},{6,7},{7,6},{8,9},{9,8},{10,11... | collective-permute-start | bytes 786440 | tf_op jit(solution)/shard_map/ppermute | solution.py:209
  61.7 0.6 collective-permute-start.18
  62.4 6.8 %collective-permute-done.19.rest_1_ = bf16[256,512]{1,0:T(8,128)(2,1)S(1)} collective-permute-done((bf16[256,512]{1,0:T(8,128)(2,1)S(1)}, bf16[256,512]{1,0:T(8,128)(2,1)S(1)}, u32[]{:S(2)}, u32[]{:S(2)}) %collective-permute-start.19) | collective-permute-done | bytes 262176 | tf_op jit(solution)/shard_map/ppermute | solution.py:209
  69.2 4.4 %attend.2.rest_2_ = bf16[256,4096]{1,0:T(8,128)(2,1)} custom-call(s32[1]{0:T(128)} %bitcast.place, s32[2]{0:T(128)S(1)} %get-tuple-element.36.needs, bf16[256,4096]{1,0:T(8,128)(2,1)S(1)} %bitcast.22, f32[256,512]{1,0:T(8,128)S(1)} %get-tuple-element.41.bias, bf16[256,512]{1,0:T(8,128)(2,1)S(1)} %get-tuple-element.48.rest_0_, ...), custom_call_target="tpu_custom_call" | custom-call | flops 1073741824 | bytes 2097152 | tf_op jit(solution)/shard_map/attend/pallas_call | solution.py:351
  73.6 4.7 %attend.3 = bf16[256,4096]{1,0:T(8,128)(2,1)} custom-call(s32[1]{0:T(128)} %bitcast.place, s32[2]{0:T(128)S(1)} %get-tuple-element.36.needs, bf16[256,4096]{1,0:T(8,128)(2,1)S(1)} %bitcast.23, f32[256,512]{1,0:T(8,128)S(1)} %get-tuple-element.41.bias, bf16[256,512]{1,0:T(8,128)(2,1)S(1)} %collective-permute-done.17.rest_0_, ...), custom_call_target="tpu_custom_call", output_to_operand_aliasing={{}: (6, {})} | custom-call | flops 1073741824 | bytes 2097152 | tf_op jit(solution)/shard_map/attend/pallas_call | solution.py:351
  (33 shorter events, 0.2 us)
Async XLA Ops:
  0.0 7.8 %copy-start.7 = (s32[1,256]{1,0:T(1,128)S(1)}, s32[1,256]{1,0:T(1,128)}, u32[]{:S(2)}) copy-start(s32[1,256]{1,0:T(1,128)} %param.15) | copy-start | bytes 3076
  0.0 7.8 %copy-start.6 = (s32[1,256]{1,0:T(1,128)S(1)}, s32[1,256]{1,0:T(1,128)}, u32[]{:S(2)}) copy-start(s32[1,256]{1,0:T(1,128)} %param.16) | copy-start | bytes 3076
  0.0 7.9 %copy-start.4 = (f32[5120]{0:T(1024)S(1)}, f32[5120]{0:T(1024)}, u32[]{:S(2)}) copy-start(f32[5120]{0:T(1024)} %param.11) | copy-start | bytes 61444
  1.3 1.8 %collective-permute-start = (bf16[2,320,256]{2,1,0:T(8,128)(2,1)S(1)}, bf16[2,320,256]{2,1,0:T(8,128)(2,1)S(1)}, u32[]{:S(2)}, u32[]{:S(2)}) collective-permute-start(bf16[2,320,256]{2,1,0:T(8,128)(2,1)S(1)} %pad_maximum_fusion), channel_id=1, source_target_pairs={{0,2},{2,0},{1,3},{3,1},{4,6},{6,4},{5,7},{7,5},{8,10},{10,8},{9,1... | collective-permute-start | bytes 983048 | tf_op jit(solution)/shard_map/ppermute | solution.py:186
  3.1 7.5 %collective-permute-start.3 = (bf16[1,256,5120]{2,1,0:T(8,128)(2,1)}, bf16[1,256,5120]{2,1,0:T(8,128)(2,1)}, u32[]{:S(2)}, u32[]{:S(2)}) collective-permute-start(bf16[1,256,5120]{2,1,0:T(8,128)(2,1)} %param.9), channel_id=1, source_target_pairs={{0,2},{2,0},{1,3},{3,1},{4,6},{6,4},{5,7},{7,5},{8,10},{10,8},{9,1... | collective-permute-start | bytes 7864328 | tf_op jit(solution)/shard_map/ppermute | solution.py:186
  3.6 12.1 %collective-permute-start.2 = (bf16[640,256]{1,0:T(8,128)(2,1)S(1)}, bf16[640,256]{1,0:T(8,128)(2,1)}, u32[]{:S(2)}, u32[]{:S(2)}) collective-permute-start(bf16[640,256]{1,0:T(8,128)(2,1)S(1)} %dynamic-slice_bitcast_fusion), channel_id=1, source_target_pairs={{0,8},{8,24},{24,16},{16,0},{1,9},{9,25},{25,17},{17,1},{2,10},{10... | collective-permute-start | bytes 983048 | tf_op jit(solution)/shard_map/ppermute | solution.py:297
  6.3 21.4 %collective-permute-start.1 = (bf16[2,640,256]{2,1,0:T(8,128)(2,1)S(1)}, bf16[2,640,256]{2,1,0:T(8,128)(2,1)}, u32[]{:S(2)}, u32[]{:S(2)}) collective-permute-start(bf16[2,640,256]{2,1,0:T(8,128)(2,1)S(1)} %constant_dynamic-update-slice_fusion.rest_0_), channel_id=1, source_target_pairs={{0,4},{4,0},{1,5},{5,1},{2,6},{6,2},{3,7},{7,3},{8,12},{12,8},{9,1... | collective-permute-start | bytes 1966088 | tf_op jit(solution)/shard_map/ppermute | solution.py:186
  7.9 6.9 %collective-permute-start.4 = (s32[2,256]{1,0:T(2,128)S(1)}, s32[2,256]{1,0:T(2,128)S(1)}, u32[]{:S(2)}, u32[]{:S(2)}) collective-permute-start(s32[2,256]{1,0:T(2,128)S(1)} %pad_add_fusion.refs_3_), channel_id=1, source_target_pairs={{0,2},{2,0},{1,3},{3,1},{4,6},{6,4},{5,7},{7,5},{8,10},{10,8},{9,1... | collective-permute-start | bytes 6152 | tf_op jit(solution)/shard_map/ppermute | solution.py:186
  13.3 1.5 %copy-start = (bf16[8,256,640]{2,1,0:T(8,128)(2,1)}, bf16[8,256,640]{2,1,0:T(8,128)(2,1)S(1)}, u32[]{:S(2)}) copy-start(bf16[8,256,640]{2,1,0:T(8,128)(2,1)S(1)} %get-tuple-element.39.other) | copy-start | bytes 7864324
  15.7 10.6 %collective-permute-start.6 = (bf16[640,256]{1,0:T(8,128)(2,1)}, bf16[640,256]{1,0:T(8,128)(2,1)}, u32[]{:S(2)}, u32[]{:S(2)}) collective-permute-start(bf16[640,256]{1,0:T(8,128)(2,1)} %collective-permute-done.2.rest_1_), channel_id=1, source_target_pairs={{0,8},{8,24},{24,16},{16,0},{1,9},{9,25},{25,17},{17,1},{2,10},{10... | collective-permute-start | bytes 983048 | tf_op jit(solution)/shard_map/ppermute | solution.py:297
  17.3 12.8 %collective-permute-start.11 = (bf16[640,256]{1,0:T(8,128)(2,1)}, bf16[640,256]{1,0:T(8,128)(2,1)}, u32[]{:S(2)}, u32[]{:S(2)}) collective-permute-start(bf16[640,256]{1,0:T(8,128)(2,1)} %collective-permute-done.2.rest_1_), channel_id=1, source_target_pairs={{0,4},{4,0},{1,5},{5,1},{2,6},{6,2},{3,7},{7,3},{8,12},{12,8},{9,1... | collective-permute-start | bytes 983048 | tf_op jit(solution)/shard_map/ppermute | solution.py:186
  17.9 11.3 %collective-permute-start.5 = (s32[2,256]{1,0:T(2,128)S(1)}, s32[2,256]{1,0:T(2,128)S(1)}, u32[]{:S(2)}, u32[]{:S(2)}) collective-permute-start(s32[2,256]{1,0:T(2,128)S(1)} %pad_add_fusion.refs_3_), channel_id=1, source_target_pairs={{0,1},{1,0},{2,3},{3,2},{4,5},{5,4},{6,7},{7,6},{8,9},{9,8},{10,11... | collective-permute-start | bytes 6152 | tf_op jit(solution)/shard_map/ppermute | solution.py:209
  19.4 20.6 %collective-permute-start.13 = (bf16[640,256]{1,0:T(8,128)(2,1)}, bf16[640,256]{1,0:T(8,128)(2,1)S(1)}, u32[]{:S(2)}, u32[]{:S(2)}) collective-permute-start(bf16[640,256]{1,0:T(8,128)(2,1)} %collective-permute-done.2.rest_1_), channel_id=1, source_target_pairs={{0,1},{1,0},{2,3},{3,2},{4,5},{5,4},{6,7},{7,6},{8,9},{9,8},{10,11... | collective-permute-start | bytes 983048 | tf_op jit(solution)/shard_map/ppermute | solution.py:186
  26.3 11.3 %collective-permute-start.7 = (bf16[640,256]{1,0:T(8,128)(2,1)}, bf16[640,256]{1,0:T(8,128)(2,1)S(1)}, u32[]{:S(2)}, u32[]{:S(2)}) collective-permute-start(bf16[640,256]{1,0:T(8,128)(2,1)} %collective-permute-done.6.rest_1_), channel_id=1, source_target_pairs={{0,8},{8,24},{24,16},{16,0},{1,9},{9,25},{25,17},{17,1},{2,10},{10... | collective-permute-start | bytes 983048 | tf_op jit(solution)/shard_map/ppermute | solution.py:297
  27.8 12.3 %collective-permute-start.10 = (bf16[640,256]{1,0:T(8,128)(2,1)}, bf16[640,256]{1,0:T(8,128)(2,1)S(1)}, u32[]{:S(2)}, u32[]{:S(2)}) collective-permute-start(bf16[640,256]{1,0:T(8,128)(2,1)} %collective-permute-done.6.rest_1_), channel_id=1, source_target_pairs={{0,1},{1,0},{2,3},{3,2},{4,5},{5,4},{6,7},{7,6},{8,9},{9,8},{10,11... | collective-permute-start | bytes 983048 | tf_op jit(solution)/shard_map/ppermute | solution.py:186
  29.3 16.4 %collective-permute-start.9 = (bf16[640,256]{1,0:T(8,128)(2,1)}, bf16[640,256]{1,0:T(8,128)(2,1)S(1)}, u32[]{:S(2)}, u32[]{:S(2)}) collective-permute-start(bf16[640,256]{1,0:T(8,128)(2,1)} %collective-permute-done.6.rest_1_), channel_id=1, source_target_pairs={{0,4},{4,0},{1,5},{5,1},{2,6},{6,2},{3,7},{7,3},{8,12},{12,8},{9,1... | collective-permute-start | bytes 983048 | tf_op jit(solution)/shard_map/ppermute | solution.py:186
  30.2 15.5 %collective-permute-start.12 = (bf16[640,256]{1,0:T(8,128)(2,1)}, bf16[640,256]{1,0:T(8,128)(2,1)S(1)}, u32[]{:S(2)}, u32[]{:S(2)}) collective-permute-start(bf16[640,256]{1,0:T(8,128)(2,1)} %collective-permute-done.11.rest_0_.rest_3_), channel_id=1, source_target_pairs={{0,1},{1,0},{2,3},{3,2},{4,5},{5,4},{6,7},{7,6},{8,9},{9,8},{10,11... | collective-permute-start | bytes 983048 | tf_op jit(solution)/shard_map/ppermute | solution.py:186
  31.7 1.7 %copy-start.1 = (bf16[8,256,640]{2,1,0:T(8,128)(2,1)S(1)}, bf16[8,256,640]{2,1,0:T(8,128)(2,1)}, u32[]{:S(2)}) copy-start(bf16[8,256,640]{2,1,0:T(8,128)(2,1)} %copy-done) | copy-start | bytes 7864324
  36.8 3.5 %copy-start.2 = (bf16[8,256,640]{2,1,0:T(8,128)(2,1)S(1)}, bf16[8,256,640]{2,1,0:T(8,128)(2,1)}, u32[]{:S(2)}) copy-start(bf16[8,256,640]{2,1,0:T(8,128)(2,1)} %copy-done) | copy-start | bytes 7864324
  37.7 11.1 %collective-permute-start.8 = (bf16[640,256]{1,0:T(8,128)(2,1)S(1)}, bf16[640,256]{1,0:T(8,128)(2,1)S(1)}, u32[]{:S(2)}, u32[]{:S(2)}) collective-permute-start(bf16[640,256]{1,0:T(8,128)(2,1)S(1)} %collective-permute-done.7.rest_0_), channel_id=1, source_target_pairs={{0,4},{4,0},{1,5},{5,1},{2,6},{6,2},{3,7},{7,3},{8,12},{12,8},{9,1... | collective-permute-start | bytes 983048 | tf_op jit(solution)/shard_map/ppermute | solution.py:186
  40.0 12.6 %collective-permute-start.15 = (bf16[640,256]{1,0:T(8,128)(2,1)S(1)}, bf16[640,256]{1,0:T(8,128)(2,1)S(1)}, u32[]{:S(2)}, u32[]{:S(2)}) collective-permute-start(bf16[640,256]{1,0:T(8,128)(2,1)S(1)} %collective-permute-done.7.rest_0_), channel_id=1, source_target_pairs={{0,1},{1,0},{2,3},{3,2},{4,5},{5,4},{6,7},{7,6},{8,9},{9,8},{10,11... | collective-permute-start | bytes 983048 | tf_op jit(solution)/shard_map/ppermute | solution.py:186
  40.1 13.3 %collective-permute-start.16 = (bf16[640,256]{1,0:T(8,128)(2,1)S(1)}, bf16[640,256]{1,0:T(8,128)(2,1)S(1)}, u32[]{:S(2)}, u32[]{:S(2)}) collective-permute-start(bf16[640,256]{1,0:T(8,128)(2,1)S(1)} %collective-permute-done.10.rest_2_), channel_id=1, source_target_pairs={{0,4},{4,0},{1,5},{5,1},{2,6},{6,2},{3,7},{7,3},{8,12},{12,8},{9,1... | collective-permute-start | bytes 983048 | tf_op jit(solution)/shard_map/ppermute | solution.py:186
  42.6 7.7 %copy-start.8 = (f32[64]{0:T(128)S(1)}, f32[64]{0:T(128)}, u32[]{:S(2)}) copy-start(f32[64]{0:T(128)} %constant.45) | copy-start | bytes 772
  48.8 9.3 %collective-permute-start.14 = (bf16[640,256]{1,0:T(8,128)(2,1)S(1)}, bf16[640,256]{1,0:T(8,128)(2,1)S(1)}, u32[]{:S(2)}, u32[]{:S(2)}) collective-permute-start(bf16[640,256]{1,0:T(8,128)(2,1)S(1)} %collective-permute-done.8.rest_0_), channel_id=1, source_target_pairs={{0,1},{1,0},{2,3},{3,2},{4,5},{5,4},{6,7},{7,6},{8,9},{9,8},{10,11... | collective-permute-start | bytes 983048 | tf_op jit(solution)/shard_map/ppermute | solution.py:186
  51.6 6.5 %copy-start.5 = (f32[128]{0:T(128)S(1)}, f32[128]{0:T(128)}, u32[]{:S(2)}) copy-start(f32[128]{0:T(128)} %param.12) | copy-start | bytes 1540
  58.1 11.1 %copy-start.3 = (bf16[1,256,4096]{2,1,0:T(8,128)(2,1)S(1)}, bf16[1,256,4096]{2,1,0:T(8,128)(2,1)}, u32[]{:S(2)}) copy-start(bf16[1,256,4096]{2,1,0:T(8,128)(2,1)} %param.10) | copy-start | bytes 6291460
  60.1 9.0 %collective-permute-start.19 = (bf16[256,512]{1,0:T(8,128)(2,1)S(1)}, bf16[256,512]{1,0:T(8,128)(2,1)S(1)}, u32[]{:S(2)}, u32[]{:S(2)}) collective-permute-start(bf16[256,512]{1,0:T(8,128)(2,1)S(1)} %get-tuple-element.48.rest_0_), channel_id=1, source_target_pairs={{0,1},{1,0},{2,3},{3,2},{4,5},{5,4},{6,7},{7,6},{8,9},{9,8},{10,11... | collective-permute-start | bytes 786440 | tf_op jit(solution)/shard_map/ppermute | solution.py:209
  61.7 11.9 %collective-permute-start.17 = (bf16[256,512]{1,0:T(8,128)(2,1)S(1)}, bf16[256,512]{1,0:T(8,128)(2,1)S(1)}, u32[]{:S(2)}, u32[]{:S(2)}) collective-permute-start(bf16[256,512]{1,0:T(8,128)(2,1)S(1)} %get-tuple-element.47), channel_id=1, source_target_pairs={{0,2},{1,3},{2,0},{3,1},{4,6},{5,7},{6,4},{7,5},{8,10},{9,11},{10,... | collective-permute-start | bytes 786440 | tf_op jit(solution)/shard_map/ppermute | solution.py:209
  61.7 11.9 %collective-permute-start.18 = (bf16[256,512]{1,0:T(8,128)(2,1)S(1)}, bf16[256,512]{1,0:T(8,128)(2,1)S(1)}, u32[]{:S(2)}, u32[]{:S(2)}) collective-permute-start(bf16[256,512]{1,0:T(8,128)(2,1)S(1)} %get-tuple-element.47), channel_id=1, source_target_pairs={{0,3},{1,2},{2,1},{3,0},{4,7},{5,6},{6,5},{7,4},{8,11},{9,10},{10,... | collective-permute-start | bytes 786440 | tf_op jit(solution)/shard_map/ppermute | solution.py:209
